TPU v7x, 32 devices: a whole 2x2x4 slice. The times are simulated.
32 devices in a mesh: dp: 8 (over y, x, core), mp: 4 (over z).
Axes of the slice: x: 2, y: 2, z: 4, core: 2. Of those that a mesh axis runs over, the one named last changes fastest.
Arguments:
- tokens: bfloat16 [8192, 1024], P('dp'), may hold values from -6 to 6
- cotangent: bfloat16 [8192, 1024], P('dp'), may hold values from -6 to 6
- ln_gains: float32 [2, 1024], replicated, may hold values from 0.5 to 1.5
- ln_biases: float32 [2, 1024], replicated, may hold values from -2 to 2
- w_qkv: bfloat16 [1024, 3, 1024], P(None, None, 'mp'), may hold values from -0.1875 to 0.1875
- w_o: bfloat16 [1024, 1024], P('mp'), may hold values from -0.75 to 0.75
- w_in: bfloat16 [1024, 4096], P(None, 'mp'), may hold values from -0.1875 to 0.1875
- w_out: bfloat16 [4096, 1024], P('mp'), may hold values from -0.1875 to 0.1875
- w_router: bfloat16 [1024, 8], replicated, may hold values from -0.125 to 0.125
- w_coef: bfloat16 [1024, 2], replicated, may hold values from -0.1875 to 0.1875
- w_up: bfloat16 [8, 1024, 4096], P('dp', None, 'mp'), may hold values from -0.1875 to 0.1875
- w_down: bfloat16 [8, 4096, 1024], P('dp', 'mp'), may hold values from -3 to 3
- routes: int32 [8192, 1], P('dp'), may hold values from 0 to 7; in each aligned block of 1024 rows (0 to 1023, 1024 to 2047, ...) at most 256 rows name the same one
- long_group: int32 [2], replicated, may hold values from 1 to 4096, as said below
Outputs:
- output: bfloat16 [8192, 1024], P('dp')
- grad_tokens: bfloat16 [8192, 1024], P('dp')
- grad_gains: float32 [2, 1024], P(None, 'dp')
- grad_biases: float32 [2, 1024], P(None, 'dp')
- grad_qkv: float32 [1024, 3, 1024], P('dp', None, 'mp')
- grad_o: float32 [1024, 1024], P('mp', 'dp')
- grad_in: float32 [1024, 4096], P('dp', 'mp')
- grad_out: float32 [4096, 1024], P('mp', 'dp')
- grad_router: float32 [1024, 8], P('dp')
- grad_coef: float32 [1024, 2], P('dp')
- grad_up: float32 [8, 1024, 4096], P('dp', None, 'mp')
- grad_down: float32 [8, 4096, 1024], P('dp', 'mp')
Inputs may be any that keep to these rules, and one draw needn't show every extreme that they name: `routes`: in the rows of one device (1024 rows) no expert is named by more than 256 rows, a bound that some block reaches. `long_group`: at least one group's first sequence fills the whole group (4096 rows).
All inputs are finite; a program needn't handle non-finite values.
Results may differ from a plain program's by a relative error of at most 0.015.
Values may be sent and summed in bfloat16 or wider, within the bound.
No kernel may reach another device: no remote copies, remote signals or barrier semaphores. Data moves between devices by JAX's collectives and lax.ppermute only.
A program may use at most 320 MiB of HBM per device.

v0:
```python
from functools import partial

import jax
import jax.numpy as jnp
from jax import lax
from jax.experimental import pallas as pl
from jax.experimental.pallas import tpu as pltpu
from jax.sharding import PartitionSpec as P

HD = 64
GROUP = 4
EPS = 1e-05
LOG2E = 1.4426950408889634
SCALE2 = 0.125 * LOG2E
HIDE = -1e30
BF = jnp.bfloat16
F32 = jnp.float32
LIGHT = pl.CostEstimate(flops=1 << 20, bytes_accessed=1 << 20, transcendentals=0)


def mm(a, b):
    return jnp.dot(a, b, preferred_element_type=F32)


def ein(spec, a, b):
    return jnp.einsum(spec, a, b, preferred_element_type=F32)


def call(kernel, name, prefetch, grid, in_specs, out_specs, out_shape, args, scratch=(), alias=None, vmem=48):
    return pl.pallas_call(
        kernel,
        grid_spec=pltpu.PrefetchScalarGridSpec(
            num_scalar_prefetch=1,
            grid=grid,
            in_specs=in_specs,
            out_specs=out_specs,
            scratch_shapes=list(scratch),
        ),
        out_shape=out_shape,
        input_output_aliases=alias or {},
        compiler_params=pltpu.CompilerParams(vmem_limit_bytes=vmem * 2**20),
        cost_estimate=LIGHT,
        name=name,
    )(prefetch, *args)


def fixed(shape):
    zeros = (0,) * len(shape)
    return pl.BlockSpec(shape, lambda *_: zeros)


def like(shape, dtype):
    return jax.ShapeDtypeStruct(shape, dtype)


def normalize(v):
    mean = jnp.mean(v, axis=-1, keepdims=True)
    centred = v - mean
    scale = lax.rsqrt(jnp.mean(centred * centred, axis=-1, keepdims=True) + EPS)
    return centred * scale, scale


def norm_back(grad, gain, normal, scale):
    g = grad * gain
    along = jnp.mean(g * normal, axis=-1, keepdims=True)
    return scale * (g - jnp.mean(g, axis=-1, keepdims=True) - normal * along)


def qkv_kernel(at_ref, x_ref, gain_ref, bias_ref, w_ref, a_ref, *outs):
    normal, _ = normalize(x_ref[...].astype(F32))
    a = (normal * gain_ref[...] + bias_ref[...]).astype(BF)
    a_ref[...] = a
    for s in range(GROUP):
        outs[s][...] = mm_t(w_ref[at_ref[0] ^ s], a).astype(BF)


def project(at, tokens, gain, bias, w_heads):
    rows, width = tokens.shape
    features = w_heads.shape[1]
    blk = min(256, rows)
    moving = pl.BlockSpec((blk, width), lambda i, n: (i, 0))
    return call(
        qkv_kernel,
        "project",
        at,
        (rows // blk,),
        [moving, fixed((1, width)), fixed((1, width)), fixed(w_heads.shape)],
        [moving] + [pl.BlockSpec((features, blk), lambda i, n: (0, i))] * GROUP,
        [like((rows, width), BF)] + [like((features, rows), BF)] * GROUP,
        (tokens, gain, bias, w_heads),
    )


def fill_keys(k_s, place, keys, first_len, blk):
    rows = place * blk + lax.broadcasted_iota(jnp.int32, (blk, 128), 0)
    lane = lax.broadcasted_iota(jnp.int32, (blk, 128), 1)
    wide = jnp.concatenate([keys.astype(F32).T, jnp.zeros((blk, 128 - HD), F32)], axis=1)
    wide = jnp.where((lane == HD) & (rows < first_len), HIDE, wide)
    k_s[pl.ds(place * blk, blk), :] = wide.astype(BF)


def wide_query(query, place, first_len, blk):
    cols = place * blk + lax.broadcasted_iota(jnp.int32, (128 - HD, blk), 1)
    sub = lax.broadcasted_iota(jnp.int32, (128 - HD, blk), 0)
    extra = jnp.where((sub == 0) & (cols >= first_len), 1.0, 0.0)
    return jnp.concatenate([query, extra.astype(BF)], axis=0)


def causal(blk):
    keys = lax.broadcasted_iota(jnp.int32, (blk, blk), 0)
    queries = lax.broadcasted_iota(jnp.int32, (blk, blk), 1)
    return keys <= queries


def attend_kernel(blk, per, at_ref, *refs):
    qkv_refs, o_refs = refs[:GROUP], refs[GROUP : 2 * GROUP]
    lse_ref, k_s, qkv_s = refs[2 * GROUP :]
    i = pl.program_id(0)
    place, first_len = at_ref[0], at_ref[3]

    @pl.when(i == 0)
    def _():
        for s in range(GROUP):
            qkv_s[place ^ s] = qkv_refs[s][...]

    def part(which, j):
        return qkv_s[j // per, HD * which : HD * (which + 1), pl.ds((j % per) * blk, blk)]

    fill_keys(k_s, i, part(1, i), first_len, blk)
    query = wide_query(part(0, i), i, first_len, blk)

    def scores(j):
        return mm(k_s[pl.ds(pl.multiple_of(j * blk, blk), blk), :], query)

    s = jnp.where(causal(blk), scores(i), HIDE)
    top = jnp.max(s, axis=0, keepdims=True)
    p = jnp.exp2((s - top) * SCALE2)
    total = jnp.sum(p, axis=0, keepdims=True)
    acc = mm(part(2, i), p.astype(BF))

    def steps(blocks, carry):
        top, total, acc = carry
        s = [scores(j) for j in blocks]
        new = top
        for one in s:
            new = jnp.maximum(new, jnp.max(one, axis=0, keepdims=True))
        keep = jnp.exp2((top - new) * SCALE2)
        total, acc = total * keep, acc * keep
        for j, one in zip(blocks, s):
            p = jnp.exp2((one - new) * SCALE2)
            total = total + jnp.sum(p, axis=0, keepdims=True)
            acc = acc + mm(part(2, j), p.astype(BF))
        return new, total, acc

    low = jnp.where(i * blk >= first_len, first_len // blk, 0)
    pairs = (i - low) // 2
    carry = lax.fori_loop(
        0, pairs, lambda t, c: steps([low + 2 * t, low + 2 * t + 1], c), (top, total, acc)
    )
    top, total, acc = lax.fori_loop(low + 2 * pairs, i, lambda j, c: steps([j], c), carry)
    out = (acc / total).astype(BF)
    for s in range(GROUP):

        @pl.when((i // per) ^ place == s)
        def _():
            o_refs[s][:, pl.ds((i % per) * blk, blk)] = out

    lse_ref[0] = top * SCALE2 + jnp.log2(total)


def attend(at, qkv):
    features, rows = qkv[0].shape
    blk = min(512, rows)
    per = rows // blk
    count = GROUP * per
    return call(
        partial(attend_kernel, blk, per),
        "attend",
        at,
        (count,),
        [fixed((features, rows))] * GROUP,
        [fixed((HD, rows))] * GROUP + [pl.BlockSpec((1, 1, blk), lambda i, n: (i, 0, 0))],
        [like((HD, rows), BF)] * GROUP + [like((count, 1, blk), F32)],
        qkv,
        scratch=[pltpu.VMEM((GROUP * rows, 128), BF), pltpu.VMEM((GROUP, features, rows), BF)],
    )


def back_kernel(blk, per, count, at_ref, *refs):
    qkv_refs, do_refs, o_refs = refs[:GROUP], refs[GROUP : 2 * GROUP], refs[2 * GROUP : 3 * GROUP]
    lse_ref, refs = refs[3 * GROUP], refs[3 * GROUP + 1 :]
    out_refs, refs = refs[:GROUP], refs[GROUP:]
    dq_ref, out_ref, k_s, kt_s, v_s, wide_s, dot_s, both_s, delta_s, acc_s = refs
    j = pl.program_id(0)
    place, first_len = at_ref[0], at_ref[3]

    @pl.when(j == 0)
    def _():
        dq_ref[...] = jnp.zeros(dq_ref.shape, F32)
        zero = jnp.zeros((blk, HD), F32)
        for s in range(GROUP):
            for sub in range(per):
                i = (place ^ s) * per + sub
                at = pl.ds(pl.multiple_of(i * blk, blk), blk)
                cut = slice(sub * blk, (sub + 1) * blk)
                query = qkv_refs[s][0:HD, cut]
                keys = qkv_refs[s][HD : 2 * HD, cut]
                grad = do_refs[s][:, cut]
                fill_keys(k_s, i, keys, first_len, blk)
                kt_s[:, at] = keys
                dot_s[:, at] = grad
                wide_s[:, at] = wide_query(query, i, first_len, blk)
                grad = grad.astype(F32)
                values = qkv_refs[s][2 * HD :, cut].astype(F32)
                v_s[at, :] = jnp.concatenate([values.T, zero], axis=1).astype(BF)
                both_s[0, at, :] = jnp.concatenate([grad.T, zero], axis=1).astype(BF)
                both_s[1, at, :] = jnp.concatenate([zero, query.astype(F32).T], axis=1).astype(BF)
                held = o_refs[s][:, cut].astype(F32)
                delta_s[i] = jnp.sum(held * grad, axis=0, keepdims=True)

    here = pl.ds(pl.multiple_of(j * blk, blk), blk)
    keys_t = kt_s[:, here]
    values = v_s[here, 0:HD]

    def pair(i, diagonal):
        at = pl.ds(pl.multiple_of(i * blk, blk), blk)
        s = mm(k_s[here, :], wide_s[:, at])
        p = jnp.exp2(s * SCALE2 - lse_ref[i])
        if diagonal:
            p = jnp.where(causal(blk), p, 0.0)
        dp = mm(values, dot_s[:, at])
        ds = (p * (dp - delta_s[i])).astype(BF)
        return mm(p.astype(BF), both_s[0, at, :]) + mm(ds, both_s[1, at, :]), mm(keys_t, ds)

    acc_s[...], dq = pair(j, True)
    dq_ref[:, here] += dq

    def step_two(t, carry):
        i = j + 1 + 2 * t
        (kv_0, dq_0), (kv_1, dq_1) = pair(i, False), pair(i + 1, False)
        acc_s[...] += kv_0 + kv_1
        at = pl.ds(pl.multiple_of(i * blk, blk), 2 * blk)
        dq_ref[:, at] += jnp.concatenate([dq_0, dq_1], axis=1)
        return carry

    def step(i, carry):
        kv, dq = pair(i, False)
        acc_s[...] += kv
        dq_ref[:, pl.ds(pl.multiple_of(i * blk, blk), blk)] += dq
        return carry

    high = jnp.where((j + 1) * blk <= first_len, (first_len + blk - 1) // blk, count)
    pairs = (high - j - 1) // 2
    lax.fori_loop(0, pairs, step_two, 0)
    lax.fori_loop(j + 1 + 2 * pairs, high, step, 0)
    both = acc_s[...].T
    out_ref[0:HD, :] = (dq_ref[:, here] * 0.125).astype(BF)
    out_ref[HD : 2 * HD, :] = (both[HD:, :] * 0.125).astype(BF)
    out_ref[2 * HD :, :] = both[:HD, :].astype(BF)
    for s in range(GROUP):

        @pl.when((j // per) ^ place == s)
        def _():
            out_refs[s][:, pl.ds(pl.multiple_of((j % per) * blk, blk), blk)] = out_ref[...]


def attend_back(at, qkv, do, o, lse):
    features, rows = qkv[0].shape
    blk = min(512, rows)
    per = rows // blk
    count = GROUP * per
    return call(
        partial(back_kernel, blk, per, count),
        "attend_back",
        at,
        (count,),
        [fixed((features, rows))] * GROUP
        + [fixed((HD, rows))] * (2 * GROUP)
        + [fixed((count, 1, blk))],
        [fixed((features, rows))] * GROUP,
        [like((features, rows), BF)] * GROUP,
        (*qkv, *do, *o, lse),
        scratch=[
            pltpu.VMEM((HD, GROUP * rows), F32),
            pltpu.VMEM((features, blk), BF),
            pltpu.VMEM((GROUP * rows, 128), BF),
            pltpu.VMEM((HD, GROUP * rows), BF),
            pltpu.VMEM((GROUP * rows, 128), BF),
            pltpu.VMEM((128, GROUP * rows), BF),
            pltpu.VMEM((HD, GROUP * rows), BF),
            pltpu.VMEM((2, GROUP * rows, 128), BF),
            pltpu.VMEM((count, 1, blk), F32),
            pltpu.VMEM((blk, 128), F32),
        ],
        vmem=36,
    )


def stack_kernel(at_ref, *refs):
    ins, out_ref = refs[:GROUP], refs[GROUP]
    for s in range(GROUP):
        head = pl.ds(pl.multiple_of((at_ref[0] ^ s) * HD, HD), HD)
        out_ref[head, :] = ins[s][...]


def stack(at, heads):
    rows = heads[0].shape[1]
    return call(
        stack_kernel,
        "stack",
        at,
        (1,),
        [fixed((HD, rows))] * GROUP,
        fixed((GROUP * HD, rows)),
        like((GROUP * HD, rows), BF),
        heads,
    )


def unsplit_kernel(at_ref, *refs):
    ins, outs = refs[:4], refs[4:]
    cols = ins[0].shape[1]
    for r in range(4):
        lanes = pl.ds(pl.multiple_of(((at_ref[1] + r) % 4) * cols, cols), cols)
        for s in range(GROUP):
            head = pl.ds(pl.multiple_of((at_ref[0] ^ s) * HD, HD), HD)
            outs[s][:, lanes] = ins[r][head, :]


def unsplit(at, pieces):
    shape = (HD, 4 * pieces[0].shape[1])
    return call(
        unsplit_kernel,
        "unsplit",
        at,
        (1,),
        [fixed(pieces[0].shape)] * 4,
        [fixed(shape)] * GROUP,
        [like(shape, BF)] * GROUP,
        pieces,
    )


def heads_of(mine, r, features):
    return pl.ds(pl.multiple_of(((mine + 4 - r) % 4) * features, features), features)


def mid_kernel(at_ref, *refs):
    pieces, (w_ref, x_ref, gain_ref, bias_ref, h_ref, b_ref) = refs[:6], refs[6:]
    h = x_ref[...].astype(F32)
    for r, piece in enumerate(in_order(at_ref[1], *[ref[...] for ref in pieces])):
        rows = heads_of(at_ref[1], 4 - r, piece.shape[0])
        h = h + mm(turned(piece), w_ref[rows, :])

    @pl.when(pl.program_id(0) == 0)
    def _():
        h_ref[...] = h

    normal, _ = normalize(h)
    b_ref[...] = (normal * gain_ref[...] + bias_ref[...]).astype(BF)


def mid(at, pieces, w_o, tokens, gain, bias):
    features, rows = pieces[0].shape
    width, quarter = tokens.shape[1], rows // 4
    return call(
        mid_kernel,
        "mid",
        at,
        (4,),
        [pl.BlockSpec((features, quarter), lambda q, n: (0, (n[1] + q) % 4))] * 6
        + [fixed(w_o.shape)]
        + [pl.BlockSpec((quarter, width), lambda q, n: ((n[1] + q) % 4, 0))]
        + [fixed((1, width))] * 2,
        [fixed((quarter, width)), pl.BlockSpec((quarter, width), lambda q, n: (q, 0))],
        [like((quarter, width), F32), like((rows, width), BF)],
        (*pieces, w_o, tokens, gain, bias),
    )


def add_up(refs):
    total = refs[0][...]
    for ref in refs[1:]:
        total = total + ref[...].astype(F32)
    return total


def mid_back_kernel(at_ref, *refs):
    shares, (w_ref, h_ref, dy_ref, gain_ref, dh_ref, low_ref, sums_ref) = refs[:4], refs[4:11]
    do_refs = refs[11:]
    db = add_up(shares)
    normal, scale = normalize(h_ref[...])
    dh = dy_ref[...].astype(F32) + norm_back(db, gain_ref[...], normal, scale)
    dh_ref[...] = dh
    low = dh.astype(BF)
    low_ref[...] = low
    sums_ref[0:1, :] = jnp.sum(db * normal, axis=0, keepdims=True)
    sums_ref[1:2, :] = jnp.sum(db, axis=0, keepdims=True)
    for r in range(4):
        rows = heads_of(at_ref[1], r, do_refs[r].shape[0])
        do_refs[r][...] = mm_t(w_ref[rows, :], low).astype(BF)


def mid_back(at, shares, w_o, h, dy, gain):
    quarter, width = h.shape
    whole = fixed((quarter, width))
    piece = (w_o.shape[0] // 4, quarter)
    return call(
        mid_back_kernel,
        "mid_back",
        at,
        (1,),
        [whole] * 4 + [fixed(w_o.shape), whole, whole, fixed((1, width))],
        [whole] * 2 + [fixed((2, width))] + [fixed(piece)] * 4,
        [like((quarter, width), F32), like((quarter, width), BF), like((2, width), F32)]
        + [like(piece, BF)] * 4,
        (*shares, w_o, h, dy, gain),
    )


def first_back_kernel(at_ref, *refs):
    shares = refs[:4]
    x_ref, dh_ref, gain_ref, out_ref = refs[4:]
    d_a = add_up(shares)
    normal, scale = normalize(x_ref[...].astype(F32))
    out_ref[...] = (dh_ref[...] + norm_back(d_a, gain_ref[...], normal, scale)).astype(BF)


def first_back(at, shares, tokens, dh, gain):
    quarter, width = dh.shape
    return call(
        first_back_kernel,
        "first_back",
        at,
        (1,),
        [fixed((quarter, width))] * 4
        + [pl.BlockSpec((quarter, width), lambda i, n: (n[1], 0))]
        + [fixed((quarter, width)), fixed((1, width))],
        fixed((quarter, width)),
        like((quarter, width), BF),
        (*shares, tokens, dh, gain),
    )


def in_order(mine, own, right, left, far, right_two, left_two):
    one = jnp.where(mine == 3, far, left)
    two = jnp.where(mine < 2, left_two, right_two)
    three = jnp.where(mine == 0, far, right)
    return own, one, two, three


def one_hot(slots, dest):
    return jnp.where(slots == dest, 1.0, 0.0).astype(BF)


def dispatch_kernel(at_ref, dest_ref, rows_ref, out_ref, spread_s):
    blk, rows = min(256, spread_s.shape[0]), dest_ref.shape[1]

    @pl.when(pl.program_id(0) == 0)
    def _():
        slot = lax.broadcasted_iota(jnp.int32, (blk, rows), 0)
        for start in range(0, spread_s.shape[0], blk):
            spread_s[start : start + blk, :] = one_hot(slot + start, dest_ref[...])

    out_ref[...] = mm(spread_s[...], rows_ref[...]).astype(BF)


def columns(rows, width):
    return pl.BlockSpec((rows, width), lambda i, n: (0, i))


def dispatch(at, dest_row, values, slots):
    rows, width = values.shape
    blk = min(256, width)
    return call(
        dispatch_kernel,
        "dispatch",
        at,
        (width // blk,),
        [fixed((1, rows)), columns(rows, blk)],
        columns(slots, blk),
        like((slots, width), BF),
        (dest_row, values),
        scratch=[pltpu.VMEM((slots, rows), BF)],
    )


def join_kernel(at_ref, *refs):
    pieces, out_ref = refs[:6], refs[6]
    r = pl.program_id(0)
    for place, piece in enumerate(in_order(at_ref[1], *[ref[...] for ref in pieces])):

        @pl.when(r == place)
        def _():
            out_ref[...] = piece


def join(at, pieces):
    each, width = pieces[0].shape
    return call(
        join_kernel,
        "join",
        at,
        (4,),
        [fixed((each, width))] * 6,
        pl.BlockSpec((each, width), lambda r, n: ((n[1] + r) % 4, 0)),
        like((4 * each, width), BF),
        pieces,
    )


def write_shares(mine, total, own_ref, one_ref, two_ref, three_ref, end_ref):
    rows = own_ref.shape[0]
    own_ref[...] = total[:rows]
    one, two, three = [total[r * rows : (r + 1) * rows].astype(BF) for r in (1, 2, 3)]
    one_ref[...] = one
    two_ref[...] = two
    three_ref[...] = three
    end_ref[...] = jnp.where(mine == 0, three, one)


def share_shapes(rows, width):
    return [like((rows, width), F32)] + [like((rows, width), BF)] * 4


def combine_kernel(count, whole, at_ref, *refs):
    dests, backs = refs[:count], refs[count : 2 * count]
    base_ref, refs, pick_s = refs[2 * count], refs[2 * count + 1 : -1], refs[-1]
    rows, slots = base_ref.shape[0], backs[0].shape[0]
    blk = rows // 4

    @pl.when(pl.program_id(0) == 0)
    def _():
        lane = lax.broadcasted_iota(jnp.int32, (blk, slots), 1)
        for k in range(count):
            for start in range(0, rows, blk):
                dest = dests[k][start : start + blk, :]
                pick_s[start : start + blk, k * slots : (k + 1) * slots] = one_hot(lane, dest)

    total = base_ref[...].astype(F32)
    for k in range(count):
        total = total + mm(pick_s[:, k * slots : (k + 1) * slots], backs[k][...])
    mine = at_ref[1]
    if whole:
        h_ref, out_ref = refs
        for r in range(4):
            part = total[r * blk : (r + 1) * blk]
            if r == 0:
                part = part + h_ref[...]
            place = pl.ds(pl.multiple_of(((mine + r) % 4) * blk, blk), blk)
            out_ref[place, :] = part.astype(BF)
    else:
        write_shares(mine, total, *refs)


def combine(at, dests, backs, base, h=None):
    count, (slots, width), rows = len(backs), backs[0].shape, base.shape[0]
    blk = min(256, width)
    whole = h is not None
    quarter = columns(rows // 4, blk)
    return call(
        partial(combine_kernel, count, whole),
        "combine",
        at,
        (width // blk,),
        [fixed((rows, 1))] * count
        + [columns(slots, blk)] * count
        + [columns(rows, blk)]
        + [quarter] * whole,
        columns(rows, blk) if whole else [quarter] * 5,
        like(base.shape, BF) if whole else share_shapes(rows // 4, width),
        (*dests, *backs, base) + ((h,) if whole else ()),
        scratch=[pltpu.VMEM((rows, count * slots), BF)],
    )


def mm_t(a, b):
    return lax.dot_general(a, b, (((1,), (1,)), ((), ())), preferred_element_type=F32)


def gelu_both(u):
    c = 0.7978845608028654
    square = u * u
    t = jnp.tanh(u * (c + (c * 0.044715) * square))
    half = 0.5 + 0.5 * t
    slope = half + (0.5 * u) * (1.0 - t * t) * (c + (3.0 * c * 0.044715) * square)
    return u * half, slope


def high_low(value):
    high = value.astype(BF)
    return high, (value - high.astype(F32)).astype(BF)


def two_coefs(logits, lane, experts):
    inside = (lane >= experts) & (lane < experts + 2)
    top = jnp.max(jnp.where(inside, logits, HIDE), axis=1, keepdims=True)
    e = jnp.where(inside, jnp.exp(logits - top), 0.0)
    e = e / jnp.sum(e, axis=1, keepdims=True)
    first = jnp.sum(jnp.where(lane == experts, e, 0.0), axis=1, keepdims=True)
    second = jnp.sum(jnp.where(lane == experts + 1, e, 0.0), axis=1, keepdims=True)
    return first, second


def small_back(d_small, rows, w_small_ref, small_ref, i):
    high, low = high_low(d_small)
    w_small = w_small_ref[...]
    high_t, low_t = high_low(d_small.T)

    @pl.when(i == 0)
    def _():
        small_ref[...] = jnp.zeros(small_ref.shape, F32)

    small_ref[...] += mm(high_t, rows) + mm(low_t, rows)
    return mm_t(high, w_small) + mm_t(low, w_small)


def expert_kernel(experts, half, at_ref, rows_ref, dy_ref, up_ref, down_ref, w_small_ref, *outs):
    if half:
        outs = outs[5:]
    rows_out_ref, hid_ref, dy_out_ref, deu_ref, y_ref, d_rows_ref, small_ref = outs
    rows = rows_ref[...]
    rows_out_ref[...] = rows
    up = mm(rows, up_ref[...])
    logits = mm(rows, w_small_ref[...])
    lane = lax.broadcasted_iota(jnp.int32, logits.shape, 1)
    routed = lane < experts
    top = jnp.max(jnp.where(routed, logits, HIDE), axis=1, keepdims=True)
    probs = jnp.where(routed, jnp.exp(logits - top), 0.0)
    probs = probs / jnp.sum(probs, axis=1, keepdims=True)
    own = jnp.where(lane == at_ref[2], 1.0, 0.0)
    gate = jnp.sum(probs * own, axis=1, keepdims=True)
    first, second = two_coefs(logits, lane, experts)
    weight = second * gate
    dy = dy_ref[...].reshape(rows.shape).astype(F32)
    d_y = (weight * dy).astype(BF)
    dy_out_ref[...] = d_y
    d_hidden = mm_t(d_y, down_ref[...])
    hidden, slope = gelu_both(up)
    hidden = hidden.astype(BF)
    hid_ref[...] = hidden
    d_up = (d_hidden * slope).astype(BF)
    deu_ref[...] = d_up
    y = mm(hidden, down_ref[...])
    y_ref[...] = (weight * y).astype(BF).reshape(y_ref.shape)
    along = gate * jnp.sum(dy * y, axis=1, keepdims=True)
    mixed = first * second * along
    d_small = (second * along) * (own - probs)
    d_small = jnp.where(routed, d_small, 0.0)
    d_small = d_small + jnp.where(lane == experts + 1, mixed, 0.0)
    d_small = d_small - jnp.where(lane == experts, mixed, 0.0)
    d_rows = mm_t(d_up, up_ref[...]) + small_back(d_small, rows, w_small_ref, small_ref, pl.program_id(0))
    d_rows_ref[...] = d_rows.astype(BF)


def expert_rows(at, rows, dy, w_up, w_down, w_small, experts, half, before):
    count, width = rows.shape
    hid, lanes = w_up.shape[1], w_small.shape[1]
    blk = min(512, count)
    capacity = count // dy.shape[0]
    steps = count // blk
    moving = pl.BlockSpec((blk, width), lambda i, n: (i, 0))
    slots = pl.BlockSpec((blk // capacity, capacity, width), lambda i, n: (i, half, 0))
    kept = [pl.BlockSpec((blk, size), lambda i, n: (i + half * steps, 0)) for size in (width, hid, width, hid)]
    return call(
        partial(expert_kernel, experts, half),
        "expert_rows",
        at,
        (steps,),
        [
            moving,
            slots,
            fixed((width, hid)),
            fixed((hid, width)),
            fixed((width, lanes)),
        ]
        + [pl.BlockSpec(memory_space=pl.ANY)] * (5 * half),
        kept + [slots, moving, fixed((lanes, width))],
        [like((2 * count, size), BF) for size in (width, hid, width, hid)]
        + [like(dy.shape, BF), like((count, width), BF)]
        + [like((lanes, width), F32)],
        (rows, dy, w_up, w_down, w_small, *before),
        alias={6 + k: k for k in range(5)} if half else None,
        vmem=56,
    )


def dense_kernel(experts, at_ref, rows_ref, dy_ref, in_ref, out_ref, w_small_ref, *outs):
    hid_ref, grad_ref, d_up_ref, mix_ref, db_ref, small_ref = outs
    rows = rows_ref[...]
    up = mm(rows, in_ref[...])
    logits = mm(rows, w_small_ref[...])
    lane = lax.broadcasted_iota(jnp.int32, logits.shape, 1)
    first, second = two_coefs(logits, lane, experts)
    dy = dy_ref[...].astype(F32)
    grad = (first * dy).astype(BF)
    grad_ref[...] = grad
    d_hidden = mm_t(grad, out_ref[...])
    hidden, slope = gelu_both(up)
    hidden = hidden.astype(BF)
    hid_ref[...] = hidden
    d_up = (d_hidden * slope).astype(BF)
    d_up_ref[...] = d_up
    dense = mm(hidden, out_ref[...])
    mix_ref[...] = first * dense
    mixed = first * second * jnp.sum(dy * dense, axis=1, keepdims=True)
    d_small = jnp.where(lane == experts, mixed, 0.0) - jnp.where(lane == experts + 1, mixed, 0.0)
    db_ref[...] = mm_t(d_up, in_ref[...]) + small_back(d_small, rows, w_small_ref, small_ref, pl.program_id(0))


def dense_rows(at, rows, dy, w_in, w_out, w_small, experts):
    (count, width), hid, lanes = rows.shape, w_in.shape[1], w_small.shape[1]
    blk = min(512, count)
    row_out = pl.BlockSpec((blk, width), lambda i, n: (i, 0))
    hid_out = pl.BlockSpec((blk, hid), lambda i, n: (i, 0))
    return call(
        partial(dense_kernel, experts),
        "dense_rows",
        at,
        (count // blk,),
        [row_out, row_out, fixed((width, hid)), fixed((hid, width)), fixed((width, lanes))],
        [hid_out, row_out, hid_out, row_out, row_out, fixed((lanes, width))],
        [
            like((count, hid), BF),
            like((count, width), BF),
            like((count, hid), BF),
            like((count, width), F32),
            like((count, width), F32),
            like((lanes, width), F32),
        ],
        (rows, dy, w_in, w_out, w_small),
        vmem=56,
    )


def turned(value):
    return value.astype(F32).T.astype(BF)


def dense_grads_kernel(at_ref, b_ref, d_up_ref, grad_ref, hid_ref, keep_ref, give_ref):
    width = d_up_ref.shape[1]
    first = mm(turned(b_ref[...]), d_up_ref[...]).astype(BF)
    second = mm(turned(grad_ref[...]), hid_ref[...]).astype(BF)
    half = pl.num_programs(0) // 2
    for side, ref in ((0, keep_ref), (1, give_ref)):

        @pl.when(pl.program_id(0) // half == side)
        def _():
            ref[0, :, :width] = first
            ref[0, :, width:] = second


def dense_grads(at, b, d_up, grad, hidden, parts):
    (rows, width), hid = b.shape, hidden.shape[1]
    own, half, bits = width // parts, parts // 2, parts.bit_length() - 1

    def part(q, n):
        turned_q = sum([((q // 2**k) % 2) * 2 ** (bits - 1 - k) for k in range(bits)])
        return turned_q ^ n[2]

    column = pl.BlockSpec((rows, own), lambda q, n: (0, part(q, n)))
    shape = (1, own, 2 * hid)
    return call(
        dense_grads_kernel,
        "dense_grads",
        at,
        (parts,),
        [column, fixed((rows, hid)), column, fixed((rows, hid))],
        [
            pl.BlockSpec(shape, lambda q, n: (jnp.minimum(q, half - 1), 0, 0)),
            pl.BlockSpec(shape, lambda q, n: (jnp.maximum(q - half, 0), 0, 0)),
        ],
        [like((half, own, 2 * hid), BF)] * 2,
        (b, d_up, grad, hidden),
    )


def attention_grads_kernel(experts, at_ref, *refs):
    grads, o_refs, refs = refs[:GROUP], refs[GROUP : GROUP + 6], refs[GROUP + 6 :]
    a_ref, dh_ref, w_ref, gain_ref, bias_ref, sums_ref = refs[:6]
    small_refs, (out_ref, all_s) = refs[6:-2], refs[-2:]
    heads, features = GROUP * HD, grads[1].shape[0]
    products, plain = 0.0, 0.0
    for k in range(GROUP):
        head = at_ref[0] ^ k
        rows = pl.ds(pl.multiple_of(head * features, features), features)
        grad = grads[k][...]
        weight = w_ref[head].astype(F32)
        total = mm(grad, a_ref[...])
        all_s[rows, :] = total
        each = jnp.sum(grad.astype(F32), axis=1, keepdims=True)
        products = products + jnp.sum(total * weight, axis=0, keepdims=True)
        plain = plain + jnp.sum(each * weight, axis=0, keepdims=True)
    first = GROUP * features
    for r, piece in enumerate(in_order(at_ref[1], *[ref[...] for ref in o_refs])):
        rows = pl.ds(pl.multiple_of(first + ((at_ref[1] + r) % 4) * heads, heads), heads)
        all_s[rows, :] = mm(piece, dh_ref[...])
    first += 4 * heads
    small = add_up(small_refs)
    row = lax.broadcasted_iota(jnp.int32, small.shape, 0)
    d_gain = (products - bias_ref[...] * plain) / gain_ref[...]
    for k, sums in enumerate((sums_ref[0:1, :], sums_ref[1:2, :], d_gain, plain)):
        small = jnp.where(row == experts + 2 + k, sums, small)
    all_s[first:, :] = small
    out_ref[...] = all_s[...].T.astype(BF)


def attention_grads(at, grads, o, a, dh, w_heads, gain, bias, sums, small, experts):
    rows, width = a.shape
    features, lanes = grads[0].shape[0], small[0].shape[0]
    piece = pl.BlockSpec((o[0].shape[0], dh.shape[0]), lambda i, n: (0, n[1]))
    height = GROUP * features + 4 * o[0].shape[0] + lanes
    blk = min(256, width)
    return call(
        partial(attention_grads_kernel, experts),
        "attention_grads",
        at,
        (width // blk,),
        [fixed((features, rows))] * GROUP
        + [piece] * 6
        + [columns(rows, blk), columns(dh.shape[0], blk)]
        + [pl.BlockSpec((GROUP, features, blk), lambda i, n: (0, 0, i))]
        + [columns(1, blk)] * 2
        + [columns(2, blk)]
        + [columns(lanes, blk)] * len(small),
        pl.BlockSpec((blk, height), lambda i, n: (i, 0)),
        like((width, height), BF),
        (*grads, *o, a, dh, w_heads, gain, bias, sums, *small),
        scratch=[pltpu.VMEM((height, blk), F32)],
    )


def project_kernel(at_ref, *refs):
    grads, w_ref, outs, turned_s = refs[:GROUP], refs[GROUP], refs[GROUP + 1 : -1], refs[-1]
    rows = turned_s.shape[1]
    blk = rows // 4

    @pl.when(pl.program_id(0) == 0)
    def _():
        for s in range(GROUP):
            for r in range(4):
                lanes = pl.ds(pl.multiple_of(((at_ref[1] + r) % 4) * blk, blk), blk)
                turned_s[s, r * blk : (r + 1) * blk, :] = turned(grads[s][:, lanes])

    total = 0.0
    for s in range(GROUP):
        total = total + mm(turned_s[s], w_ref[at_ref[0] ^ s])
    write_shares(at_ref[1], total, *outs)


def project_back(at, grads, w_heads):
    features, rows = grads[0].shape
    width = w_heads.shape[2]
    blk = min(256, width)
    return call(
        project_kernel,
        "project_back",
        at,
        (width // blk,),
        [fixed((features, rows))] * GROUP
        + [pl.BlockSpec((GROUP, features, blk), lambda i, n: (0, 0, i))],
        [columns(rows // 4, blk)] * 5,
        share_shapes(rows // 4, width),
        (*grads, w_heads),
        scratch=[pltpu.VMEM((GROUP, rows, features), BF)],
    )


def hop(value, *pairs):
    return lax.ppermute(value, "mp", pairs)


def rotate(value, steps):
    return hop(value, *[(s, (s + steps) % 4) for s in range(4)])


def gather_near(own):
    right = hop(own, (0, 1), (1, 2), (2, 3))
    left = hop(own, (1, 0), (2, 1), (3, 2))
    return own, right, left, hop(own, (0, 3), (3, 0))


def gather_far(near):
    _, right, left, _ = near
    return *near, hop(right, (1, 2), (2, 3)), hop(left, (1, 0), (2, 1))


def gather_pieces(own):
    return gather_far(gather_near(own))


def scatter_far(shares):
    _, _, two, _, end = shares
    return hop(two, (2, 1), (3, 2)), hop(two, (0, 1), (1, 2)), hop(end, (0, 3), (3, 0))


def scatter_near(shares, came):
    own, one, _, three, _ = shares
    from_right, from_left, from_end = came
    three = (three.astype(F32) + from_right.astype(F32)).astype(BF)
    one = (one.astype(F32) + from_left.astype(F32)).astype(BF)
    return own, hop(three, (1, 0), (2, 1), (3, 2)), hop(one, (0, 1), (1, 2), (2, 3)), from_end


def group_swap(value, s):
    count = lax.axis_size("dp")
    return lax.ppermute(value, "dp", [(t, t ^ s) for t in range(count)])


def expert_swap(value, experts):
    wide = value.reshape(experts, value.shape[0] // experts, value.shape[1])
    return lax.all_to_all(wide, "dp", 0, 0, tiled=True).reshape(value.shape)


def roll_rows(value, start):
    twice = jnp.concatenate([value, value], axis=0)
    return lax.dynamic_slice_in_dim(twice, start, value.shape[0], 0)


def add_halves(keep, came):
    return (keep.astype(F32) + came.astype(F32)).astype(BF)


def body(
    tokens,
    cotangent,
    ln_gains,
    ln_biases,
    w_qkv,
    w_o,
    w_in,
    w_out,
    w_router,
    w_coef,
    w_up,
    w_down,
    routes,
    long_group,
):
    rows, width = tokens.shape
    dps = lax.axis_size("dp")
    mine, position = lax.axis_index("mp"), lax.axis_index("dp")
    quarter = rows // 4
    start = mine * quarter
    heads_loc = w_qkv.shape[2] // HD
    hid = w_in.shape[1]
    experts = w_router.shape[1]
    capacity = max(2, 2 * rows // experts)
    half = capacity // 2
    barrier = lax.optimization_barrier
    first_len = lax.dynamic_index_in_dim(long_group, position // GROUP, 0, keepdims=False)
    at = jnp.stack([position % GROUP, mine, position, first_len]).astype(jnp.int32)
    gains = [ln_gains[0:1], ln_gains[1:2]]
    biases = [ln_biases[0:1], ln_biases[1:2]]
    w_o_all = lax.all_gather(w_o, "mp", axis=0, tiled=True)

    w_heads = w_qkv.reshape(width, 3, heads_loc, HD).transpose(2, 1, 3, 0)
    w_heads = w_heads.reshape(heads_loc, 3 * HD, width)
    a_r, *qkv = project(at, tokens, gains[0], biases[0], w_heads)
    qkv = [qkv[0]] + [group_swap(qkv[s], s) for s in (1, 2, 3)]

    route = roll_rows(routes, start)[:, 0]
    picked = (route[:, None] == jnp.arange(experts, dtype=jnp.int32)[None, :]).astype(jnp.int32)
    slot = jnp.sum((jnp.cumsum(picked, axis=0) - picked) * picked, axis=1)
    dy_b = roll_rows(cotangent, start)
    full = route * capacity + slot
    send_dy = dispatch(at, full[None, :], dy_b, experts * capacity)
    *qkv, send_dy = barrier((*qkv, send_dy))
    in_half = [slot < half, slot >= half]
    dests = [
        jnp.where(in_half[k], route * half + slot - k * half, -1).astype(jnp.int32) for k in (0, 1)
    ]

    *o_t, lse = attend(at, qkv)
    *o_t, w_o_all = barrier((*o_t, w_o_all))
    o_heads = [o_t[0]] + [group_swap(o_t[s], s) for s in (1, 2, 3)]
    lanes = -(-(experts + 2) // 128) * 128
    w_small = jnp.concatenate(
        [w_router, w_coef, jnp.zeros((width, lanes - experts - 2), BF)], axis=1
    )
    *o_heads, send_dy, w_small = barrier((*o_heads, send_dy, w_small))
    got_dy = expert_swap(send_dy, experts).reshape(experts, capacity, width)
    o_pieces = gather_pieces(stack(at, o_heads))
    h, b_r = mid(at, o_pieces, w_o_all, tokens, gains[1], biases[1])

    send_0 = dispatch(at, dests[0][None, :], b_r, experts * half)
    send_0, got_dy = barrier((send_0, got_dy))
    got_0 = expert_swap(send_0, experts)
    send_1 = dispatch(at, dests[1][None, :], b_r, experts * half)
    b_r, send_1 = barrier((b_r, send_1))
    hidden, dense_grad, d_up, mix_base, db_base, small_t = dense_rows(
        at, b_r, dy_b, w_in, w_out, w_small, experts
    )
    send_1, got_0, db_base = barrier((send_1, got_0, db_base))
    got_1 = expert_swap(send_1, experts)

    *kept, d_rows_0, small_0 = expert_rows(
        at, got_0, got_dy, w_up[0], w_down[0], w_small, experts, 0, ()
    )
    back_0 = expert_swap(d_rows_0, experts)
    *kept, d_rows_1, small_1 = expert_rows(
        at, got_1, got_dy, w_up[0], w_down[0], w_small, experts, 1, kept
    )
    got, hidden_e, d_y, d_eu, back_y = kept
    back_1 = expert_swap(d_rows_1, experts)
    d_rows_1, b_r = barrier((d_rows_1, b_r))
    halving = width == dps * 128
    if halving:
        grads = dense_grads(at, b_r, d_up, dense_grad, hidden, dps)
    else:
        grads = [ein("td,tf->df", b_r, d_up).astype(BF), ein("td,tf->df", dense_grad, hidden).astype(BF)]
    back_0, back_1, back_y, *grads = barrier((back_0, back_1, back_y, *grads))

    dest_cols = [dest[:, None] for dest in dests]
    tok_y = expert_swap(back_y.reshape(experts * capacity, width), experts)
    shares = combine(at, dest_cols, [back_0, back_1], db_base)
    far = scatter_far(shares)
    *far, g_0, g_1 = barrier((*far, *grads))
    grads = [g_0, g_1]
    shares = scatter_near(shares, far)

    mix = combine(at, [full[:, None]], [tok_y], mix_base, h)
    *shares, mix = barrier((*shares, mix))
    output = lax.psum(mix, "mp")
    dh, dh_r, sums_2, *do_q = mid_back(at, shares, w_o_all, h, dy_b, gains[1])
    do_q = [do_q[0]] + [rotate(do_q[r], -r) for r in (1, 2, 3)]
    do_heads = unsplit(at, do_q)
    do_t = [do_heads[0]] + [group_swap(do_heads[s], s) for s in (1, 2, 3)]
    if halving:
        came_1 = group_swap(grads[1], 1)
        half = dps // 4
        give = add_halves(grads[0][half:], came_1[half:])
        *do_t, give = barrier((*do_t, give))
        came_2 = group_swap(give, 2)
    d_qkv = attend_back(at, qkv, do_t, o_t, lse)
    if halving:
        keep = add_halves(grads[0][:half], came_1[:half])
        *d_qkv, came_2, keep = barrier((*d_qkv, came_2, keep))
        grads = add_halves(keep, came_2)
        bit = 4
        while bit < dps:
            half = grads.shape[0] // 2
            grads = add_halves(grads[:half], group_swap(grads[half:], bit))
            bit *= 2
        grads = [grads[0][:, :hid], grads[0][:, hid:]]
    else:
        grads = [lax.psum_scatter(grad, "dp", scatter_dimension=0, tiled=True) for grad in grads]

    d_own, got, hidden_e, d_y, d_eu = barrier((d_qkv[0], got, hidden_e, d_y, d_eu))
    d_qkv = [d_own] + [group_swap(d_qkv[s], s) for s in (1, 2, 3)]
    grad_down = ein("rf,rd->fd", hidden_e, d_y)
    *d_qkv, grad_down = barrier((*d_qkv, grad_down))
    shares = project_back(at, d_qkv, w_heads)
    far = scatter_far(shares)
    grads_a = attention_grads(
        at, d_qkv, o_pieces, a_r, dh_r, w_heads, gains[0], biases[0], sums_2, (small_0, small_1, small_t), experts
    )
    grad_up = ein("rd,rf->df", got, d_eu)
    grads_a, output, grad_up, *far = barrier((grads_a, output, grad_up, *far))
    grads_a = lax.psum_scatter(grads_a, "dp", scatter_dimension=0, tiled=True).T
    shares = scatter_near(shares, far)
    grad_q = first_back(at, shares, tokens, dh, gains[0])
    grad_tokens = join(at, gather_pieces(grad_q))

    own, heads = width // dps, heads_loc * HD
    grad_qkv = grads_a[: 3 * heads].astype(F32).reshape(heads_loc, 3, HD, own).transpose(3, 1, 0, 2)
    grad_qkv = grad_qkv.reshape(own, 3, heads)
    grad_in = grads[0].astype(F32)
    grad_out = grads[1].astype(F32).T
    rest = grads_a[3 * heads : 7 * heads].reshape(4, heads, own)
    small = jnp.broadcast_to(grads_a[7 * heads :], (4, lanes, own))
    rest = lax.all_to_all(jnp.concatenate([rest, small], axis=1), "mp", 0, 0, tiled=True)
    rest = jnp.sum(rest.astype(F32), axis=0)
    grad_o, small = rest[:heads], rest[heads:]
    small_out = small[: experts + 2].T
    return (
        output,
        grad_tokens,
        jnp.stack([small[experts + 4], small[experts + 2]]),
        jnp.stack([small[experts + 5], small[experts + 3]]),
        grad_qkv,
        grad_o,
        grad_in,
        grad_out,
        small_out[:, :experts],
        small_out[:, experts:],
        grad_up[None],
        grad_down[None],
    )


def solution(mesh):
    in_specs = (
        P("dp", None),
        P("dp", None),
        P(),
        P(),
        P(None, None, "mp"),
        P("mp", None),
        P(None, "mp"),
        P("mp", None),
        P(),
        P(),
        P("dp", None, "mp"),
        P("dp", "mp", None),
        P("dp", None),
        P(),
    )
    out_specs = (
        P("dp", None),
        P("dp", None),
        P(None, "dp"),
        P(None, "dp"),
        P("dp", None, "mp"),
        P("mp", "dp"),
        P("dp", "mp"),
        P("mp", "dp"),
        P("dp", None),
        P("dp", None),
        P("dp", None, "mp"),
        P("dp", "mp", None),
    )
    return jax.shard_map(body, mesh=mesh, in_specs=in_specs, out_specs=out_specs, check_vma=False)
```

profile of v0, /device:TPU:0, one launch (start us, length us, event | category | flops | bytes accessed | tf_op | source)
XLA Modules:
  0.0 555.5 jit_solution(11369958703366158399)
XLA Ops:
  12.2 6.9 %project.1 = (bf16[1024,1024]{1,0:T(8,128)(2,1)S(1)}, bf16[192,1024]{1,0:T(8,128)(2,1)S(1)}, bf16[192,1024]{1,0:T(8,128)(2,1)}, bf16[192,1024]{1,0:T(8,128)(2,1)}, bf16[192,1024]{1,0:T(8,128)(2,1)}) custom-call(s32[4]{0:T(128)S(1)} %pad_add_fusion.at_ref, bf16[1024,1024]{1,0:T(8,128)(2,1)} %refs_4_.1, ...), custom_call_target="tpu_custom_call" | custom-call | flops 1048576 | bytes 1048576 | tf_op jit(solution)/shard_map/project/pallas_call | solution.py:30
  20.9 2.5 collective-permute-start.1
  24.6 2.3 reduce-window.6
  27.6 2.3 multiply_add_fusion.1
  30.4 3.4 fusion.rows_ref.dy_ref.refs_6_
  34.5 7.6 %dispatch.3 = bf16[2048,1024]{1,0:T(8,128)(2,1)} custom-call(s32[4]{0:T(128)S(1)} %pad_add_fusion.at_ref, s32[1,1024]{1,0:T(1,128)S(1)} %get-tuple-element.331.dest_ref, bf16[1024,1024]{1,0:T(8,128)(2,1)S(1)} %fusion.rows_ref.dy_ref.refs_6_), custom_call_target="tpu_custom_call" | custom-call | flops 1048576 | bytes 1048576 | tf_op jit(solution)/shard_map/dispatch/pallas_call | solution.py:30
  42.1 15.9 %attend.1 = (bf16[64,1024]{1,0:T(8,128)(2,1)S(1)}, bf16[64,1024]{1,0:T(8,128)(2,1)S(1)}, bf16[64,1024]{1,0:T(8,128)(2,1)S(1)}, bf16[64,1024]{1,0:T(8,128)(2,1)S(1)}, f32[8,1,512]{2,1,0:T(1,128)S(1)}) custom-call(s32[4]{0:T(128)S(1)} %pad_add_fusion.at_ref, bf16[192,1024]{1,0:T(8,128)(2,1)S(1)} %get-tuple-element.141.refs_0_, ...), custom_call_target="tpu_custom_call" | custom-call | flops 1048576 | bytes 1048576 | tf_op jit(solution)/shard_map/attend/pallas_call | solution.py:30
  58.7 1.9 collective-permute-start.4
  61.5 3.6 collective-permute-done.4.refs_2_
  65.1 1.9 collective-permute-done.5.refs_3_
  67.0 8.9 %all-to-all-start = ((bf16[8,256,1024]{2,1,0:T(8,128)(2,1)}), bf16[8,256,1024]{2,1,0:T(8,128)(2,1)}, u32[]{:S(2)}, u32[]{:S(2)}) async-start(bf16[8,256,1024]{2,1,0:T(8,128)(2,1)} %bitcast.72), calls=%async_computation | async-start | bytes 8388608 | tf_op jit(solution)/shard_map/all_to_all | solution.py:912
  77.8 4.6 collective-permute-start.6
  82.4 3.2 collective-permute-start.8
  85.7 7.1 %collective-permute-done.7.refs_2_.refs_6_ = bf16[256,1024]{1,0:T(8,128)(2,1)S(1)} collective-permute-done((bf16[256,1024]{1,0:T(8,128)(2,1)S(1)}, bf16[256,1024]{1,0:T(8,128)(2,1)S(1)}, u32[]{:S(2)}, u32[]{:S(2)}) %collective-permute-start.7) | collective-permute-done | bytes 524320 | tf_op jit(solution)/shard_map/ppermute | solution.py:870
  95.5 10.5 %collective-permute-done.8.refs_3_.refs_7_ = bf16[256,1024]{1,0:T(8,128)(2,1)S(1)} collective-permute-done((bf16[256,1024]{1,0:T(8,128)(2,1)S(1)}, bf16[256,1024]{1,0:T(8,128)(2,1)S(1)}, u32[]{:S(2)}, u32[]{:S(2)}) %collective-permute-start.8) | collective-permute-done | bytes 524320 | tf_op jit(solution)/shard_map/ppermute | solution.py:870
  106.1 11.1 %collective-permute-done.10.refs_5_.refs_9_ = bf16[256,1024]{1,0:T(8,128)(2,1)S(1)} collective-permute-done((bf16[256,1024]{1,0:T(8,128)(2,1)S(1)}, bf16[256,1024]{1,0:T(8,128)(2,1)S(1)}, u32[]{:S(2)}, u32[]{:S(2)}) %collective-permute-start.10) | collective-permute-done | bytes 524320 | tf_op jit(solution)/shard_map/ppermute | solution.py:870
  117.2 8.5 %mid.1 = (f32[256,1024]{1,0:T(8,128)S(1)}, bf16[1024,1024]{1,0:T(8,128)(2,1)}) custom-call(s32[4]{0:T(128)S(1)} %pad_add_fusion.at_ref, bf16[256,1024]{1,0:T(8,128)(2,1)S(1)} %stack.26.refs_0_.refs_4_, bf16[256,1024]{1,0:T(8,128)(2,1)S(1)} %collective-permute-done.6.refs_1_.refs_5_, bf16[256,1024]{1,0:T(8,128)(2,1)S(1)} %collective-permute-done.7.refs_2_.refs_6_, ...), custom_call_target="tpu_custom_call" | custom-call | flops 1048576 | bytes 1048576 | tf_op jit(solution)/shard_map/mid/pallas_call | solution.py:30
  128.2 4.3 dispatch.5
  133.8 4.6 all-to-all-start.1
  139.1 4.3 dispatch.4
  144.7 19.4 %dense_rows.1 = (bf16[1024,1024]{1,0:T(8,128)(2,1)}, bf16[1024,1024]{1,0:T(8,128)(2,1)}, bf16[1024,1024]{1,0:T(8,128)(2,1)}, f32[1024,1024]{1,0:T(8,128)}, f32[1024,1024]{1,0:T(8,128)}, /*index=5*/f32[128,1024]{1,0:T(8,128)}) custom-call(s32[4]{0:T(128)} %copy-done.45, bf16[1024,1024]{1,0:T(8,128)(2,1)} %get-tuple-element.177.rows_ref.b_ref, ...), custom_call_target="tpu_custom_call" | custom-call | flops 1048576 | bytes 1048576 | tf_op jit(solution)/shard_map/dense_rows/pallas_call | solution.py:30
  165.2 4.0 all-to-all-start.3
  169.2 19.6 %expert_rows.2 = (bf16[2048,1024]{1,0:T(8,128)(2,1)}, bf16[2048,1024]{1,0:T(8,128)(2,1)}, bf16[2048,1024]{1,0:T(8,128)(2,1)}, bf16[2048,1024]{1,0:T(8,128)(2,1)}...) custom-call(s32[4]{0:T(128)} %copy-done.45, ...), custom_call_target="tpu_custom_call" | custom-call | flops 1048576 | bytes 1048576 | tf_op jit(solution)/shard_map/expert_rows/pallas_call | solution.py:30
  188.8 6.9 %all-to-all-done.3 = bf16[8,128,1024]{2,1,0:T(8,128)(2,1)S(1)} async-done(((bf16[8,128,1024]{2,1,0:T(8,128)(2,1)}), bf16[8,128,1024]{2,1,0:T(8,128)(2,1)S(1)}, u32[]{:S(2)}, u32[]{:S(2)}) %all-to-all-start.3) | async-done | bytes 2097184 | tf_op jit(solution)/shard_map/all_to_all | solution.py:912
  197.1 3.8 all-to-all-start.2
  200.9 19.7 %expert_rows.3 = (bf16[2048,1024]{1,0:T(8,128)(2,1)}, bf16[2048,1024]{1,0:T(8,128)(2,1)}, bf16[2048,1024]{1,0:T(8,128)(2,1)}, bf16[2048,1024]{1,0:T(8,128)(2,1)}...) custom-call(s32[4]{0:T(128)} %copy-done.45, ...), custom_call_target="tpu_custom_call", output_to_operand_aliasing={{0}: (6, {}), {1}: (7, {}), {2}: (8, {}), {3}: (9, {}), {4}... | custom-call | flops 1048576 | bytes 1048576 | tf_op jit(solution)/shard_map/expert_rows/pallas_call | solution.py:30
  220.6 6.8 %all-to-all-done.2 = bf16[8,128,1024]{2,1,0:T(8,128)(2,1)S(1)} async-done(((bf16[8,128,1024]{2,1,0:T(8,128)(2,1)}), bf16[8,128,1024]{2,1,0:T(8,128)(2,1)S(1)}, u32[]{:S(2)}, u32[]{:S(2)}) %all-to-all-start.2) | async-done | bytes 2097184 | tf_op jit(solution)/shard_map/all_to_all | solution.py:912
  228.8 4.3 all-to-all-start.4
  233.1 11.5 %dense_grads.1 = (bf16[4,128,2048]{2,1,0:T(8,128)(2,1)S(1)}, bf16[4,128,2048]{2,1,0:T(8,128)(2,1)}) custom-call(s32[4]{0:T(128)S(1)} %copy-done.46, bf16[1024,1024]{1,0:T(8,128)(2,1)} %get-tuple-element.177.rows_ref.b_ref, bf16[1024,1024]{1,0:T(8,128)(2,1)} %get-tuple-element.178.d_up_ref, bf16[1024,1024]{1,0:T(8,128)(2,1)} %get-tuple-element.179.grad_ref, ...), custom_call_target="tpu_custom_call" | custom-call | flops 1048576 | bytes 1048576 | tf_op jit(solution)/shard_map/dense_grads/pallas_call | solution.py:30
  245.9 13.9 %all-to-all-done.4 = bf16[8,128,1024]{2,1,0:T(8,128)(2,1)} async-done(((bf16[8,128,1024]{2,1,0:T(8,128)(2,1)}), bf16[8,128,1024]{2,1,0:T(8,128)(2,1)}, u32[]{:S(2)}, u32[]{:S(2)}) %all-to-all-start.4) | async-done | bytes 2097184 | tf_op jit(solution)/shard_map/all_to_all | solution.py:912
  259.8 4.7 all-to-all-start.5
  264.6 8.5 %combine.2 = (f32[256,1024]{1,0:T(8,128)S(1)}, bf16[256,1024]{1,0:T(8,128)(2,1)S(1)}, bf16[256,1024]{1,0:T(8,128)(2,1)S(1)}, bf16[256,1024]{1,0:T(8,128)(2,1)S(1)}, bf16[256,1024]{1,0:T(8,128)(2,1)S(1)}) custom-call(s32[4]{0:T(128)S(1)} %copy-done.46, s32[1024,1]{1,0:T(8,128)S(1)} %copy-done.21, s32[1024,1]{1,0:T(8,128)S(1)} %copy-done.20, ...), custom_call_target="tpu_custom_call" | custom-call | flops 1048576 | bytes 1048576 | tf_op jit(solution)/shard_map/combine/pallas_call | solution.py:30
  274.1 5.8 %collective-permute-start.13 = (bf16[256,1024]{1,0:T(8,128)(2,1)S(1)}, bf16[256,1024]{1,0:T(8,128)(2,1)S(1)}, u32[]{:S(2)}, u32[]{:S(2)}) collective-permute-start(bf16[256,1024]{1,0:T(8,128)(2,1)S(1)} %get-tuple-element.189), channel_id=1, source_target_pairs={{0,3},{3,0},{4,7},{7,4},{8,11},{11,8},{12,15},{15,12},{16,19},{19,... | collective-permute-start | bytes 1572872 | tf_op jit(solution)/shard_map/ppermute | solution.py:870
  281.9 10.7 %collective-permute-done.13.refs_3_ = bf16[256,1024]{1,0:T(8,128)(2,1)S(1)} collective-permute-done((bf16[256,1024]{1,0:T(8,128)(2,1)S(1)}, bf16[256,1024]{1,0:T(8,128)(2,1)S(1)}, u32[]{:S(2)}, u32[]{:S(2)}) %collective-permute-start.13) | collective-permute-done | bytes 524320 | tf_op jit(solution)/shard_map/ppermute | solution.py:870
  292.6 10.2 %collective-permute-done.12 = bf16[256,1024]{1,0:T(8,128)(2,1)S(1)} collective-permute-done((bf16[256,1024]{1,0:T(8,128)(2,1)S(1)}, bf16[256,1024]{1,0:T(8,128)(2,1)S(1)}, u32[]{:S(2)}, u32[]{:S(2)}) %collective-permute-start.12) | collective-permute-done | bytes 524320 | tf_op jit(solution)/shard_map/ppermute | solution.py:870
  303.8 5.2 collective-permute-start.15
  311.5 2.1 all-to-all-done.5
  313.6 9.3 %combine.3 = bf16[1024,1024]{1,0:T(8,128)(2,1)} custom-call(s32[4]{0:T(128)S(1)} %copy-done.46, s32[1024,1]{1,0:T(8,128)S(1)} %copy-done.19, bf16[2048,1024]{1,0:T(8,128)(2,1)} %bitcast.20.refs_1_, f32[1024,1024]{1,0:T(8,128)} %get-tuple-element.197.refs_2_, f32[256,1024]{1,0:T(8,128)S(1)} %copy-done.7), custom_call_target="tpu_custom_call" | custom-call | flops 1048576 | bytes 1048576 | tf_op jit(solution)/shard_map/combine/pallas_call | solution.py:30
  322.9 3.3 collective-permute-done.14.refs_1_
  328.5 4.3 mid_back.1
  335.8 3.4 collective-permute-done.16.refs_1_
  339.2 7.0 %collective-permute-done.17.refs_2_ = bf16[256,256]{1,0:T(8,128)(2,1)S(1)} collective-permute-done((bf16[256,256]{1,0:T(8,128)(2,1)S(1)}, bf16[256,256]{1,0:T(8,128)(2,1)S(1)}, u32[]{:S(2)}, u32[]{:S(2)}) %collective-permute-start.17) | collective-permute-done | bytes 131104 | tf_op jit(solution)/shard_map/ppermute | solution.py:870
  348.7 3.5 add_convert_fusion.1
  353.2 1.9 collective-permute-done.21.refs_7_
  359.2 25.1 %attend_back.1 = (bf16[192,1024]{1,0:T(8,128)(2,1)S(1)}, bf16[192,1024]{1,0:T(8,128)(2,1)S(1)}, bf16[192,1024]{1,0:T(8,128)(2,1)S(1)}, bf16[192,1024]{1,0:T(8,128)(2,1)S(1)}) custom-call(s32[4]{0:T(128)S(1)} %copy-done.46, bf16[192,1024]{1,0:T(8,128)(2,1)S(1)} %get-tuple-element.141.refs_0_, bf16[192,1024]{1,0:T(8,128)(2,1)S(1)} %copy-done.23, ...), custom_call_target="tpu_custom_call" | custom-call | flops 1048576 | bytes 1048576 | tf_op jit(solution)/shard_map/attend_back/pallas_call | solution.py:30
  386.3 10.2 %fusion.10 = f32[1024,1024]{1,0:T(8,128)} fusion(bf16[2048,1024]{1,0:T(8,128)(2,1)} %get-tuple-element.232, bf16[2048,1024]{1,0:T(8,128)(2,1)} %get-tuple-element.233), kind=kOutput, calls=%fused_computation.46 | convolution fusion | flops 4294967296 | bytes 12582912 | tf_op jit(solution)/shard_map/rf,rd->fd/dot_general | solution.py:26
  396.5 7.5 %collective-permute-done.26.refs_3_ = bf16[192,1024]{1,0:T(8,128)(2,1)S(1)} collective-permute-done((bf16[192,1024]{1,0:T(8,128)(2,1)S(1)}, bf16[192,1024]{1,0:T(8,128)(2,1)S(1)}, u32[]{:S(2)}, u32[]{:S(2)}) %collective-permute-start.26) | collective-permute-done | bytes 393248 | tf_op jit(solution)/shard_map/ppermute | solution.py:907
  403.9 6.3 %project_back.1 = (f32[256,1024]{1,0:T(8,128)S(1)}, bf16[256,1024]{1,0:T(8,128)(2,1)S(1)}, bf16[256,1024]{1,0:T(8,128)(2,1)}, bf16[256,1024]{1,0:T(8,128)(2,1)S(1)}, bf16[256,1024]{1,0:T(8,128)(2,1)}) custom-call(s32[4]{0:T(128)S(1)} %copy-done.46, bf16[192,1024]{1,0:T(8,128)(2,1)S(1)} %get-tuple-element.234.refs_0_, ...), custom_call_target="tpu_custom_call" | custom-call | flops 1048576 | bytes 1048576 | tf_op jit(solution)/shard_map/project_back/pallas_call | solution.py:30
  411.1 2.0 collective-permute-start.28
  414.7 6.4 %collective-permute-start.29 = (bf16[256,1024]{1,0:T(8,128)(2,1)}, bf16[256,1024]{1,0:T(8,128)(2,1)S(1)}, u32[]{:S(2)}, u32[]{:S(2)}) collective-permute-start(bf16[256,1024]{1,0:T(8,128)(2,1)} %get-tuple-element.248), channel_id=1, source_target_pairs={{0,3},{3,0},{4,7},{7,4},{8,11},{11,8},{12,15},{15,12},{16,19},{19,... | collective-permute-start | bytes 1572872 | tf_op jit(solution)/shard_map/ppermute | solution.py:870
  421.1 8.3 %fusion.11 = f32[1024,1024]{1,0:T(8,128)} fusion(bf16[2048,1024]{1,0:T(8,128)(2,1)S(1)} %copy-done.63, bf16[2048,1024]{1,0:T(8,128)(2,1)} %get-tuple-element.246), kind=kOutput, calls=%fused_computation.47 | convolution fusion | flops 4294967296 | bytes 12582912 | tf_op jit(solution)/shard_map/rd,rf->df/dot_general | solution.py:26
  429.5 8.6 %attention_grads.1 = bf16[1024,1920]{1,0:T(8,128)(2,1)} custom-call(s32[4]{0:T(128)S(1)} %copy-done.46, bf16[192,1024]{1,0:T(8,128)(2,1)S(1)} %get-tuple-element.234.refs_0_, bf16[192,1024]{1,0:T(8,128)(2,1)S(1)} %collective-permute-done.24.refs_1_, bf16[192,1024]{1,0:T(8,128)(2,1)S(1)} %collective-permute-done.25.refs_2_, ...), custom_call_target="tpu_custom_call" | custom-call | flops 1048576 | bytes 1048576 | tf_op jit(solution)/shard_map/attention_grads/pallas_call | solution.py:30
  438.1 27.0 %all-reduce.2.cloned.1.call-done = bf16[1024,1024]{1,0:T(8,128)(2,1)} async-done(((bf16[1024,1024]{1,0:T(8,128)(2,1)}), bf16[1024,1024]{1,0:T(8,128)(2,1)}) %all-reduce.2.cloned.1.call-update) | async-done | bytes 2097168 | tf_op jit(solution)/shard_map/psum | solution.py:1024
  468.0 4.6 collective-permute-start.31
  472.6 8.1 %collective-permute-done.30.refs_1_ = bf16[256,1024]{1,0:T(8,128)(2,1)S(1)} collective-permute-done((bf16[256,1024]{1,0:T(8,128)(2,1)S(1)}, bf16[256,1024]{1,0:T(8,128)(2,1)S(1)}, u32[]{:S(2)}, u32[]{:S(2)}) %collective-permute-start.30) | collective-permute-done | bytes 524320 | tf_op jit(solution)/shard_map/ppermute | solution.py:870
  483.2 2.5 first_back.1.refs_0_
  487.0 5.0 collective-permute-start.32
  494.5 3.5 collective-permute-start.37
  498.1 2.5 collective-permute-start.34
  503.5 19.9 %reduce-scatter.2.cloned.1.call-done = bf16[128,1920]{1,0:T(8,128)(2,1)} async-done(((bf16[1024,1920]{1,0:T(8,128)(2,1)}), bf16[128,1920]{1,0:T(8,128)(2,1)}) %reduce-scatter.2.cloned.1.call-update) | async-done | bytes 491536 | tf_op jit(solution)/shard_map/reduce_scatter | solution.py:1060
  526.0 4.6 all-to-all-start.6
  533.0 2.0 copy.91
  535.0 2.9 join.1
  540.0 2.3 all-to-all-done.6
  (259 shorter events, 75.9 us)
Async XLA Ops:
  7.2 51.4 %all-gather.2.cloned.1.call-start = ((), (), s32[]{:S(2)}) async-start(), calls=%async_computation.8 | async-start | bytes 2621440 | tf_op jit(solution)/shard_map/all_gather | solution.py:955
  11.6 126.8 %copy-start.45 = (s32[4]{0:T(128)}, s32[4]{0:T(128)S(1)}, u32[]{:S(2)}) copy-start(s32[4]{0:T(128)S(1)} %pad_add_fusion.at_ref) | copy-start | bytes 52
  20.4 21.6 %collective-permute-start = (bf16[192,1024]{1,0:T(8,128)(2,1)}, bf16[192,1024]{1,0:T(8,128)(2,1)S(1)}, u32[]{:S(2)}, u32[]{:S(2)}) collective-permute-start(bf16[192,1024]{1,0:T(8,128)(2,1)} %get-tuple-element.138), channel_id=1, source_target_pairs={{0,4},{4,0},{8,12},{12,8},{16,20},{20,16},{24,28},{28,24},{1,5},{5... | collective-permute-start | bytes 1179656 | tf_op jit(solution)/shard_map/ppermute | solution.py:907
  20.9 21.2 %collective-permute-start.1 = (bf16[192,1024]{1,0:T(8,128)(2,1)}, bf16[192,1024]{1,0:T(8,128)(2,1)S(1)}, u32[]{:S(2)}, u32[]{:S(2)}) collective-permute-start(bf16[192,1024]{1,0:T(8,128)(2,1)} %get-tuple-element.139), channel_id=1, source_target_pairs={{0,8},{4,12},{8,0},{12,4},{16,24},{20,28},{24,16},{28,20},{1,9},{5... | collective-permute-start | bytes 1179656 | tf_op jit(solution)/shard_map/ppermute | solution.py:907
  23.4 18.7 %collective-permute-start.2 = (bf16[192,1024]{1,0:T(8,128)(2,1)}, bf16[192,1024]{1,0:T(8,128)(2,1)S(1)}, u32[]{:S(2)}, u32[]{:S(2)}) collective-permute-start(bf16[192,1024]{1,0:T(8,128)(2,1)} %get-tuple-element.140), channel_id=1, source_target_pairs={{0,12},{4,8},{8,4},{12,0},{16,28},{20,24},{24,20},{28,16},{1,13},{... | collective-permute-start | bytes 1179656 | tf_op jit(solution)/shard_map/ppermute | solution.py:907
  42.1 24.9 %copy-start.22 = (bf16[192,1024]{1,0:T(8,128)(2,1)}, bf16[192,1024]{1,0:T(8,128)(2,1)S(1)}, u32[]{:S(2)}) copy-start(bf16[192,1024]{1,0:T(8,128)(2,1)S(1)} %collective-permute-done.refs_1_) | copy-start | bytes 1179652
  42.1 24.9 %copy-start.24 = (bf16[192,1024]{1,0:T(8,128)(2,1)}, bf16[192,1024]{1,0:T(8,128)(2,1)S(1)}, u32[]{:S(2)}) copy-start(bf16[192,1024]{1,0:T(8,128)(2,1)S(1)} %collective-permute-done.1.refs_2_) | copy-start | bytes 1179652
  42.1 24.9 %copy-start.26 = (bf16[192,1024]{1,0:T(8,128)(2,1)}, bf16[192,1024]{1,0:T(8,128)(2,1)S(1)}, u32[]{:S(2)}) copy-start(bf16[192,1024]{1,0:T(8,128)(2,1)S(1)} %collective-permute-done.2.refs_3_) | copy-start | bytes 1179652
  58.6 2.9 collective-permute-start.3
  58.7 6.3 %collective-permute-start.4 = (bf16[64,1024]{1,0:T(8,128)(2,1)S(1)}, bf16[64,1024]{1,0:T(8,128)(2,1)S(1)}, u32[]{:S(2)}, u32[]{:S(2)}) collective-permute-start(bf16[64,1024]{1,0:T(8,128)(2,1)S(1)} %get-tuple-element.151.refs_10_), channel_id=1, source_target_pairs={{0,8},{4,12},{8,0},{12,4},{16,24},{20,28},{24,16},{28,20},{1,9},{5... | collective-permute-start | bytes 393224 | tf_op jit(solution)/shard_map/ppermute | solution.py:907
  60.6 6.3 %collective-permute-start.5 = (bf16[64,1024]{1,0:T(8,128)(2,1)S(1)}, bf16[64,1024]{1,0:T(8,128)(2,1)S(1)}, u32[]{:S(2)}, u32[]{:S(2)}) collective-permute-start(bf16[64,1024]{1,0:T(8,128)(2,1)S(1)} %get-tuple-element.152.refs_11_), channel_id=1, source_target_pairs={{0,12},{4,8},{8,4},{12,0},{16,28},{20,24},{24,20},{28,16},{1,13},{... | collective-permute-start | bytes 393224 | tf_op jit(solution)/shard_map/ppermute | solution.py:907
  67.0 50.2 %copy-start.58 = (f32[1,1024]{1,0:T(1,128)S(1)}, f32[1,1024]{1,0:T(1,128)}, u32[]{:S(2)}) copy-start(f32[1,1024]{1,0:T(1,128)} %get-tuple-element.327.refs_9_) | copy-start | bytes 12292
  67.0 66.8 %all-to-all-start = ((bf16[8,256,1024]{2,1,0:T(8,128)(2,1)}), bf16[8,256,1024]{2,1,0:T(8,128)(2,1)}, u32[]{:S(2)}, u32[]{:S(2)}) async-start(bf16[8,256,1024]{2,1,0:T(8,128)(2,1)} %bitcast.72), calls=%async_computation | async-start | bytes 8388608 | tf_op jit(solution)/shard_map/all_to_all | solution.py:912
  76.5 16.2 %collective-permute-start.7 = (bf16[256,1024]{1,0:T(8,128)(2,1)S(1)}, bf16[256,1024]{1,0:T(8,128)(2,1)S(1)}, u32[]{:S(2)}, u32[]{:S(2)}) collective-permute-start(bf16[256,1024]{1,0:T(8,128)(2,1)S(1)} %stack.26.refs_0_.refs_4_), channel_id=1, source_target_pairs={{1,0},{2,1},{3,2},{5,4},{6,5},{7,6},{9,8},{10,9},{11,10},{13,12},{... | collective-permute-start | bytes 1572872 | tf_op jit(solution)/shard_map/ppermute | solution.py:870
  77.8 16.8 %collective-permute-start.6 = (bf16[256,1024]{1,0:T(8,128)(2,1)S(1)}, bf16[256,1024]{1,0:T(8,128)(2,1)S(1)}, u32[]{:S(2)}, u32[]{:S(2)}) collective-permute-start(bf16[256,1024]{1,0:T(8,128)(2,1)S(1)} %stack.26.refs_0_.refs_4_), channel_id=1, source_target_pairs={{0,1},{1,2},{2,3},{4,5},{5,6},{6,7},{8,9},{9,10},{10,11},{12,13},{... | collective-permute-start | bytes 1572872 | tf_op jit(solution)/shard_map/ppermute | solution.py:870
  82.4 23.7 %collective-permute-start.8 = (bf16[256,1024]{1,0:T(8,128)(2,1)S(1)}, bf16[256,1024]{1,0:T(8,128)(2,1)S(1)}, u32[]{:S(2)}, u32[]{:S(2)}) collective-permute-start(bf16[256,1024]{1,0:T(8,128)(2,1)S(1)} %stack.26.refs_0_.refs_4_), channel_id=1, source_target_pairs={{0,3},{3,0},{4,7},{7,4},{8,11},{11,8},{12,15},{15,12},{16,19},{19,... | collective-permute-start | bytes 1572872 | tf_op jit(solution)/shard_map/ppermute | solution.py:870
  92.7 24.4 %collective-permute-start.10 = (bf16[256,1024]{1,0:T(8,128)(2,1)S(1)}, bf16[256,1024]{1,0:T(8,128)(2,1)S(1)}, u32[]{:S(2)}, u32[]{:S(2)}) collective-permute-start(bf16[256,1024]{1,0:T(8,128)(2,1)S(1)} %collective-permute-done.7.refs_2_.refs_6_), channel_id=1, source_target_pairs={{1,0},{2,1},{5,4},{6,5},{9,8},{10,9},{13,12},{14,13},{17,16},{18,1... | collective-permute-start | bytes 1572872 | tf_op jit(solution)/shard_map/ppermute | solution.py:870
  94.6 31.0 %copy-start.8 = (bf16[256,1024]{1,0:T(8,128)(2,1)}, bf16[256,1024]{1,0:T(8,128)(2,1)S(1)}, u32[]{:S(2)}) copy-start(bf16[256,1024]{1,0:T(8,128)(2,1)S(1)} %collective-permute-done.6.refs_1_.refs_5_) | copy-start | bytes 1572868
  94.6 22.5 %collective-permute-start.9 = (bf16[256,1024]{1,0:T(8,128)(2,1)S(1)}, bf16[256,1024]{1,0:T(8,128)(2,1)S(1)}, u32[]{:S(2)}, u32[]{:S(2)}) collective-permute-start(bf16[256,1024]{1,0:T(8,128)(2,1)S(1)} %collective-permute-done.6.refs_1_.refs_5_), channel_id=1, source_target_pairs={{1,2},{2,3},{5,6},{6,7},{9,10},{10,11},{13,14},{14,15},{17,18},{18... | collective-permute-start | bytes 1572872 | tf_op jit(solution)/shard_map/ppermute | solution.py:870
  106.1 19.6 %copy-start.10 = (bf16[256,1024]{1,0:T(8,128)(2,1)}, bf16[256,1024]{1,0:T(8,128)(2,1)S(1)}, u32[]{:S(2)}) copy-start(bf16[256,1024]{1,0:T(8,128)(2,1)S(1)} %collective-permute-done.8.refs_3_.refs_7_) | copy-start | bytes 1572868
  133.8 31.3 %all-to-all-start.1 = ((bf16[8,128,1024]{2,1,0:T(8,128)(2,1)}), bf16[8,128,1024]{2,1,0:T(8,128)(2,1)}, u32[]{:S(2)}, u32[]{:S(2)}) async-start(bf16[8,128,1024]{2,1,0:T(8,128)(2,1)} %bitcast.71), calls=%async_computation.1 | async-start | bytes 4194304 | tf_op jit(solution)/shard_map/all_to_all | solution.py:912
  165.2 30.6 %all-to-all-start.3 = ((bf16[8,128,1024]{2,1,0:T(8,128)(2,1)}), bf16[8,128,1024]{2,1,0:T(8,128)(2,1)S(1)}, u32[]{:S(2)}, u32[]{:S(2)}) async-start(bf16[8,128,1024]{2,1,0:T(8,128)(2,1)} %bitcast.70), calls=%async_computation.3 | async-start | bytes 4194304 | tf_op jit(solution)/shard_map/all_to_all | solution.py:912
  197.1 30.4 %all-to-all-start.2 = ((bf16[8,128,1024]{2,1,0:T(8,128)(2,1)}), bf16[8,128,1024]{2,1,0:T(8,128)(2,1)S(1)}, u32[]{:S(2)}, u32[]{:S(2)}) async-start(bf16[8,128,1024]{2,1,0:T(8,128)(2,1)} %bitcast.81), calls=%async_computation.2 | async-start | bytes 4194304 | tf_op jit(solution)/shard_map/all_to_all | solution.py:912
  228.8 31.0 %all-to-all-start.4 = ((bf16[8,128,1024]{2,1,0:T(8,128)(2,1)}), bf16[8,128,1024]{2,1,0:T(8,128)(2,1)}, u32[]{:S(2)}, u32[]{:S(2)}) async-start(bf16[8,128,1024]{2,1,0:T(8,128)(2,1)} %bitcast.80), calls=%async_computation.4 | async-start | bytes 4194304 | tf_op jit(solution)/shard_map/all_to_all | solution.py:912
  259.8 53.8 %all-to-all-start.5 = ((bf16[8,256,1024]{2,1,0:T(8,128)(2,1)}), bf16[8,256,1024]{2,1,0:T(8,128)(2,1)}, u32[]{:S(2)}, u32[]{:S(2)}) async-start(bf16[8,256,1024]{2,1,0:T(8,128)(2,1)} %get-tuple-element.196), calls=%async_computation.5 | async-start | bytes 8388608 | tf_op jit(solution)/shard_map/all_to_all | solution.py:912
  264.5 200.5 %all-reduce.2.cloned.1.call-start = ((), (), s32[]{:S(2)}) async-start(), calls=%async_computation.9 | async-start | bytes 4194304 | tf_op jit(solution)/shard_map/psum | solution.py:1024
  274.1 39.5 %copy-start.7 = (f32[256,1024]{1,0:T(8,128)S(1)}, f32[256,1024]{1,0:T(8,128)}, u32[]{:S(2)}) copy-start(f32[256,1024]{1,0:T(8,128)} %copy-done.6) | copy-start | bytes 3145732
  274.1 39.5 %copy-start.19 = (s32[1024,1]{1,0:T(8,128)S(1)}, s32[1024,1]{1,0:T(8,128)}, u32[]{:S(2)}) copy-start(s32[1024,1]{1,0:T(8,128)} %get-tuple-element.314.refs_0_) | copy-start | bytes 12292
  274.1 18.6 %collective-permute-start.13 = (bf16[256,1024]{1,0:T(8,128)(2,1)S(1)}, bf16[256,1024]{1,0:T(8,128)(2,1)S(1)}, u32[]{:S(2)}, u32[]{:S(2)}) collective-permute-start(bf16[256,1024]{1,0:T(8,128)(2,1)S(1)} %get-tuple-element.189), channel_id=1, source_target_pairs={{0,3},{3,0},{4,7},{7,4},{8,11},{11,8},{12,15},{15,12},{16,19},{19,... | collective-permute-start | bytes 1572872 | tf_op jit(solution)/shard_map/ppermute | solution.py:870
  279.9 22.9 %collective-permute-start.12 = (bf16[256,1024]{1,0:T(8,128)(2,1)S(1)}, bf16[256,1024]{1,0:T(8,128)(2,1)S(1)}, u32[]{:S(2)}, u32[]{:S(2)}) collective-permute-start(bf16[256,1024]{1,0:T(8,128)(2,1)S(1)} %get-tuple-element.188), channel_id=1, source_target_pairs={{0,1},{1,2},{4,5},{5,6},{8,9},{9,10},{12,13},{13,14},{16,17},{17,1... | collective-permute-start | bytes 1572872 | tf_op jit(solution)/shard_map/ppermute | solution.py:870
  281.2 21.6 %collective-permute-start.11 = (bf16[256,1024]{1,0:T(8,128)(2,1)S(1)}, bf16[256,1024]{1,0:T(8,128)(2,1)S(1)}, u32[]{:S(2)}, u32[]{:S(2)}) collective-permute-start(bf16[256,1024]{1,0:T(8,128)(2,1)S(1)} %get-tuple-element.188), channel_id=1, source_target_pairs={{2,1},{3,2},{6,5},{7,6},{10,9},{11,10},{14,13},{15,14},{18,17},{19... | collective-permute-start | bytes 1572872 | tf_op jit(solution)/shard_map/ppermute | solution.py:870
  292.6 30.3 %copy-start.37 = (bf16[256,1024]{1,0:T(8,128)(2,1)}, bf16[256,1024]{1,0:T(8,128)(2,1)S(1)}, u32[]{:S(2)}) copy-start(bf16[256,1024]{1,0:T(8,128)(2,1)S(1)} %collective-permute-done.13.refs_3_) | copy-start | bytes 1572868
  302.8 45.9 %collective-permute-start.22 = (bf16[4,128,2048]{2,1,0:T(8,128)(2,1)}, bf16[4,128,2048]{2,1,0:T(8,128)(2,1)}, u32[]{:S(2)}, u32[]{:S(2)}) collective-permute-start(bf16[4,128,2048]{2,1,0:T(8,128)(2,1)} %get-tuple-element.212), channel_id=1, source_target_pairs={{0,4},{4,0},{8,12},{12,8},{16,20},{20,16},{24,28},{28,24},{1,5},{5... | collective-permute-start | bytes 6291464 | tf_op jit(solution)/shard_map/ppermute | solution.py:907
  303.8 19.1 %collective-permute-start.15 = (bf16[256,1024]{1,0:T(8,128)(2,1)}, bf16[256,1024]{1,0:T(8,128)(2,1)}, u32[]{:S(2)}, u32[]{:S(2)}) collective-permute-start(bf16[256,1024]{1,0:T(8,128)(2,1)} %add_convert_fusion.6), channel_id=1, source_target_pairs={{0,1},{1,2},{2,3},{4,5},{5,6},{6,7},{8,9},{9,10},{10,11},{12,13},{... | collective-permute-start | bytes 1572872 | tf_op jit(solution)/shard_map/ppermute | solution.py:870
  310.0 16.3 %collective-permute-start.14 = (bf16[256,1024]{1,0:T(8,128)(2,1)}, bf16[256,1024]{1,0:T(8,128)(2,1)}, u32[]{:S(2)}, u32[]{:S(2)}) collective-permute-start(bf16[256,1024]{1,0:T(8,128)(2,1)} %add_convert_fusion.7), channel_id=1, source_target_pairs={{1,0},{2,1},{3,2},{5,4},{6,5},{7,6},{9,8},{10,9},{11,10},{13,12},{... | collective-permute-start | bytes 1572872 | tf_op jit(solution)/shard_map/ppermute | solution.py:870
  328.5 20.2 %copy-start.18 = (bf16[4,128,2048]{2,1,0:T(8,128)(2,1)S(1)}, bf16[4,128,2048]{2,1,0:T(8,128)(2,1)}, u32[]{:S(2)}) copy-start(bf16[4,128,2048]{2,1,0:T(8,128)(2,1)} %copy-done.17) | copy-start | bytes 6291460
  333.7 18.5 %copy-start.33 = (bf16[256,1024]{1,0:T(8,128)(2,1)}, bf16[256,1024]{1,0:T(8,128)(2,1)S(1)}, u32[]{:S(2)}) copy-start(bf16[256,1024]{1,0:T(8,128)(2,1)S(1)} %get-tuple-element.239.refs_11_) | copy-start | bytes 1572868
  333.7 18.5 %copy-start.59 = (f32[2,1024]{1,0:T(2,128)}, f32[2,1024]{1,0:T(2,128)S(1)}, u32[]{:S(2)}) copy-start(f32[2,1024]{1,0:T(2,128)S(1)} %get-tuple-element.240.refs_15_) | copy-start | bytes 24580
  333.7 5.5 collective-permute-start.16
  334.2 12.0 %collective-permute-start.17 = (bf16[256,256]{1,0:T(8,128)(2,1)S(1)}, bf16[256,256]{1,0:T(8,128)(2,1)S(1)}, u32[]{:S(2)}, u32[]{:S(2)}) collective-permute-start(bf16[256,256]{1,0:T(8,128)(2,1)S(1)} %get-tuple-element.205), channel_id=1, source_target_pairs={{0,2},{1,3},{2,0},{3,1},{4,6},{5,7},{6,4},{7,5},{8,10},{9,11},{10,... | collective-permute-start | bytes 393224 | tf_op jit(solution)/shard_map/ppermute | solution.py:870
  334.7 11.4 %collective-permute-start.18 = (bf16[256,256]{1,0:T(8,128)(2,1)S(1)}, bf16[256,256]{1,0:T(8,128)(2,1)S(1)}, u32[]{:S(2)}, u32[]{:S(2)}) collective-permute-start(bf16[256,256]{1,0:T(8,128)(2,1)S(1)} %get-tuple-element.206), channel_id=1, source_target_pairs={{0,1},{1,2},{2,3},{3,0},{4,5},{5,6},{6,7},{7,4},{8,9},{9,10},{10,1... | collective-permute-start | bytes 393224 | tf_op jit(solution)/shard_map/ppermute | solution.py:870
  346.8 5.5 collective-permute-start.19
  346.9 6.4 %collective-permute-start.20 = (bf16[64,1024]{1,0:T(8,128)(2,1)S(1)}, bf16[64,1024]{1,0:T(8,128)(2,1)S(1)}, u32[]{:S(2)}, u32[]{:S(2)}) collective-permute-start(bf16[64,1024]{1,0:T(8,128)(2,1)S(1)} %get-tuple-element.209), channel_id=1, source_target_pairs={{0,8},{4,12},{8,0},{12,4},{16,24},{20,28},{24,16},{28,20},{1,9},{5... | collective-permute-start | bytes 393224 | tf_op jit(solution)/shard_map/ppermute | solution.py:907
  348.6 6.5 %collective-permute-start.21 = (bf16[64,1024]{1,0:T(8,128)(2,1)S(1)}, bf16[64,1024]{1,0:T(8,128)(2,1)S(1)}, u32[]{:S(2)}, u32[]{:S(2)}) collective-permute-start(bf16[64,1024]{1,0:T(8,128)(2,1)S(1)} %get-tuple-element.210), channel_id=1, source_target_pairs={{0,12},{4,8},{8,4},{12,0},{16,28},{20,24},{24,20},{28,16},{1,13},{... | collective-permute-start | bytes 393224 | tf_op jit(solution)/shard_map/ppermute | solution.py:907
  355.8 28.5 %collective-permute-start.23 = (bf16[2,128,2048]{2,1,0:T(8,128)(2,1)}, bf16[2,128,2048]{2,1,0:T(8,128)(2,1)}, u32[]{:S(2)}, u32[]{:S(2)}) collective-permute-start(bf16[2,128,2048]{2,1,0:T(8,128)(2,1)} %get-tuple-element.222), channel_id=1, source_target_pairs={{0,8},{4,12},{8,0},{12,4},{16,24},{20,28},{24,16},{28,20},{1,9},{5... | collective-permute-start | bytes 3145736 | tf_op jit(solution)/shard_map/ppermute | solution.py:907
  357.5 165.9 %reduce-scatter.2.cloned.1.call-start = ((), (), s32[]{:S(2)}) async-start(), calls=%async_computation.10 | async-start | bytes 4423680 | tf_op jit(solution)/shard_map/reduce_scatter | solution.py:1060
  384.3 12.1 %collective-permute-start.24 = (bf16[192,1024]{1,0:T(8,128)(2,1)S(1)}, bf16[192,1024]{1,0:T(8,128)(2,1)S(1)}, u32[]{:S(2)}, u32[]{:S(2)}) collective-permute-start(bf16[192,1024]{1,0:T(8,128)(2,1)S(1)} %get-tuple-element.229), channel_id=1, source_target_pairs={{0,4},{4,0},{8,12},{12,8},{16,20},{20,16},{24,28},{28,24},{1,5},{5... | collective-permute-start | bytes 1179656 | tf_op jit(solution)/shard_map/ppermute | solution.py:907
  384.4 12.0 %collective-permute-start.25 = (bf16[192,1024]{1,0:T(8,128)(2,1)S(1)}, bf16[192,1024]{1,0:T(8,128)(2,1)S(1)}, u32[]{:S(2)}, u32[]{:S(2)}) collective-permute-start(bf16[192,1024]{1,0:T(8,128)(2,1)S(1)} %get-tuple-element.230), channel_id=1, source_target_pairs={{0,8},{4,12},{8,0},{12,4},{16,24},{20,28},{24,16},{28,20},{1,9},{5... | collective-permute-start | bytes 1179656 | tf_op jit(solution)/shard_map/ppermute | solution.py:907
  384.8 19.1 %collective-permute-start.26 = (bf16[192,1024]{1,0:T(8,128)(2,1)S(1)}, bf16[192,1024]{1,0:T(8,128)(2,1)S(1)}, u32[]{:S(2)}, u32[]{:S(2)}) collective-permute-start(bf16[192,1024]{1,0:T(8,128)(2,1)S(1)} %get-tuple-element.231), channel_id=1, source_target_pairs={{0,12},{4,8},{8,4},{12,0},{16,28},{20,24},{24,20},{28,16},{1,13},{... | collective-permute-start | bytes 1179656 | tf_op jit(solution)/shard_map/ppermute | solution.py:907
  386.3 34.8 %copy-start.63 = (bf16[2048,1024]{1,0:T(8,128)(2,1)S(1)}, bf16[2048,1024]{1,0:T(8,128)(2,1)}, u32[]{:S(2)}) copy-start(bf16[2048,1024]{1,0:T(8,128)(2,1)} %get-tuple-element.245) | copy-start | bytes 12582916
  411.1 54.0 %collective-permute-start.28 = (bf16[256,1024]{1,0:T(8,128)(2,1)}, bf16[256,1024]{1,0:T(8,128)(2,1)S(1)}, u32[]{:S(2)}, u32[]{:S(2)}) collective-permute-start(bf16[256,1024]{1,0:T(8,128)(2,1)} %get-tuple-element.247), channel_id=1, source_target_pairs={{0,1},{1,2},{4,5},{5,6},{8,9},{9,10},{12,13},{13,14},{16,17},{17,1... | collective-permute-start | bytes 1572872 | tf_op jit(solution)/shard_map/ppermute | solution.py:870
  413.1 52.0 %collective-permute-start.27 = (bf16[256,1024]{1,0:T(8,128)(2,1)}, bf16[256,1024]{1,0:T(8,128)(2,1)}, u32[]{:S(2)}, u32[]{:S(2)}) collective-permute-start(bf16[256,1024]{1,0:T(8,128)(2,1)} %get-tuple-element.247), channel_id=1, source_target_pairs={{2,1},{3,2},{6,5},{7,6},{10,9},{11,10},{14,13},{15,14},{18,17},{19... | collective-permute-start | bytes 1572872 | tf_op jit(solution)/shard_map/ppermute | solution.py:870
  414.7 50.4 %collective-permute-start.29 = (bf16[256,1024]{1,0:T(8,128)(2,1)}, bf16[256,1024]{1,0:T(8,128)(2,1)S(1)}, u32[]{:S(2)}, u32[]{:S(2)}) collective-permute-start(bf16[256,1024]{1,0:T(8,128)(2,1)} %get-tuple-element.248), channel_id=1, source_target_pairs={{0,3},{3,0},{4,7},{7,4},{8,11},{11,8},{12,15},{15,12},{16,19},{19,... | collective-permute-start | bytes 1572872 | tf_op jit(solution)/shard_map/ppermute | solution.py:870
  438.1 27.0 %copy-start.42 = (bf16[256,1024]{1,0:T(8,128)(2,1)S(1)}, bf16[256,1024]{1,0:T(8,128)(2,1)}, u32[]{:S(2)}) copy-start(bf16[256,1024]{1,0:T(8,128)(2,1)} %copy-done.41) | copy-start | bytes 1572868
  438.1 29.7 %copy-start.40 = (bf16[256,1024]{1,0:T(8,128)(2,1)S(1)}, bf16[256,1024]{1,0:T(8,128)(2,1)}, u32[]{:S(2)}) copy-start(bf16[256,1024]{1,0:T(8,128)(2,1)} %copy-done.39) | copy-start | bytes 1572868
  466.5 14.2 %collective-permute-start.30 = (bf16[256,1024]{1,0:T(8,128)(2,1)S(1)}, bf16[256,1024]{1,0:T(8,128)(2,1)S(1)}, u32[]{:S(2)}, u32[]{:S(2)}) collective-permute-start(bf16[256,1024]{1,0:T(8,128)(2,1)S(1)} %add_convert_fusion.5), channel_id=1, source_target_pairs={{1,0},{2,1},{3,2},{5,4},{6,5},{7,6},{9,8},{10,9},{11,10},{13,12},{... | collective-permute-start | bytes 1572872 | tf_op jit(solution)/shard_map/ppermute | solution.py:870
  468.0 14.1 %collective-permute-start.31 = (bf16[256,1024]{1,0:T(8,128)(2,1)S(1)}, bf16[256,1024]{1,0:T(8,128)(2,1)S(1)}, u32[]{:S(2)}, u32[]{:S(2)}) collective-permute-start(bf16[256,1024]{1,0:T(8,128)(2,1)S(1)} %add_convert_fusion.4), channel_id=1, source_target_pairs={{0,1},{1,2},{2,3},{4,5},{5,6},{6,7},{8,9},{9,10},{10,11},{12,13},{... | collective-permute-start | bytes 1572872 | tf_op jit(solution)/shard_map/ppermute | solution.py:870
  485.7 14.9 %collective-permute-start.33 = (bf16[256,1024]{1,0:T(8,128)(2,1)S(1)}, bf16[256,1024]{1,0:T(8,128)(2,1)S(1)}, u32[]{:S(2)}, u32[]{:S(2)}) collective-permute-start(bf16[256,1024]{1,0:T(8,128)(2,1)S(1)} %first_back.1.refs_0_), channel_id=1, source_target_pairs={{1,0},{2,1},{3,2},{5,4},{6,5},{7,6},{9,8},{10,9},{11,10},{13,12},{... | collective-permute-start | bytes 1572872 | tf_op jit(solution)/shard_map/ppermute | solution.py:870
  487.0 15.9 %collective-permute-start.32 = (bf16[256,1024]{1,0:T(8,128)(2,1)S(1)}, bf16[256,1024]{1,0:T(8,128)(2,1)S(1)}, u32[]{:S(2)}, u32[]{:S(2)}) collective-permute-start(bf16[256,1024]{1,0:T(8,128)(2,1)S(1)} %first_back.1.refs_0_), channel_id=1, source_target_pairs={{0,1},{1,2},{2,3},{4,5},{5,6},{6,7},{8,9},{9,10},{10,11},{12,13},{... | collective-permute-start | bytes 1572872 | tf_op jit(solution)/shard_map/ppermute | solution.py:870
  494.5 36.0 %collective-permute-start.37 = (bf16[1,128,2048]{2,1,0:T(8,128)(2,1)}, bf16[1,128,2048]{2,1,0:T(8,128)(2,1)}, u32[]{:S(2)}, u32[]{:S(2)}) collective-permute-start(bf16[1,128,2048]{2,1,0:T(8,128)(2,1)} %slice.118), channel_id=1, source_target_pairs={{0,16},{4,20},{8,24},{12,28},{16,0},{20,4},{24,8},{28,12},{1,17},{... | collective-permute-start | bytes 1572872 | tf_op jit(solution)/shard_map/ppermute | solution.py:907
  498.1 36.9 %collective-permute-start.34 = (bf16[256,1024]{1,0:T(8,128)(2,1)S(1)}, bf16[256,1024]{1,0:T(8,128)(2,1)S(1)}, u32[]{:S(2)}, u32[]{:S(2)}) collective-permute-start(bf16[256,1024]{1,0:T(8,128)(2,1)S(1)} %first_back.1.refs_0_), channel_id=1, source_target_pairs={{0,3},{3,0},{4,7},{7,4},{8,11},{11,8},{12,15},{15,12},{16,19},{19,... | collective-permute-start | bytes 1572872 | tf_op jit(solution)/shard_map/ppermute | solution.py:870
  500.6 34.5 %collective-permute-start.36 = (bf16[256,1024]{1,0:T(8,128)(2,1)S(1)}, bf16[256,1024]{1,0:T(8,128)(2,1)S(1)}, u32[]{:S(2)}, u32[]{:S(2)}) collective-permute-start(bf16[256,1024]{1,0:T(8,128)(2,1)S(1)} %collective-permute-done.33.refs_2_), channel_id=1, source_target_pairs={{1,0},{2,1},{5,4},{6,5},{9,8},{10,9},{13,12},{14,13},{17,16},{18,1... | collective-permute-start | bytes 1572872 | tf_op jit(solution)/shard_map/ppermute | solution.py:870
  502.8 32.2 %collective-permute-start.35 = (bf16[256,1024]{1,0:T(8,128)(2,1)S(1)}, bf16[256,1024]{1,0:T(8,128)(2,1)S(1)}, u32[]{:S(2)}, u32[]{:S(2)}) collective-permute-start(bf16[256,1024]{1,0:T(8,128)(2,1)S(1)} %collective-permute-done.32.refs_1_), channel_id=1, source_target_pairs={{1,2},{2,3},{5,6},{6,7},{9,10},{10,11},{13,14},{14,15},{17,18},{18... | collective-permute-start | bytes 1572872 | tf_op jit(solution)/shard_map/ppermute | solution.py:870
  526.0 16.4 %all-to-all-start.6 = ((bf16[4,384,128]{1,2,0:T(8,128)(2,1)}), bf16[4,384,128]{1,2,0:T(8,128)(2,1)}, u32[]{:S(2)}, u32[]{:S(2)}) async-start(bf16[4,384,128]{1,2,0:T(8,128)(2,1)} %pad_maximum_fusion), calls=%async_computation.7 | async-start | bytes 786432 | tf_op jit(solution)/shard_map/all_to_all | solution.py:1072
  (57 other events, 360.6 us)
Sparse Core Ops, SparseCore 0:
  9.6 48.6 all-gather.1
  357.6 107.3 all-reduce.1
  469.0 54.3 reduce-scatter.1
where the time goes:
time: 565 us; the launch traced here: 555 us
  Pallas kernels  186 us (33%)
  waiting for transfers between devices  171 us (30%)
  starting transfers between devices  104 us (18%)
  local copies, waits for them, and re-layouts  35.4 us (6%)
  other arithmetic  25.6 us (5%)
  matrix products  18.5 us (3%)
  between operations  15.3 us (3%)
    pallas_call x20, Pallas kernels, call(): pl.pallas_call(kernel, grid_spec=pltpu.PrefetchScalarGridSpec(num_scalar_...  186 us
    ppermute x23, waiting for transfers between devices, hop(): return lax.ppermute(value, 'mp', pairs)  74.5 us
    ppermute x23, starting transfers between devices, hop(): return lax.ppermute(value, 'mp', pairs)  54.4 us
    all_to_all x6, waiting for transfers between devices, expert_swap(): return lax.all_to_all(wide, 'dp', 0, 0, tiled=True).reshape(value.shape)  30.8 us
    all_to_all x6, starting transfers between devices, expert_swap(): return lax.all_to_all(wide, 'dp', 0, 0, tiled=True).reshape(value.shape)  30.3 us
    unnamed x156, local copies, waits for them, and re-layouts  30.2 us
    psum x1, waiting for transfers between devices, body(): output = lax.psum(mix, 'mp')  27 us
    reduce_scatter x1, waiting for transfers between devices, body(): grads_a = lax.psum_scatter(grads_a, 'dp', scatter_dimension=0, tiled=True).T  19.9 us
  transfers between devices with their start and end apart: 48, of which 25 were waited for; matrix products, arithmetic and copies ran while one was open for 9% of the time, Pallas kernels for 34%

commit v1 on v0

--- a/solution.py
+++ b/solution.py
@@ -1015,7 +1015,9 @@
     tok_y = expert_swap(back_y.reshape(experts * capacity, width), experts)
     shares = combine(at, dest_cols, [back_0, back_1], db_base)
     far = scatter_far(shares)
-    *far, g_0, g_1 = barrier((*far, *grads))
+    grad_down = ein("rf,rd->fd", hidden_e, d_y)
+    grad_up = ein("rd,rf->df", got, d_eu)
+    *far, g_0, g_1, grad_down, grad_up = barrier((*far, *grads, grad_down, grad_up))
     grads = [g_0, g_1]
     shares = scatter_near(shares, far)
 
@@ -1046,17 +1048,14 @@
     else:
         grads = [lax.psum_scatter(grad, "dp", scatter_dimension=0, tiled=True) for grad in grads]
 
-    d_own, got, hidden_e, d_y, d_eu = barrier((d_qkv[0], got, hidden_e, d_y, d_eu))
-    d_qkv = [d_own] + [group_swap(d_qkv[s], s) for s in (1, 2, 3)]
-    grad_down = ein("rf,rd->fd", hidden_e, d_y)
-    *d_qkv, grad_down = barrier((*d_qkv, grad_down))
+    d_qkv = [d_qkv[0]] + [group_swap(d_qkv[s], s) for s in (1, 2, 3)]
+    *d_qkv, output = barrier((*d_qkv, output))
     shares = project_back(at, d_qkv, w_heads)
     far = scatter_far(shares)
     grads_a = attention_grads(
         at, d_qkv, o_pieces, a_r, dh_r, w_heads, gains[0], biases[0], sums_2, (small_0, small_1, small_t), experts
     )
-    grad_up = ein("rd,rf->df", got, d_eu)
-    grads_a, output, grad_up, *far = barrier((grads_a, output, grad_up, *far))
+    grads_a, *far = barrier((grads_a, *far))
     grads_a = lax.psum_scatter(grads_a, "dp", scatter_dimension=0, tiled=True).T
     shares = scatter_near(shares, far)
     grad_q = first_back(at, shares, tokens, dh, gains[0])

time: 565 us -> 573 us (1.014)
  Pallas kernels: 186 us -> 200 us
  starting transfers between devices: 104 us -> 94.6 us
    ppermute x23, waiting for transfers between devices: 74.5 us -> 106 us  [hop(): return lax.ppermute(value, 'mp', pairs)]
    reduce_scatter x1, waiting for transfers between devices: 19.9 us -> 1.26 us  [body(): grads_a = lax.psum_scatter(grads_a, 'dp', scatter_dimension=0, tiled=True).T]
    psum x1, waiting for transfers between devices: 27 us -> 9.08 us  [body(): output = lax.psum(mix, 'mp')]
    pallas_call x20, Pallas kernels: 186 us -> 200 us  [call(): pl.pallas_call(kernel, grid_spec=pltpu.PrefetchScalarGridSpec(num_scalar_...]
    ppermute x15, waiting for transfers between devices: 15.7 us -> 24.3 us  [group_swap(): return lax.ppermute(value, 'dp', [(t, t ^ s) for t in range(count)])]
    unnamed x156 -> x178, local copies, waits for them, and re-layouts: 30.2 us -> 35.7 us
  transfers between devices with their start and end apart: 48 -> 48, of which waited for: 25 -> 26; matrix products, arithmetic and copies ran while one was open for 9% -> 9% of each run, Pallas kernels for 34% -> 34%
where the time goes in v1:
time: 573 us; the launch traced here: 564 us
  Pallas kernels  200 us (35%)
  waiting for transfers between devices  173 us (30%)
  starting transfers between devices  94.6 us (17%)
  local copies, waits for them, and re-layouts  40.9 us (7%)
  other arithmetic  24.1 us (4%)
  matrix products  16.2 us (3%)
  between operations  15.1 us (3%)
    pallas_call x20, Pallas kernels, call(): pl.pallas_call(kernel, grid_spec=pltpu.PrefetchScalarGridSpec(num_scalar_...  200 us
    ppermute x23, waiting for transfers between devices, hop(): return lax.ppermute(value, 'mp', pairs)  106 us
    ppermute x23, starting transfers between devices, hop(): return lax.ppermute(value, 'mp', pairs)  51.1 us
    unnamed x178, local copies, waits for them, and re-layouts  35.7 us
    all_to_all x6, waiting for transfers between devices, expert_swap(): return lax.all_to_all(wide, 'dp', 0, 0, tiled=True).reshape(value.shape)  29.2 us
    all_to_all x6, starting transfers between devices, expert_swap(): return lax.all_to_all(wide, 'dp', 0, 0, tiled=True).reshape(value.shape)  25.7 us
    ppermute x15, waiting for transfers between devices, group_swap(): return lax.ppermute(value, 'dp', [(t, t ^ s) for t in range(count)])  24.3 us
    dot_general x2, matrix products, ein(): return jnp.einsum(spec, a, b, preferred_element_type=F32)  16.2 us
  transfers between devices with their start and end apart: 48, of which 26 were waited for; matrix products, arithmetic and copies ran while one was open for 9% of the time, Pallas kernels for 34%

profile of v1, /device:TPU:0, one launch (start us, length us, event | category | flops | bytes accessed | tf_op | source)
XLA Modules:
  0.0 563.9 jit_solution(11144936286861073942)
XLA Ops:
  12.2 6.9 %project.1 = (bf16[1024,1024]{1,0:T(8,128)(2,1)S(1)}, bf16[192,1024]{1,0:T(8,128)(2,1)S(1)}, bf16[192,1024]{1,0:T(8,128)(2,1)}, bf16[192,1024]{1,0:T(8,128)(2,1)}, bf16[192,1024]{1,0:T(8,128)(2,1)}) custom-call(s32[4]{0:T(128)S(1)} %pad_add_fusion.at_ref, bf16[1024,1024]{1,0:T(8,128)(2,1)} %refs_4_.1, ...), custom_call_target="tpu_custom_call" | custom-call | flops 1048576 | bytes 1048576 | tf_op jit(solution)/shard_map/project/pallas_call | solution.py:30
  20.9 2.5 collective-permute-start.1
  24.6 2.3 reduce-window.6
  27.6 2.3 multiply_add_fusion.1
  30.4 3.4 fusion.rows_ref.dy_ref.refs_6_
  34.5 7.6 %dispatch.3 = bf16[2048,1024]{1,0:T(8,128)(2,1)} custom-call(s32[4]{0:T(128)S(1)} %pad_add_fusion.at_ref, s32[1,1024]{1,0:T(1,128)S(1)} %get-tuple-element.321.dest_ref, bf16[1024,1024]{1,0:T(8,128)(2,1)S(1)} %fusion.rows_ref.dy_ref.refs_6_), custom_call_target="tpu_custom_call" | custom-call | flops 1048576 | bytes 1048576 | tf_op jit(solution)/shard_map/dispatch/pallas_call | solution.py:30
  42.2 21.0 %attend.1 = (bf16[64,1024]{1,0:T(8,128)(2,1)S(1)}, bf16[64,1024]{1,0:T(8,128)(2,1)S(1)}, bf16[64,1024]{1,0:T(8,128)(2,1)S(1)}, bf16[64,1024]{1,0:T(8,128)(2,1)S(1)}, f32[8,1,512]{2,1,0:T(1,128)S(1)}) custom-call(s32[4]{0:T(128)S(1)} %pad_add_fusion.at_ref, bf16[192,1024]{1,0:T(8,128)(2,1)S(1)} %get-tuple-element.136.refs_0_, ...), custom_call_target="tpu_custom_call" | custom-call | flops 1048576 | bytes 1048576 | tf_op jit(solution)/shard_map/attend/pallas_call | solution.py:30
  66.7 3.6 collective-permute-done.4.refs_2_
  72.1 4.6 all-to-all-start
  78.6 4.6 collective-permute-start.6
  83.2 3.2 collective-permute-start.8
  86.4 7.0 %collective-permute-done.7.refs_2_.refs_6_ = bf16[256,1024]{1,0:T(8,128)(2,1)S(1)} collective-permute-done((bf16[256,1024]{1,0:T(8,128)(2,1)S(1)}, bf16[256,1024]{1,0:T(8,128)(2,1)S(1)}, u32[]{:S(2)}, u32[]{:S(2)}) %collective-permute-start.7) | collective-permute-done | bytes 524320 | tf_op jit(solution)/shard_map/ppermute | solution.py:870
  96.3 10.5 %collective-permute-done.8.refs_3_.refs_7_ = bf16[256,1024]{1,0:T(8,128)(2,1)S(1)} collective-permute-done((bf16[256,1024]{1,0:T(8,128)(2,1)S(1)}, bf16[256,1024]{1,0:T(8,128)(2,1)S(1)}, u32[]{:S(2)}, u32[]{:S(2)}) %collective-permute-start.8) | collective-permute-done | bytes 524320 | tf_op jit(solution)/shard_map/ppermute | solution.py:870
  106.8 11.1 %collective-permute-done.10.refs_5_.refs_9_ = bf16[256,1024]{1,0:T(8,128)(2,1)S(1)} collective-permute-done((bf16[256,1024]{1,0:T(8,128)(2,1)S(1)}, bf16[256,1024]{1,0:T(8,128)(2,1)S(1)}, u32[]{:S(2)}, u32[]{:S(2)}) %collective-permute-start.10) | collective-permute-done | bytes 524320 | tf_op jit(solution)/shard_map/ppermute | solution.py:870
  117.9 8.5 %mid.1 = (f32[256,1024]{1,0:T(8,128)S(1)}, bf16[1024,1024]{1,0:T(8,128)(2,1)}) custom-call(s32[4]{0:T(128)S(1)} %pad_add_fusion.at_ref, bf16[256,1024]{1,0:T(8,128)(2,1)S(1)} %stack.26.refs_0_.refs_4_, bf16[256,1024]{1,0:T(8,128)(2,1)S(1)} %collective-permute-done.6.refs_1_.refs_5_, bf16[256,1024]{1,0:T(8,128)(2,1)S(1)} %collective-permute-done.7.refs_2_.refs_6_, ...), custom_call_target="tpu_custom_call" | custom-call | flops 1048576 | bytes 1048576 | tf_op jit(solution)/shard_map/mid/pallas_call | solution.py:30
  129.0 4.3 dispatch.5
  134.6 4.5 all-to-all-start.1
  139.1 4.3 dispatch.4
  144.7 19.4 %dense_rows.1 = (bf16[1024,1024]{1,0:T(8,128)(2,1)}, bf16[1024,1024]{1,0:T(8,128)(2,1)}, bf16[1024,1024]{1,0:T(8,128)(2,1)}, f32[1024,1024]{1,0:T(8,128)}, f32[1024,1024]{1,0:T(8,128)}, /*index=5*/f32[128,1024]{1,0:T(8,128)}) custom-call(s32[4]{0:T(128)} %copy-done.55, bf16[1024,1024]{1,0:T(8,128)(2,1)} %get-tuple-element.172.rows_ref.b_ref, ...), custom_call_target="tpu_custom_call" | custom-call | flops 1048576 | bytes 1048576 | tf_op jit(solution)/shard_map/dense_rows/pallas_call | solution.py:30
  165.7 3.8 all-to-all-start.3
  169.5 19.6 %expert_rows.2 = (bf16[2048,1024]{1,0:T(8,128)(2,1)}, bf16[2048,1024]{1,0:T(8,128)(2,1)}, bf16[2048,1024]{1,0:T(8,128)(2,1)}, bf16[2048,1024]{1,0:T(8,128)(2,1)}...) custom-call(s32[4]{0:T(128)} %copy-done.55, ...), custom_call_target="tpu_custom_call" | custom-call | flops 1048576 | bytes 1048576 | tf_op jit(solution)/shard_map/expert_rows/pallas_call | solution.py:30
  189.2 6.9 %all-to-all-done.3 = bf16[8,128,1024]{2,1,0:T(8,128)(2,1)S(1)} async-done(((bf16[8,128,1024]{2,1,0:T(8,128)(2,1)}), bf16[8,128,1024]{2,1,0:T(8,128)(2,1)S(1)}, u32[]{:S(2)}, u32[]{:S(2)}) %all-to-all-start.3) | async-done | bytes 2097184 | tf_op jit(solution)/shard_map/all_to_all | solution.py:912
  197.4 3.9 all-to-all-start.2
  201.3 19.8 %expert_rows.3 = (bf16[2048,1024]{1,0:T(8,128)(2,1)}, bf16[2048,1024]{1,0:T(8,128)(2,1)}, bf16[2048,1024]{1,0:T(8,128)(2,1)}, bf16[2048,1024]{1,0:T(8,128)(2,1)}...) custom-call(s32[4]{0:T(128)} %copy-done.55, ...), custom_call_target="tpu_custom_call", output_to_operand_aliasing={{0}: (6, {}), {1}: (7, {}), {2}: (8, {}), {3}: (9, {}), {4}... | custom-call | flops 1048576 | bytes 1048576 | tf_op jit(solution)/shard_map/expert_rows/pallas_call | solution.py:30
  221.1 6.8 %all-to-all-done.2 = bf16[8,128,1024]{2,1,0:T(8,128)(2,1)S(1)} async-done(((bf16[8,128,1024]{2,1,0:T(8,128)(2,1)}), bf16[8,128,1024]{2,1,0:T(8,128)(2,1)S(1)}, u32[]{:S(2)}, u32[]{:S(2)}) %all-to-all-start.2) | async-done | bytes 2097184 | tf_op jit(solution)/shard_map/all_to_all | solution.py:912
  229.2 4.4 all-to-all-start.4
  233.6 11.5 %dense_grads.1 = (bf16[4,128,2048]{2,1,0:T(8,128)(2,1)S(1)}, bf16[4,128,2048]{2,1,0:T(8,128)(2,1)}) custom-call(s32[4]{0:T(128)S(1)} %copy-done.56, bf16[1024,1024]{1,0:T(8,128)(2,1)} %get-tuple-element.172.rows_ref.b_ref, bf16[1024,1024]{1,0:T(8,128)(2,1)} %get-tuple-element.173.d_up_ref, bf16[1024,1024]{1,0:T(8,128)(2,1)} %get-tuple-element.174.grad_ref, ...), custom_call_target="tpu_custom_call" | custom-call | flops 1048576 | bytes 1048576 | tf_op jit(solution)/shard_map/dense_grads/pallas_call | solution.py:30
  246.3 13.9 %all-to-all-done.4 = bf16[8,128,1024]{2,1,0:T(8,128)(2,1)} async-done(((bf16[8,128,1024]{2,1,0:T(8,128)(2,1)}), bf16[8,128,1024]{2,1,0:T(8,128)(2,1)}, u32[]{:S(2)}, u32[]{:S(2)}) %all-to-all-start.4) | async-done | bytes 2097184 | tf_op jit(solution)/shard_map/all_to_all | solution.py:912
  260.2 4.6 all-to-all-start.5
  265.3 10.1 %fusion.10 = f32[1024,1024]{1,0:T(8,128)} fusion(bf16[2048,1024]{1,0:T(8,128)(2,1)} %get-tuple-element.187, bf16[2048,1024]{1,0:T(8,128)(2,1)} %get-tuple-element.188), kind=kOutput, calls=%fused_computation.46 | convolution fusion | flops 4294967296 | bytes 12582912 | tf_op jit(solution)/shard_map/rf,rd->fd/dot_general | solution.py:26
  275.5 8.8 %combine.2 = (f32[256,1024]{1,0:T(8,128)S(1)}, bf16[256,1024]{1,0:T(8,128)(2,1)S(1)}, bf16[256,1024]{1,0:T(8,128)(2,1)S(1)}, bf16[256,1024]{1,0:T(8,128)(2,1)S(1)}, bf16[256,1024]{1,0:T(8,128)(2,1)S(1)}) custom-call(s32[4]{0:T(128)S(1)} %copy-done.56, s32[1024,1]{1,0:T(8,128)S(1)} %copy-done.21, s32[1024,1]{1,0:T(8,128)S(1)} %copy-done.20, ...), custom_call_target="tpu_custom_call" | custom-call | flops 1048576 | bytes 1048576 | tf_op jit(solution)/shard_map/combine/pallas_call | solution.py:30
  284.3 2.7 collective-permute-start.12
  287.7 5.9 %collective-permute-start.13 = (bf16[256,1024]{1,0:T(8,128)(2,1)S(1)}, bf16[256,1024]{1,0:T(8,128)(2,1)S(1)}, u32[]{:S(2)}, u32[]{:S(2)}) collective-permute-start(bf16[256,1024]{1,0:T(8,128)(2,1)S(1)} %get-tuple-element.184), channel_id=1, source_target_pairs={{0,3},{3,0},{4,7},{7,4},{8,11},{11,8},{12,15},{15,12},{16,19},{19,... | collective-permute-start | bytes 1572872 | tf_op jit(solution)/shard_map/ppermute | solution.py:870
  293.6 6.1 %fusion.11 = f32[1024,1024]{1,0:T(8,128)} fusion(bf16[2048,1024]{1,0:T(8,128)(2,1)S(1)} %copy-done.71, bf16[2048,1024]{1,0:T(8,128)(2,1)S(1)} %copy-done.72), kind=kOutput, calls=%fused_computation.47 | convolution fusion | flops 4294967296 | bytes 12582912 | tf_op jit(solution)/shard_map/rd,rf->df/dot_general | solution.py:26
  299.7 15.4 %collective-permute-done.13.refs_3_ = bf16[256,1024]{1,0:T(8,128)(2,1)S(1)} collective-permute-done((bf16[256,1024]{1,0:T(8,128)(2,1)S(1)}, bf16[256,1024]{1,0:T(8,128)(2,1)S(1)}, u32[]{:S(2)}, u32[]{:S(2)}) %collective-permute-start.13) | collective-permute-done | bytes 524320 | tf_op jit(solution)/shard_map/ppermute | solution.py:870
  316.2 4.0 collective-permute-start.15
  322.6 9.3 %combine.3 = bf16[1024,1024]{1,0:T(8,128)(2,1)} custom-call(s32[4]{0:T(128)S(1)} %copy-done.56, s32[1024,1]{1,0:T(8,128)S(1)} %copy-done.19, bf16[2048,1024]{1,0:T(8,128)(2,1)} %bitcast.20.refs_1_, f32[1024,1024]{1,0:T(8,128)} %get-tuple-element.196.refs_2_, f32[256,1024]{1,0:T(8,128)S(1)} %copy-done.7), custom_call_target="tpu_custom_call" | custom-call | flops 1048576 | bytes 1048576 | tf_op jit(solution)/shard_map/combine/pallas_call | solution.py:30
  331.9 5.4 collective-permute-done.14.refs_1_
  339.6 4.9 mid_back.1
  349.0 3.6 collective-permute-done.16.refs_1_
  352.5 13.8 %collective-permute-done.17.refs_2_ = bf16[256,256]{1,0:T(8,128)(2,1)S(1)} collective-permute-done((bf16[256,256]{1,0:T(8,128)(2,1)}, bf16[256,256]{1,0:T(8,128)(2,1)S(1)}, u32[]{:S(2)}, u32[]{:S(2)}) %collective-permute-start.17) | collective-permute-done | bytes 131104 | tf_op jit(solution)/shard_map/ppermute | solution.py:870
  367.9 2.0 collective-permute-start.20
  370.1 3.3 add_convert_fusion.1
  374.4 2.1 collective-permute-done.21.refs_7_
  378.2 32.1 %attend_back.1 = (bf16[192,1024]{1,0:T(8,128)(2,1)S(1)}, bf16[192,1024]{1,0:T(8,128)(2,1)S(1)}, bf16[192,1024]{1,0:T(8,128)(2,1)S(1)}, bf16[192,1024]{1,0:T(8,128)(2,1)S(1)}) custom-call(s32[4]{0:T(128)S(1)} %copy-done.56, bf16[192,1024]{1,0:T(8,128)(2,1)S(1)} %copy-done.31, bf16[192,1024]{1,0:T(8,128)(2,1)S(1)} %copy-done.33, ...), custom_call_target="tpu_custom_call" | custom-call | flops 1048576 | bytes 1048576 | tf_op jit(solution)/shard_map/attend_back/pallas_call | solution.py:30
  413.0 9.7 %collective-permute-done.25.refs_2_ = bf16[192,1024]{1,0:T(8,128)(2,1)S(1)} collective-permute-done((bf16[192,1024]{1,0:T(8,128)(2,1)S(1)}, bf16[192,1024]{1,0:T(8,128)(2,1)S(1)}, u32[]{:S(2)}, u32[]{:S(2)}) %collective-permute-start.25) | collective-permute-done | bytes 393248 | tf_op jit(solution)/shard_map/ppermute | solution.py:907
  423.5 6.0 %collective-permute-done.26.refs_3_ = bf16[192,1024]{1,0:T(8,128)(2,1)S(1)} collective-permute-done((bf16[192,1024]{1,0:T(8,128)(2,1)S(1)}, bf16[192,1024]{1,0:T(8,128)(2,1)S(1)}, u32[]{:S(2)}, u32[]{:S(2)}) %collective-permute-start.26) | collective-permute-done | bytes 393248 | tf_op jit(solution)/shard_map/ppermute | solution.py:907
  430.3 9.1 %all-reduce.2.cloned.1.call-done = bf16[1024,1024]{1,0:T(8,128)(2,1)} async-done(((bf16[1024,1024]{1,0:T(8,128)(2,1)}), bf16[1024,1024]{1,0:T(8,128)(2,1)}) %all-reduce.2.cloned.1.call-update) | async-done | bytes 2097168 | tf_op jit(solution)/shard_map/psum | solution.py:1026
  442.4 6.3 %project_back.1 = (f32[256,1024]{1,0:T(8,128)S(1)}, bf16[256,1024]{1,0:T(8,128)(2,1)S(1)}, bf16[256,1024]{1,0:T(8,128)(2,1)}, bf16[256,1024]{1,0:T(8,128)(2,1)S(1)}, bf16[256,1024]{1,0:T(8,128)(2,1)}) custom-call(s32[4]{0:T(128)S(1)} %copy-done.56, bf16[192,1024]{1,0:T(8,128)(2,1)S(1)} %get-tuple-element.228.refs_0_, bf16[192,1024]{1,0:T(8,128)(2,1)S(1)} %copy-done.23, ...), custom_call_target="tpu_custom_call" | custom-call | flops 1048576 | bytes 1048576 | tf_op jit(solution)/shard_map/project_back/pallas_call | solution.py:30
  451.2 3.2 collective-permute-start.29
  454.5 2.1 collective-permute-start.28
  460.4 8.4 %attention_grads.1 = bf16[1024,1920]{1,0:T(8,128)(2,1)} custom-call(s32[4]{0:T(128)S(1)} %copy-done.56, bf16[192,1024]{1,0:T(8,128)(2,1)S(1)} %get-tuple-element.228.refs_0_, bf16[192,1024]{1,0:T(8,128)(2,1)S(1)} %copy-done.24, bf16[192,1024]{1,0:T(8,128)(2,1)S(1)} %copy-done.27, bf16[192,1024]{1,0:T(8,128)(2,1)S(1)} %copy-done.29, ...), custom_call_target="tpu_custom_call" | custom-call | flops 1048576 | bytes 1048576 | tf_op jit(solution)/shard_map/attention_grads/pallas_call | solution.py:30
  470.1 7.4 %collective-permute-done.28 = bf16[256,1024]{1,0:T(8,128)(2,1)} collective-permute-done((bf16[256,1024]{1,0:T(8,128)(2,1)}, bf16[256,1024]{1,0:T(8,128)(2,1)}, u32[]{:S(2)}, u32[]{:S(2)}) %collective-permute-start.28) | collective-permute-done | bytes 524320 | tf_op jit(solution)/shard_map/ppermute | solution.py:870
  478.8 5.2 collective-permute-start.31
  486.5 8.8 %collective-permute-done.31.refs_2_ = bf16[256,1024]{1,0:T(8,128)(2,1)S(1)} collective-permute-done((bf16[256,1024]{1,0:T(8,128)(2,1)S(1)}, bf16[256,1024]{1,0:T(8,128)(2,1)S(1)}, u32[]{:S(2)}, u32[]{:S(2)}) %collective-permute-start.31) | collective-permute-done | bytes 524320 | tf_op jit(solution)/shard_map/ppermute | solution.py:870
  495.3 5.4 collective-permute-done.30.refs_1_
  500.7 2.8 first_back.1.refs_0_
  504.8 4.6 collective-permute-start.32
  512.4 1.9 collective-permute-start.34
  514.3 15.5 %collective-permute-done.33.refs_2_ = bf16[256,1024]{1,0:T(8,128)(2,1)S(1)} collective-permute-done((bf16[256,1024]{1,0:T(8,128)(2,1)S(1)}, bf16[256,1024]{1,0:T(8,128)(2,1)S(1)}, u32[]{:S(2)}, u32[]{:S(2)}) %collective-permute-start.33) | collective-permute-done | bytes 524320 | tf_op jit(solution)/shard_map/ppermute | solution.py:870
  535.7 4.6 all-to-all-start.6
  542.7 2.0 copy.91
  544.8 2.9 join.1
  549.8 2.2 all-to-all-done.6
  (281 shorter events, 84.7 us)
Async XLA Ops:
  7.2 56.6 %all-gather.2.cloned.1.call-start = ((), (), s32[]{:S(2)}) async-start(), calls=%async_computation.8 | async-start | bytes 2621440 | tf_op jit(solution)/shard_map/all_gather | solution.py:955
  11.6 127.4 %copy-start.55 = (s32[4]{0:T(128)}, s32[4]{0:T(128)S(1)}, u32[]{:S(2)}) copy-start(s32[4]{0:T(128)S(1)} %pad_add_fusion.at_ref) | copy-start | bytes 52
  20.4 21.7 %copy-start.30 = (bf16[192,1024]{1,0:T(8,128)(2,1)}, bf16[192,1024]{1,0:T(8,128)(2,1)S(1)}, u32[]{:S(2)}) copy-start(bf16[192,1024]{1,0:T(8,128)(2,1)S(1)} %get-tuple-element.136.refs_0_) | copy-start | bytes 1179652
  20.4 21.7 %collective-permute-start = (bf16[192,1024]{1,0:T(8,128)(2,1)}, bf16[192,1024]{1,0:T(8,128)(2,1)S(1)}, u32[]{:S(2)}, u32[]{:S(2)}) collective-permute-start(bf16[192,1024]{1,0:T(8,128)(2,1)} %get-tuple-element.133), channel_id=1, source_target_pairs={{0,4},{4,0},{8,12},{12,8},{16,20},{20,16},{24,28},{28,24},{1,5},{5... | collective-permute-start | bytes 1179656 | tf_op jit(solution)/shard_map/ppermute | solution.py:907
  20.9 21.2 %collective-permute-start.1 = (bf16[192,1024]{1,0:T(8,128)(2,1)}, bf16[192,1024]{1,0:T(8,128)(2,1)S(1)}, u32[]{:S(2)}, u32[]{:S(2)}) collective-permute-start(bf16[192,1024]{1,0:T(8,128)(2,1)} %get-tuple-element.134), channel_id=1, source_target_pairs={{0,8},{4,12},{8,0},{12,4},{16,24},{20,28},{24,16},{28,20},{1,9},{5... | collective-permute-start | bytes 1179656 | tf_op jit(solution)/shard_map/ppermute | solution.py:907
  23.4 18.8 %collective-permute-start.2 = (bf16[192,1024]{1,0:T(8,128)(2,1)}, bf16[192,1024]{1,0:T(8,128)(2,1)S(1)}, u32[]{:S(2)}, u32[]{:S(2)}) collective-permute-start(bf16[192,1024]{1,0:T(8,128)(2,1)} %get-tuple-element.135), channel_id=1, source_target_pairs={{0,12},{4,8},{8,4},{12,0},{16,28},{20,24},{24,20},{28,16},{1,13},{... | collective-permute-start | bytes 1179656 | tf_op jit(solution)/shard_map/ppermute | solution.py:907
  42.1 30.0 %copy-start.32 = (bf16[192,1024]{1,0:T(8,128)(2,1)}, bf16[192,1024]{1,0:T(8,128)(2,1)S(1)}, u32[]{:S(2)}) copy-start(bf16[192,1024]{1,0:T(8,128)(2,1)S(1)} %collective-permute-done.refs_1_) | copy-start | bytes 1179652
  42.1 30.0 %copy-start.34 = (bf16[192,1024]{1,0:T(8,128)(2,1)}, bf16[192,1024]{1,0:T(8,128)(2,1)S(1)}, u32[]{:S(2)}) copy-start(bf16[192,1024]{1,0:T(8,128)(2,1)S(1)} %collective-permute-done.1.refs_2_) | copy-start | bytes 1179652
  42.1 30.0 %copy-start.36 = (bf16[192,1024]{1,0:T(8,128)(2,1)}, bf16[192,1024]{1,0:T(8,128)(2,1)S(1)}, u32[]{:S(2)}) copy-start(bf16[192,1024]{1,0:T(8,128)(2,1)S(1)} %collective-permute-done.2.refs_3_) | copy-start | bytes 1179652
  63.8 2.9 collective-permute-start.3
  63.9 6.3 %collective-permute-start.4 = (bf16[64,1024]{1,0:T(8,128)(2,1)S(1)}, bf16[64,1024]{1,0:T(8,128)(2,1)S(1)}, u32[]{:S(2)}, u32[]{:S(2)}) collective-permute-start(bf16[64,1024]{1,0:T(8,128)(2,1)S(1)} %get-tuple-element.146.refs_10_), channel_id=1, source_target_pairs={{0,8},{4,12},{8,0},{12,4},{16,24},{20,28},{24,16},{28,20},{1,9},{5... | collective-permute-start | bytes 393224 | tf_op jit(solution)/shard_map/ppermute | solution.py:907
  65.8 6.3 %collective-permute-start.5 = (bf16[64,1024]{1,0:T(8,128)(2,1)S(1)}, bf16[64,1024]{1,0:T(8,128)(2,1)S(1)}, u32[]{:S(2)}, u32[]{:S(2)}) collective-permute-start(bf16[64,1024]{1,0:T(8,128)(2,1)S(1)} %get-tuple-element.147.refs_11_), channel_id=1, source_target_pairs={{0,12},{4,8},{8,4},{12,0},{16,28},{20,24},{24,20},{28,16},{1,13},{... | collective-permute-start | bytes 393224 | tf_op jit(solution)/shard_map/ppermute | solution.py:907
  72.1 45.8 %copy-start.66 = (f32[1,1024]{1,0:T(1,128)S(1)}, f32[1,1024]{1,0:T(1,128)}, u32[]{:S(2)}) copy-start(f32[1,1024]{1,0:T(1,128)} %get-tuple-element.317.refs_9_) | copy-start | bytes 12292
  72.1 62.4 %all-to-all-start = ((bf16[8,256,1024]{2,1,0:T(8,128)(2,1)}), bf16[8,256,1024]{2,1,0:T(8,128)(2,1)}, u32[]{:S(2)}, u32[]{:S(2)}) async-start(bf16[8,256,1024]{2,1,0:T(8,128)(2,1)} %bitcast.72), calls=%async_computation | async-start | bytes 8388608 | tf_op jit(solution)/shard_map/all_to_all | solution.py:912
  77.3 16.1 %collective-permute-start.7 = (bf16[256,1024]{1,0:T(8,128)(2,1)S(1)}, bf16[256,1024]{1,0:T(8,128)(2,1)S(1)}, u32[]{:S(2)}, u32[]{:S(2)}) collective-permute-start(bf16[256,1024]{1,0:T(8,128)(2,1)S(1)} %stack.26.refs_0_.refs_4_), channel_id=1, source_target_pairs={{1,0},{2,1},{3,2},{5,4},{6,5},{7,6},{9,8},{10,9},{11,10},{13,12},{... | collective-permute-start | bytes 1572872 | tf_op jit(solution)/shard_map/ppermute | solution.py:870
  78.6 16.8 %collective-permute-start.6 = (bf16[256,1024]{1,0:T(8,128)(2,1)S(1)}, bf16[256,1024]{1,0:T(8,128)(2,1)S(1)}, u32[]{:S(2)}, u32[]{:S(2)}) collective-permute-start(bf16[256,1024]{1,0:T(8,128)(2,1)S(1)} %stack.26.refs_0_.refs_4_), channel_id=1, source_target_pairs={{0,1},{1,2},{2,3},{4,5},{5,6},{6,7},{8,9},{9,10},{10,11},{12,13},{... | collective-permute-start | bytes 1572872 | tf_op jit(solution)/shard_map/ppermute | solution.py:870
  83.2 23.6 %collective-permute-start.8 = (bf16[256,1024]{1,0:T(8,128)(2,1)S(1)}, bf16[256,1024]{1,0:T(8,128)(2,1)S(1)}, u32[]{:S(2)}, u32[]{:S(2)}) collective-permute-start(bf16[256,1024]{1,0:T(8,128)(2,1)S(1)} %stack.26.refs_0_.refs_4_), channel_id=1, source_target_pairs={{0,3},{3,0},{4,7},{7,4},{8,11},{11,8},{12,15},{15,12},{16,19},{19,... | collective-permute-start | bytes 1572872 | tf_op jit(solution)/shard_map/ppermute | solution.py:870
  93.4 24.5 %collective-permute-start.10 = (bf16[256,1024]{1,0:T(8,128)(2,1)S(1)}, bf16[256,1024]{1,0:T(8,128)(2,1)S(1)}, u32[]{:S(2)}, u32[]{:S(2)}) collective-permute-start(bf16[256,1024]{1,0:T(8,128)(2,1)S(1)} %collective-permute-done.7.refs_2_.refs_6_), channel_id=1, source_target_pairs={{1,0},{2,1},{5,4},{6,5},{9,8},{10,9},{13,12},{14,13},{17,16},{18,1... | collective-permute-start | bytes 1572872 | tf_op jit(solution)/shard_map/ppermute | solution.py:870
  95.5 30.9 %copy-start.8 = (bf16[256,1024]{1,0:T(8,128)(2,1)}, bf16[256,1024]{1,0:T(8,128)(2,1)S(1)}, u32[]{:S(2)}) copy-start(bf16[256,1024]{1,0:T(8,128)(2,1)S(1)} %collective-permute-done.6.refs_1_.refs_5_) | copy-start | bytes 1572868
  95.5 22.4 %collective-permute-start.9 = (bf16[256,1024]{1,0:T(8,128)(2,1)S(1)}, bf16[256,1024]{1,0:T(8,128)(2,1)S(1)}, u32[]{:S(2)}, u32[]{:S(2)}) collective-permute-start(bf16[256,1024]{1,0:T(8,128)(2,1)S(1)} %collective-permute-done.6.refs_1_.refs_5_), channel_id=1, source_target_pairs={{1,2},{2,3},{5,6},{6,7},{9,10},{10,11},{13,14},{14,15},{17,18},{18... | collective-permute-start | bytes 1572872 | tf_op jit(solution)/shard_map/ppermute | solution.py:870
  134.6 31.2 %all-to-all-start.1 = ((bf16[8,128,1024]{2,1,0:T(8,128)(2,1)}), bf16[8,128,1024]{2,1,0:T(8,128)(2,1)}, u32[]{:S(2)}, u32[]{:S(2)}) async-start(bf16[8,128,1024]{2,1,0:T(8,128)(2,1)} %bitcast.71), calls=%async_computation.1 | async-start | bytes 4194304 | tf_op jit(solution)/shard_map/all_to_all | solution.py:912
  165.7 30.4 %all-to-all-start.3 = ((bf16[8,128,1024]{2,1,0:T(8,128)(2,1)}), bf16[8,128,1024]{2,1,0:T(8,128)(2,1)S(1)}, u32[]{:S(2)}, u32[]{:S(2)}) async-start(bf16[8,128,1024]{2,1,0:T(8,128)(2,1)} %bitcast.70), calls=%async_computation.3 | async-start | bytes 4194304 | tf_op jit(solution)/shard_map/all_to_all | solution.py:912
  197.4 30.4 %all-to-all-start.2 = ((bf16[8,128,1024]{2,1,0:T(8,128)(2,1)}), bf16[8,128,1024]{2,1,0:T(8,128)(2,1)S(1)}, u32[]{:S(2)}, u32[]{:S(2)}) async-start(bf16[8,128,1024]{2,1,0:T(8,128)(2,1)} %bitcast.81), calls=%async_computation.2 | async-start | bytes 4194304 | tf_op jit(solution)/shard_map/all_to_all | solution.py:912
  229.2 31.0 %all-to-all-start.4 = ((bf16[8,128,1024]{2,1,0:T(8,128)(2,1)}), bf16[8,128,1024]{2,1,0:T(8,128)(2,1)}, u32[]{:S(2)}, u32[]{:S(2)}) async-start(bf16[8,128,1024]{2,1,0:T(8,128)(2,1)} %bitcast.80), calls=%async_computation.4 | async-start | bytes 4194304 | tf_op jit(solution)/shard_map/all_to_all | solution.py:912
  260.2 62.4 %all-to-all-start.5 = ((bf16[8,256,1024]{2,1,0:T(8,128)(2,1)}), bf16[8,256,1024]{2,1,0:T(8,128)(2,1)}, u32[]{:S(2)}, u32[]{:S(2)}) async-start(bf16[8,256,1024]{2,1,0:T(8,128)(2,1)} %get-tuple-element.195), calls=%async_computation.5 | async-start | bytes 8388608 | tf_op jit(solution)/shard_map/all_to_all | solution.py:912
  264.8 174.6 %all-reduce.2.cloned.1.call-start = ((), (), s32[]{:S(2)}) async-start(), calls=%async_computation.9 | async-start | bytes 4194304 | tf_op jit(solution)/shard_map/psum | solution.py:1026
  284.3 30.8 %collective-permute-start.12 = (bf16[256,1024]{1,0:T(8,128)(2,1)S(1)}, bf16[256,1024]{1,0:T(8,128)(2,1)S(1)}, u32[]{:S(2)}, u32[]{:S(2)}) collective-permute-start(bf16[256,1024]{1,0:T(8,128)(2,1)S(1)} %get-tuple-element.183), channel_id=1, source_target_pairs={{0,1},{1,2},{4,5},{5,6},{8,9},{9,10},{12,13},{13,14},{16,17},{17,1... | collective-permute-start | bytes 1572872 | tf_op jit(solution)/shard_map/ppermute | solution.py:870
  287.0 28.1 %collective-permute-start.11 = (bf16[256,1024]{1,0:T(8,128)(2,1)S(1)}, bf16[256,1024]{1,0:T(8,128)(2,1)S(1)}, u32[]{:S(2)}, u32[]{:S(2)}) collective-permute-start(bf16[256,1024]{1,0:T(8,128)(2,1)S(1)} %get-tuple-element.183), channel_id=1, source_target_pairs={{2,1},{3,2},{6,5},{7,6},{10,9},{11,10},{14,13},{15,14},{18,17},{19... | collective-permute-start | bytes 1572872 | tf_op jit(solution)/shard_map/ppermute | solution.py:870
  287.7 27.4 %collective-permute-start.13 = (bf16[256,1024]{1,0:T(8,128)(2,1)S(1)}, bf16[256,1024]{1,0:T(8,128)(2,1)S(1)}, u32[]{:S(2)}, u32[]{:S(2)}) collective-permute-start(bf16[256,1024]{1,0:T(8,128)(2,1)S(1)} %get-tuple-element.184), channel_id=1, source_target_pairs={{0,3},{3,0},{4,7},{7,4},{8,11},{11,8},{12,15},{15,12},{16,19},{19,... | collective-permute-start | bytes 1572872 | tf_op jit(solution)/shard_map/ppermute | solution.py:870
  299.7 22.9 %copy-start.7 = (f32[256,1024]{1,0:T(8,128)S(1)}, f32[256,1024]{1,0:T(8,128)}, u32[]{:S(2)}) copy-start(f32[256,1024]{1,0:T(8,128)} %copy-done.6) | copy-start | bytes 3145732
  299.7 22.9 %copy-start.19 = (s32[1024,1]{1,0:T(8,128)S(1)}, s32[1024,1]{1,0:T(8,128)}, u32[]{:S(2)}) copy-start(s32[1024,1]{1,0:T(8,128)} %get-tuple-element.304.refs_0_) | copy-start | bytes 12292
  315.1 55.1 %collective-permute-start.22 = (bf16[4,128,2048]{2,1,0:T(8,128)(2,1)}, bf16[4,128,2048]{2,1,0:T(8,128)(2,1)}, u32[]{:S(2)}, u32[]{:S(2)}) collective-permute-start(bf16[4,128,2048]{2,1,0:T(8,128)(2,1)} %get-tuple-element.211), channel_id=1, source_target_pairs={{0,4},{4,0},{8,12},{12,8},{16,20},{20,16},{24,28},{28,24},{1,5},{5... | collective-permute-start | bytes 6291464 | tf_op jit(solution)/shard_map/ppermute | solution.py:907
  316.2 15.8 %collective-permute-start.15 = (bf16[256,1024]{1,0:T(8,128)(2,1)}, bf16[256,1024]{1,0:T(8,128)(2,1)}, u32[]{:S(2)}, u32[]{:S(2)}) collective-permute-start(bf16[256,1024]{1,0:T(8,128)(2,1)} %add_convert_fusion.6), channel_id=1, source_target_pairs={{0,1},{1,2},{2,3},{4,5},{5,6},{6,7},{8,9},{9,10},{10,11},{12,13},{... | collective-permute-start | bytes 1572872 | tf_op jit(solution)/shard_map/ppermute | solution.py:870
  321.1 16.3 %collective-permute-start.14 = (bf16[256,1024]{1,0:T(8,128)(2,1)}, bf16[256,1024]{1,0:T(8,128)(2,1)}, u32[]{:S(2)}, u32[]{:S(2)}) collective-permute-start(bf16[256,1024]{1,0:T(8,128)(2,1)} %add_convert_fusion.7), channel_id=1, source_target_pairs={{1,0},{2,1},{3,2},{5,4},{6,5},{7,6},{9,8},{10,9},{11,10},{13,12},{... | collective-permute-start | bytes 1572872 | tf_op jit(solution)/shard_map/ppermute | solution.py:870
  346.9 23.2 %copy-start.18 = (bf16[4,128,2048]{2,1,0:T(8,128)(2,1)S(1)}, bf16[4,128,2048]{2,1,0:T(8,128)(2,1)}, u32[]{:S(2)}) copy-start(bf16[4,128,2048]{2,1,0:T(8,128)(2,1)} %copy-done.17) | copy-start | bytes 6291460
  346.9 5.7 %collective-permute-start.16 = (bf16[256,256]{1,0:T(8,128)(2,1)}, bf16[256,256]{1,0:T(8,128)(2,1)S(1)}, u32[]{:S(2)}, u32[]{:S(2)}) collective-permute-start(bf16[256,256]{1,0:T(8,128)(2,1)} %get-tuple-element.203), channel_id=1, source_target_pairs={{0,3},{1,0},{2,1},{3,2},{4,7},{5,4},{6,5},{7,6},{8,11},{9,8},{10,9... | collective-permute-start | bytes 393224 | tf_op jit(solution)/shard_map/ppermute | solution.py:870
  346.9 19.5 %collective-permute-start.17 = (bf16[256,256]{1,0:T(8,128)(2,1)}, bf16[256,256]{1,0:T(8,128)(2,1)S(1)}, u32[]{:S(2)}, u32[]{:S(2)}) collective-permute-start(bf16[256,256]{1,0:T(8,128)(2,1)} %get-tuple-element.204), channel_id=1, source_target_pairs={{0,2},{1,3},{2,0},{3,1},{4,6},{5,7},{6,4},{7,5},{8,10},{9,11},{10,... | collective-permute-start | bytes 393224 | tf_op jit(solution)/shard_map/ppermute | solution.py:870
  347.9 18.5 %collective-permute-start.18 = (bf16[256,256]{1,0:T(8,128)(2,1)}, bf16[256,256]{1,0:T(8,128)(2,1)}, u32[]{:S(2)}, u32[]{:S(2)}) collective-permute-start(bf16[256,256]{1,0:T(8,128)(2,1)} %get-tuple-element.205), channel_id=1, source_target_pairs={{0,1},{1,2},{2,3},{3,0},{4,5},{5,6},{6,7},{7,4},{8,9},{9,10},{10,1... | collective-permute-start | bytes 393224 | tf_op jit(solution)/shard_map/ppermute | solution.py:870
  348.9 184.2 %reduce-scatter.2.cloned.1.call-start = ((), (), s32[]{:S(2)}) async-start(), calls=%async_computation.10 | async-start | bytes 4423680 | tf_op jit(solution)/shard_map/reduce_scatter | solution.py:1059
  367.9 5.5 collective-permute-start.19
  367.9 6.4 %collective-permute-start.20 = (bf16[64,1024]{1,0:T(8,128)(2,1)S(1)}, bf16[64,1024]{1,0:T(8,128)(2,1)S(1)}, u32[]{:S(2)}, u32[]{:S(2)}) collective-permute-start(bf16[64,1024]{1,0:T(8,128)(2,1)S(1)} %get-tuple-element.208), channel_id=1, source_target_pairs={{0,8},{4,12},{8,0},{12,4},{16,24},{20,28},{24,16},{28,20},{1,9},{5... | collective-permute-start | bytes 393224 | tf_op jit(solution)/shard_map/ppermute | solution.py:907
  370.0 6.5 %collective-permute-start.21 = (bf16[64,1024]{1,0:T(8,128)(2,1)S(1)}, bf16[64,1024]{1,0:T(8,128)(2,1)S(1)}, u32[]{:S(2)}, u32[]{:S(2)}) collective-permute-start(bf16[64,1024]{1,0:T(8,128)(2,1)S(1)} %get-tuple-element.209), channel_id=1, source_target_pairs={{0,12},{4,8},{8,4},{12,0},{16,28},{20,24},{24,20},{28,16},{1,13},{... | collective-permute-start | bytes 393224 | tf_op jit(solution)/shard_map/ppermute | solution.py:907
  376.5 33.9 %collective-permute-start.23 = (bf16[2,128,2048]{2,1,0:T(8,128)(2,1)S(1)}, bf16[2,128,2048]{2,1,0:T(8,128)(2,1)S(1)}, u32[]{:S(2)}, u32[]{:S(2)}) collective-permute-start(bf16[2,128,2048]{2,1,0:T(8,128)(2,1)S(1)} %get-tuple-element.221), channel_id=1, source_target_pairs={{0,8},{4,12},{8,0},{12,4},{16,24},{20,28},{24,16},{28,20},{1,9},{5... | collective-permute-start | bytes 3145736 | tf_op jit(solution)/shard_map/ppermute | solution.py:907
  410.3 47.9 %copy-start.9 = (bf16[256,1024]{1,0:T(8,128)(2,1)S(1)}, bf16[256,1024]{1,0:T(8,128)(2,1)}, u32[]{:S(2)}) copy-start(bf16[256,1024]{1,0:T(8,128)(2,1)} %copy-done.8) | copy-start | bytes 1572868
  410.3 47.9 %copy-start.11 = (bf16[256,1024]{1,0:T(8,128)(2,1)S(1)}, bf16[256,1024]{1,0:T(8,128)(2,1)}, u32[]{:S(2)}) copy-start(bf16[256,1024]{1,0:T(8,128)(2,1)} %copy-done.10) | copy-start | bytes 1572868
  410.3 47.9 %copy-start.13 = (bf16[256,1024]{1,0:T(8,128)(2,1)S(1)}, bf16[256,1024]{1,0:T(8,128)(2,1)}, u32[]{:S(2)}) copy-start(bf16[256,1024]{1,0:T(8,128)(2,1)} %copy-done.12) | copy-start | bytes 1572868
  410.3 47.9 %copy-start.15 = (bf16[256,1024]{1,0:T(8,128)(2,1)S(1)}, bf16[256,1024]{1,0:T(8,128)(2,1)}, u32[]{:S(2)}) copy-start(bf16[256,1024]{1,0:T(8,128)(2,1)} %copy-done.14) | copy-start | bytes 1572868
  410.4 1.9 collective-permute-start.24
  410.8 12.0 %collective-permute-start.25 = (bf16[192,1024]{1,0:T(8,128)(2,1)S(1)}, bf16[192,1024]{1,0:T(8,128)(2,1)S(1)}, u32[]{:S(2)}, u32[]{:S(2)}) collective-permute-start(bf16[192,1024]{1,0:T(8,128)(2,1)S(1)} %get-tuple-element.224), channel_id=1, source_target_pairs={{0,8},{4,12},{8,0},{12,4},{16,24},{20,28},{24,16},{28,20},{1,9},{5... | collective-permute-start | bytes 1179656 | tf_op jit(solution)/shard_map/ppermute | solution.py:907
  411.1 18.4 %collective-permute-start.26 = (bf16[192,1024]{1,0:T(8,128)(2,1)S(1)}, bf16[192,1024]{1,0:T(8,128)(2,1)S(1)}, u32[]{:S(2)}, u32[]{:S(2)}) collective-permute-start(bf16[192,1024]{1,0:T(8,128)(2,1)S(1)} %get-tuple-element.225), channel_id=1, source_target_pairs={{0,12},{4,8},{8,4},{12,0},{16,28},{20,24},{24,20},{28,16},{1,13},{... | collective-permute-start | bytes 1179656 | tf_op jit(solution)/shard_map/ppermute | solution.py:907
  451.2 18.9 %collective-permute-start.29 = (bf16[256,1024]{1,0:T(8,128)(2,1)}, bf16[256,1024]{1,0:T(8,128)(2,1)}, u32[]{:S(2)}, u32[]{:S(2)}) collective-permute-start(bf16[256,1024]{1,0:T(8,128)(2,1)} %get-tuple-element.241), channel_id=1, source_target_pairs={{0,3},{3,0},{4,7},{7,4},{8,11},{11,8},{12,15},{15,12},{16,19},{19,... | collective-permute-start | bytes 1572872 | tf_op jit(solution)/shard_map/ppermute | solution.py:870
  454.5 23.0 %collective-permute-start.28 = (bf16[256,1024]{1,0:T(8,128)(2,1)}, bf16[256,1024]{1,0:T(8,128)(2,1)}, u32[]{:S(2)}, u32[]{:S(2)}) collective-permute-start(bf16[256,1024]{1,0:T(8,128)(2,1)} %get-tuple-element.240), channel_id=1, source_target_pairs={{0,1},{1,2},{4,5},{5,6},{8,9},{9,10},{12,13},{13,14},{16,17},{17,1... | collective-permute-start | bytes 1572872 | tf_op jit(solution)/shard_map/ppermute | solution.py:870
  456.6 20.8 %collective-permute-start.27 = (bf16[256,1024]{1,0:T(8,128)(2,1)}, bf16[256,1024]{1,0:T(8,128)(2,1)}, u32[]{:S(2)}, u32[]{:S(2)}) collective-permute-start(bf16[256,1024]{1,0:T(8,128)(2,1)} %get-tuple-element.240), channel_id=1, source_target_pairs={{2,1},{3,2},{6,5},{7,6},{10,9},{11,10},{14,13},{15,14},{18,17},{19... | collective-permute-start | bytes 1572872 | tf_op jit(solution)/shard_map/ppermute | solution.py:870
  477.5 23.2 %copy-start.41 = (f32[256,1024]{1,0:T(8,128)S(1)}, f32[256,1024]{1,0:T(8,128)}, u32[]{:S(2)}) copy-start(f32[256,1024]{1,0:T(8,128)} %copy-done.40) | copy-start | bytes 3145732
  477.5 23.2 %copy-start.43 = (f32[256,1024]{1,0:T(8,128)S(1)}, f32[256,1024]{1,0:T(8,128)}, u32[]{:S(2)}) copy-start(f32[256,1024]{1,0:T(8,128)} %copy-done.42) | copy-start | bytes 3145732
  478.8 16.5 %collective-permute-start.31 = (bf16[256,1024]{1,0:T(8,128)(2,1)S(1)}, bf16[256,1024]{1,0:T(8,128)(2,1)S(1)}, u32[]{:S(2)}, u32[]{:S(2)}) collective-permute-start(bf16[256,1024]{1,0:T(8,128)(2,1)S(1)} %add_convert_fusion.4), channel_id=1, source_target_pairs={{0,1},{1,2},{2,3},{4,5},{5,6},{6,7},{8,9},{9,10},{10,11},{12,13},{... | collective-permute-start | bytes 1572872 | tf_op jit(solution)/shard_map/ppermute | solution.py:870
  485.2 15.5 %collective-permute-start.30 = (bf16[256,1024]{1,0:T(8,128)(2,1)S(1)}, bf16[256,1024]{1,0:T(8,128)(2,1)S(1)}, u32[]{:S(2)}, u32[]{:S(2)}) collective-permute-start(bf16[256,1024]{1,0:T(8,128)(2,1)S(1)} %add_convert_fusion.5), channel_id=1, source_target_pairs={{1,0},{2,1},{3,2},{5,4},{6,5},{7,6},{9,8},{10,9},{11,10},{13,12},{... | collective-permute-start | bytes 1572872 | tf_op jit(solution)/shard_map/ppermute | solution.py:870
  503.5 26.4 %collective-permute-start.33 = (bf16[256,1024]{1,0:T(8,128)(2,1)S(1)}, bf16[256,1024]{1,0:T(8,128)(2,1)S(1)}, u32[]{:S(2)}, u32[]{:S(2)}) collective-permute-start(bf16[256,1024]{1,0:T(8,128)(2,1)S(1)} %first_back.1.refs_0_), channel_id=1, source_target_pairs={{1,0},{2,1},{3,2},{5,4},{6,5},{7,6},{9,8},{10,9},{11,10},{13,12},{... | collective-permute-start | bytes 1572872 | tf_op jit(solution)/shard_map/ppermute | solution.py:870
  504.8 26.4 %collective-permute-start.32 = (bf16[256,1024]{1,0:T(8,128)(2,1)S(1)}, bf16[256,1024]{1,0:T(8,128)(2,1)S(1)}, u32[]{:S(2)}, u32[]{:S(2)}) collective-permute-start(bf16[256,1024]{1,0:T(8,128)(2,1)S(1)} %first_back.1.refs_0_), channel_id=1, source_target_pairs={{0,1},{1,2},{2,3},{4,5},{5,6},{6,7},{8,9},{9,10},{10,11},{12,13},{... | collective-permute-start | bytes 1572872 | tf_op jit(solution)/shard_map/ppermute | solution.py:870
  510.7 29.6 %collective-permute-start.37 = (bf16[1,128,2048]{2,1,0:T(8,128)(2,1)}, bf16[1,128,2048]{2,1,0:T(8,128)(2,1)}, u32[]{:S(2)}, u32[]{:S(2)}) collective-permute-start(bf16[1,128,2048]{2,1,0:T(8,128)(2,1)} %slice.118), channel_id=1, source_target_pairs={{0,16},{4,20},{8,24},{12,28},{16,0},{20,4},{24,8},{28,12},{1,17},{... | collective-permute-start | bytes 1572872 | tf_op jit(solution)/shard_map/ppermute | solution.py:907
  512.4 32.4 %collective-permute-start.34 = (bf16[256,1024]{1,0:T(8,128)(2,1)S(1)}, bf16[256,1024]{1,0:T(8,128)(2,1)S(1)}, u32[]{:S(2)}, u32[]{:S(2)}) collective-permute-start(bf16[256,1024]{1,0:T(8,128)(2,1)S(1)} %first_back.1.refs_0_), channel_id=1, source_target_pairs={{0,3},{3,0},{4,7},{7,4},{8,11},{11,8},{12,15},{15,12},{16,19},{19,... | collective-permute-start | bytes 1572872 | tf_op jit(solution)/shard_map/ppermute | solution.py:870
  529.9 14.9 %collective-permute-start.36 = (bf16[256,1024]{1,0:T(8,128)(2,1)S(1)}, bf16[256,1024]{1,0:T(8,128)(2,1)S(1)}, u32[]{:S(2)}, u32[]{:S(2)}) collective-permute-start(bf16[256,1024]{1,0:T(8,128)(2,1)S(1)} %collective-permute-done.33.refs_2_), channel_id=1, source_target_pairs={{1,0},{2,1},{5,4},{6,5},{9,8},{10,9},{13,12},{14,13},{17,16},{18,1... | collective-permute-start | bytes 1572872 | tf_op jit(solution)/shard_map/ppermute | solution.py:870
  531.2 13.6 %collective-permute-start.35 = (bf16[256,1024]{1,0:T(8,128)(2,1)S(1)}, bf16[256,1024]{1,0:T(8,128)(2,1)S(1)}, u32[]{:S(2)}, u32[]{:S(2)}) collective-permute-start(bf16[256,1024]{1,0:T(8,128)(2,1)S(1)} %collective-permute-done.32.refs_1_), channel_id=1, source_target_pairs={{1,2},{2,3},{5,6},{6,7},{9,10},{10,11},{13,14},{14,15},{17,18},{18... | collective-permute-start | bytes 1572872 | tf_op jit(solution)/shard_map/ppermute | solution.py:870
  535.7 16.3 %all-to-all-start.6 = ((bf16[4,384,128]{1,2,0:T(8,128)(2,1)}), bf16[4,384,128]{1,2,0:T(8,128)(2,1)S(1)}, u32[]{:S(2)}, u32[]{:S(2)}) async-start(bf16[4,384,128]{1,2,0:T(8,128)(2,1)} %pad_maximum_fusion), calls=%async_computation.7 | async-start | bytes 786432 | tf_op jit(solution)/shard_map/all_to_all | solution.py:1071
  (68 other events, 464.8 us)
Sparse Core Ops, SparseCore 0:
  9.6 48.6 all-gather.1
  349.0 90.2 all-reduce.1
  477.6 55.5 reduce-scatter.1

commit v2 on v0

--- a/solution.py
+++ b/solution.py
@@ -114,7 +114,7 @@
 
 def attend_kernel(blk, per, at_ref, *refs):
     qkv_refs, o_refs = refs[:GROUP], refs[GROUP : 2 * GROUP]
-    lse_ref, k_s, qkv_s = refs[2 * GROUP :]
+    lse_ref, k_s, v_s, qkv_s = refs[2 * GROUP :]
     i = pl.program_id(0)
     place, first_len = at_ref[0], at_ref[3]
 
@@ -128,37 +128,39 @@
 
     fill_keys(k_s, i, part(1, i), first_len, blk)
     query = wide_query(part(0, i), i, first_len, blk)
+    ones = jnp.where(lax.broadcasted_iota(jnp.int32, (16, blk), 0) == 0, 1.0, 0.0)
+    here = pl.ds(pl.multiple_of(i * blk, blk), blk)
+    v_s[:, here] = jnp.concatenate([part(2, i), ones.astype(BF)], axis=0)
+
+    def values(j):
+        return v_s[:, pl.ds(pl.multiple_of(j * blk, blk), blk)]
 
     def scores(j):
         return mm(k_s[pl.ds(pl.multiple_of(j * blk, blk), blk), :], query)
 
     s = jnp.where(causal(blk), scores(i), HIDE)
     top = jnp.max(s, axis=0, keepdims=True)
-    p = jnp.exp2((s - top) * SCALE2)
-    total = jnp.sum(p, axis=0, keepdims=True)
-    acc = mm(part(2, i), p.astype(BF))
+    acc = mm(values(i), jnp.exp2(((s - top) * SCALE2).astype(BF)))
 
     def steps(blocks, carry):
-        top, total, acc = carry
+        top, acc = carry
         s = [scores(j) for j in blocks]
         new = top
         for one in s:
             new = jnp.maximum(new, jnp.max(one, axis=0, keepdims=True))
-        keep = jnp.exp2((top - new) * SCALE2)
-        total, acc = total * keep, acc * keep
+        acc = acc * jnp.exp2((top - new) * SCALE2)
         for j, one in zip(blocks, s):
-            p = jnp.exp2((one - new) * SCALE2)
-            total = total + jnp.sum(p, axis=0, keepdims=True)
-            acc = acc + mm(part(2, j), p.astype(BF))
-        return new, total, acc
+            acc = acc + mm(values(j), jnp.exp2(((one - new) * SCALE2).astype(BF)))
+        return new, acc
 
     low = jnp.where(i * blk >= first_len, first_len // blk, 0)
     pairs = (i - low) // 2
     carry = lax.fori_loop(
-        0, pairs, lambda t, c: steps([low + 2 * t, low + 2 * t + 1], c), (top, total, acc)
-    )
-    top, total, acc = lax.fori_loop(low + 2 * pairs, i, lambda j, c: steps([j], c), carry)
-    out = (acc / total).astype(BF)
+        0, pairs, lambda t, c: steps([low + 2 * t, low + 2 * t + 1], c), (top, acc)
+    )
+    top, acc = lax.fori_loop(low + 2 * pairs, i, lambda j, c: steps([j], c), carry)
+    total = acc[HD : HD + 1]
+    out = (acc[:HD] / total).astype(BF)
     for s in range(GROUP):
 
         @pl.when((i // per) ^ place == s)
@@ -182,7 +184,11 @@
         [fixed((HD, rows))] * GROUP + [pl.BlockSpec((1, 1, blk), lambda i, n: (i, 0, 0))],
         [like((HD, rows), BF)] * GROUP + [like((count, 1, blk), F32)],
         qkv,
-        scratch=[pltpu.VMEM((GROUP * rows, 128), BF), pltpu.VMEM((GROUP, features, rows), BF)],
+        scratch=[
+            pltpu.VMEM((GROUP * rows, 128), BF),
+            pltpu.VMEM((HD + 16, GROUP * rows), BF),
+            pltpu.VMEM((GROUP, features, rows), BF),
+        ],
     )
 
 
@@ -420,13 +426,13 @@
 
 def first_back_kernel(at_ref, *refs):
     shares = refs[:4]
-    x_ref, dh_ref, gain_ref, out_ref = refs[4:]
+    x_ref, dh_ref, gain_ref, _, out_ref = refs[4:]
     d_a = add_up(shares)
     normal, scale = normalize(x_ref[...].astype(F32))
     out_ref[...] = (dh_ref[...] + norm_back(d_a, gain_ref[...], normal, scale)).astype(BF)
 
 
-def first_back(at, shares, tokens, dh, gain):
+def first_back(at, shares, tokens, dh, gain, after):
     quarter, width = dh.shape
     return call(
         first_back_kernel,
@@ -435,10 +441,10 @@
         (1,),
         [fixed((quarter, width))] * 4
         + [pl.BlockSpec((quarter, width), lambda i, n: (n[1], 0))]
-        + [fixed((quarter, width)), fixed((1, width))],
+        + [fixed((quarter, width)), fixed((1, width)), pl.BlockSpec(memory_space=pl.ANY)],
         fixed((quarter, width)),
         like((quarter, width), BF),
-        (*shares, tokens, dh, gain),
+        (*shares, tokens, dh, gain, after),
     )
 
 
@@ -1056,10 +1062,10 @@
         at, d_qkv, o_pieces, a_r, dh_r, w_heads, gains[0], biases[0], sums_2, (small_0, small_1, small_t), experts
     )
     grad_up = ein("rd,rf->df", got, d_eu)
-    grads_a, output, grad_up, *far = barrier((grads_a, output, grad_up, *far))
+    grads_a, corner, grad_up, *far = barrier((grads_a, output[:16, :128], grad_up, *far))
     grads_a = lax.psum_scatter(grads_a, "dp", scatter_dimension=0, tiled=True).T
     shares = scatter_near(shares, far)
-    grad_q = first_back(at, shares, tokens, dh, gains[0])
+    grad_q = first_back(at, shares, tokens, dh, gains[0], corner)
     grad_tokens = join(at, gather_pieces(grad_q))
 
     own, heads = width // dps, heads_loc * HD

time: 565 us -> 567 us (level)
  Pallas kernels: 186 us -> 200 us
  starting transfers between devices: 104 us -> 92.7 us
    ppermute x23, waiting for transfers between devices: 74.5 us -> 89.7 us  [hop(): return lax.ppermute(value, 'mp', pairs)]
    psum x1, waiting for transfers between devices: 27 us -> 13.4 us  [body(): output = lax.psum(mix, 'mp')]
    pallas_call x20, Pallas kernels: 186 us -> 200 us  [call(): pl.pallas_call(kernel, grid_spec=pltpu.PrefetchScalarGridSpec(num_scalar_...]
  transfers between devices with their start and end apart: 48 -> 48, of which waited for: 25 -> 27; matrix products, arithmetic and copies ran while one was open for 9% -> 10% of each run, Pallas kernels for 34% -> 36%
where the time goes in v2:
time: 567 us; the launch traced here: 558 us
  Pallas kernels  200 us (35%)
  waiting for transfers between devices  171 us (30%)
  starting transfers between devices  92.7 us (16%)
  local copies, waits for them, and re-layouts  36.1 us (6%)
  other arithmetic  25.6 us (5%)
  matrix products  18.5 us (3%)
  between operations  15.3 us (3%)
    pallas_call x20, Pallas kernels, call(): pl.pallas_call(kernel, grid_spec=pltpu.PrefetchScalarGridSpec(num_scalar_...  200 us
    ppermute x23, waiting for transfers between devices, hop(): return lax.ppermute(value, 'mp', pairs)  89.7 us
    ppermute x23, starting transfers between devices, hop(): return lax.ppermute(value, 'mp', pairs)  50.1 us
    all_to_all x6, waiting for transfers between devices, expert_swap(): return lax.all_to_all(wide, 'dp', 0, 0, tiled=True).reshape(value.shape)  30.8 us
    unnamed x156, local copies, waits for them, and re-layouts  30.2 us
    all_to_all x6, starting transfers between devices, expert_swap(): return lax.all_to_all(wide, 'dp', 0, 0, tiled=True).reshape(value.shape)  25.9 us
    dot_general x2, matrix products, ein(): return jnp.einsum(spec, a, b, preferred_element_type=F32)  18.5 us
    reduce_scatter x1, waiting for transfers between devices, body(): grads_a = lax.psum_scatter(grads_a, 'dp', scatter_dimension=0, tiled=True).T  18 us
  transfers between devices with their start and end apart: 48, of which 27 were waited for; matrix products, arithmetic and copies ran while one was open for 10% of the time, Pallas kernels for 36%

profile of v2, /device:TPU:0, one launch (start us, length us, event | category | flops | bytes accessed | tf_op | source)
XLA Modules:
  0.0 558.4 jit_solution(6582293140369265726)
XLA Ops:
  12.2 6.9 %project.1 = (bf16[1024,1024]{1,0:T(8,128)(2,1)S(1)}, bf16[192,1024]{1,0:T(8,128)(2,1)S(1)}, bf16[192,1024]{1,0:T(8,128)(2,1)}, bf16[192,1024]{1,0:T(8,128)(2,1)}, bf16[192,1024]{1,0:T(8,128)(2,1)}) custom-call(s32[4]{0:T(128)S(1)} %pad_add_fusion.at_ref, bf16[1024,1024]{1,0:T(8,128)(2,1)} %refs_4_.1, ...), custom_call_target="tpu_custom_call" | custom-call | flops 1048576 | bytes 1048576 | tf_op jit(solution)/shard_map/project/pallas_call | solution.py:30
  20.9 2.5 collective-permute-start.1
  24.6 2.3 reduce-window.6
  27.6 2.3 multiply_add_fusion
  30.4 3.4 fusion.rows_ref.dy_ref.refs_6_
  34.5 7.6 %dispatch.3 = bf16[2048,1024]{1,0:T(8,128)(2,1)} custom-call(s32[4]{0:T(128)S(1)} %pad_add_fusion.at_ref, s32[1,1024]{1,0:T(1,128)S(1)} %get-tuple-element.331.dest_ref, bf16[1024,1024]{1,0:T(8,128)(2,1)S(1)} %fusion.rows_ref.dy_ref.refs_6_), custom_call_target="tpu_custom_call" | custom-call | flops 1048576 | bytes 1048576 | tf_op jit(solution)/shard_map/dispatch/pallas_call | solution.py:30
  42.1 22.2 %attend.1 = (bf16[64,1024]{1,0:T(8,128)(2,1)S(1)}, bf16[64,1024]{1,0:T(8,128)(2,1)S(1)}, bf16[64,1024]{1,0:T(8,128)(2,1)S(1)}, bf16[64,1024]{1,0:T(8,128)(2,1)S(1)}, f32[8,1,512]{2,1,0:T(1,128)S(1)}) custom-call(s32[4]{0:T(128)S(1)} %pad_add_fusion.at_ref, bf16[192,1024]{1,0:T(8,128)(2,1)S(1)} %get-tuple-element.141.refs_0_, ...), custom_call_target="tpu_custom_call" | custom-call | flops 1048576 | bytes 1048576 | tf_op jit(solution)/shard_map/attend/pallas_call | solution.py:30
  65.1 1.9 collective-permute-start.4
  67.9 3.5 collective-permute-done.4.refs_2_
  71.4 1.9 collective-permute-done.5.refs_3_
  73.3 4.6 all-to-all-start
  79.8 4.6 collective-permute-start.6
  84.4 3.2 collective-permute-start.8
  87.6 7.0 %collective-permute-done.7.refs_2_.refs_6_ = bf16[256,1024]{1,0:T(8,128)(2,1)S(1)} collective-permute-done((bf16[256,1024]{1,0:T(8,128)(2,1)S(1)}, bf16[256,1024]{1,0:T(8,128)(2,1)S(1)}, u32[]{:S(2)}, u32[]{:S(2)}) %collective-permute-start.7) | collective-permute-done | bytes 524320 | tf_op jit(solution)/shard_map/ppermute | solution.py:876
  97.6 10.4 %collective-permute-done.8.refs_3_.refs_7_ = bf16[256,1024]{1,0:T(8,128)(2,1)S(1)} collective-permute-done((bf16[256,1024]{1,0:T(8,128)(2,1)S(1)}, bf16[256,1024]{1,0:T(8,128)(2,1)S(1)}, u32[]{:S(2)}, u32[]{:S(2)}) %collective-permute-start.8) | collective-permute-done | bytes 524320 | tf_op jit(solution)/shard_map/ppermute | solution.py:876
  108.0 11.1 %collective-permute-done.10.refs_5_.refs_9_ = bf16[256,1024]{1,0:T(8,128)(2,1)S(1)} collective-permute-done((bf16[256,1024]{1,0:T(8,128)(2,1)S(1)}, bf16[256,1024]{1,0:T(8,128)(2,1)S(1)}, u32[]{:S(2)}, u32[]{:S(2)}) %collective-permute-start.10) | collective-permute-done | bytes 524320 | tf_op jit(solution)/shard_map/ppermute | solution.py:876
  119.1 8.5 %mid.1 = (f32[256,1024]{1,0:T(8,128)S(1)}, bf16[1024,1024]{1,0:T(8,128)(2,1)}) custom-call(s32[4]{0:T(128)S(1)} %pad_add_fusion.at_ref, bf16[256,1024]{1,0:T(8,128)(2,1)S(1)} %stack.26.refs_0_.refs_4_, bf16[256,1024]{1,0:T(8,128)(2,1)S(1)} %collective-permute-done.6.refs_1_.refs_5_, bf16[256,1024]{1,0:T(8,128)(2,1)S(1)} %collective-permute-done.7.refs_2_.refs_6_, ...), custom_call_target="tpu_custom_call" | custom-call | flops 1048576 | bytes 1048576 | tf_op jit(solution)/shard_map/mid/pallas_call | solution.py:30
  130.2 4.3 dispatch.5
  135.8 4.5 all-to-all-start.1
  141.0 4.3 dispatch.4
  146.6 19.4 %dense_rows.1 = (bf16[1024,1024]{1,0:T(8,128)(2,1)}, bf16[1024,1024]{1,0:T(8,128)(2,1)}, bf16[1024,1024]{1,0:T(8,128)(2,1)}, f32[1024,1024]{1,0:T(8,128)}, f32[1024,1024]{1,0:T(8,128)}, /*index=5*/f32[128,1024]{1,0:T(8,128)}) custom-call(s32[4]{0:T(128)} %copy-done.45, bf16[1024,1024]{1,0:T(8,128)(2,1)} %get-tuple-element.177.rows_ref.b_ref, ...), custom_call_target="tpu_custom_call" | custom-call | flops 1048576 | bytes 1048576 | tf_op jit(solution)/shard_map/dense_rows/pallas_call | solution.py:30
  166.9 4.0 all-to-all-start.3
  170.9 19.6 %expert_rows.2 = (bf16[2048,1024]{1,0:T(8,128)(2,1)}, bf16[2048,1024]{1,0:T(8,128)(2,1)}, bf16[2048,1024]{1,0:T(8,128)(2,1)}, bf16[2048,1024]{1,0:T(8,128)(2,1)}...) custom-call(s32[4]{0:T(128)} %copy-done.45, ...), custom_call_target="tpu_custom_call" | custom-call | flops 1048576 | bytes 1048576 | tf_op jit(solution)/shard_map/expert_rows/pallas_call | solution.py:30
  190.6 6.9 %all-to-all-done.3 = bf16[8,128,1024]{2,1,0:T(8,128)(2,1)S(1)} async-done(((bf16[8,128,1024]{2,1,0:T(8,128)(2,1)}), bf16[8,128,1024]{2,1,0:T(8,128)(2,1)S(1)}, u32[]{:S(2)}, u32[]{:S(2)}) %all-to-all-start.3) | async-done | bytes 2097184 | tf_op jit(solution)/shard_map/all_to_all | solution.py:918
  198.8 3.8 all-to-all-start.2
  202.6 19.7 %expert_rows.3 = (bf16[2048,1024]{1,0:T(8,128)(2,1)}, bf16[2048,1024]{1,0:T(8,128)(2,1)}, bf16[2048,1024]{1,0:T(8,128)(2,1)}, bf16[2048,1024]{1,0:T(8,128)(2,1)}...) custom-call(s32[4]{0:T(128)} %copy-done.45, ...), custom_call_target="tpu_custom_call", output_to_operand_aliasing={{0}: (6, {}), {1}: (7, {}), {2}: (8, {}), {3}: (9, {}), {4}... | custom-call | flops 1048576 | bytes 1048576 | tf_op jit(solution)/shard_map/expert_rows/pallas_call | solution.py:30
  222.4 6.8 %all-to-all-done.2 = bf16[8,128,1024]{2,1,0:T(8,128)(2,1)S(1)} async-done(((bf16[8,128,1024]{2,1,0:T(8,128)(2,1)}), bf16[8,128,1024]{2,1,0:T(8,128)(2,1)S(1)}, u32[]{:S(2)}, u32[]{:S(2)}) %all-to-all-start.2) | async-done | bytes 2097184 | tf_op jit(solution)/shard_map/all_to_all | solution.py:918
  230.5 4.3 all-to-all-start.4
  234.9 11.5 %dense_grads.1 = (bf16[4,128,2048]{2,1,0:T(8,128)(2,1)S(1)}, bf16[4,128,2048]{2,1,0:T(8,128)(2,1)}) custom-call(s32[4]{0:T(128)S(1)} %copy-done.46, bf16[1024,1024]{1,0:T(8,128)(2,1)} %get-tuple-element.177.rows_ref.b_ref, bf16[1024,1024]{1,0:T(8,128)(2,1)} %get-tuple-element.178.d_up_ref, bf16[1024,1024]{1,0:T(8,128)(2,1)} %get-tuple-element.179.grad_ref, ...), custom_call_target="tpu_custom_call" | custom-call | flops 1048576 | bytes 1048576 | tf_op jit(solution)/shard_map/dense_grads/pallas_call | solution.py:30
  247.6 13.9 %all-to-all-done.4 = bf16[8,128,1024]{2,1,0:T(8,128)(2,1)} async-done(((bf16[8,128,1024]{2,1,0:T(8,128)(2,1)}), bf16[8,128,1024]{2,1,0:T(8,128)(2,1)}, u32[]{:S(2)}, u32[]{:S(2)}) %all-to-all-start.4) | async-done | bytes 2097184 | tf_op jit(solution)/shard_map/all_to_all | solution.py:918
  261.5 4.7 all-to-all-start.5
  266.3 8.5 %combine.2 = (f32[256,1024]{1,0:T(8,128)S(1)}, bf16[256,1024]{1,0:T(8,128)(2,1)S(1)}, bf16[256,1024]{1,0:T(8,128)(2,1)S(1)}, bf16[256,1024]{1,0:T(8,128)(2,1)S(1)}, bf16[256,1024]{1,0:T(8,128)(2,1)S(1)}) custom-call(s32[4]{0:T(128)S(1)} %copy-done.46, s32[1024,1]{1,0:T(8,128)S(1)} %copy-done.21, s32[1024,1]{1,0:T(8,128)S(1)} %copy-done.20, ...), custom_call_target="tpu_custom_call" | custom-call | flops 1048576 | bytes 1048576 | tf_op jit(solution)/shard_map/combine/pallas_call | solution.py:30
  275.8 5.7 %collective-permute-start.13 = (bf16[256,1024]{1,0:T(8,128)(2,1)S(1)}, bf16[256,1024]{1,0:T(8,128)(2,1)S(1)}, u32[]{:S(2)}, u32[]{:S(2)}) collective-permute-start(bf16[256,1024]{1,0:T(8,128)(2,1)S(1)} %get-tuple-element.189), channel_id=1, source_target_pairs={{0,3},{3,0},{4,7},{7,4},{8,11},{11,8},{12,15},{15,12},{16,19},{19,... | collective-permute-start | bytes 1572872 | tf_op jit(solution)/shard_map/ppermute | solution.py:876
  283.6 10.8 %collective-permute-done.13.refs_3_ = bf16[256,1024]{1,0:T(8,128)(2,1)S(1)} collective-permute-done((bf16[256,1024]{1,0:T(8,128)(2,1)S(1)}, bf16[256,1024]{1,0:T(8,128)(2,1)S(1)}, u32[]{:S(2)}, u32[]{:S(2)}) %collective-permute-start.13) | collective-permute-done | bytes 524320 | tf_op jit(solution)/shard_map/ppermute | solution.py:876
  294.4 10.1 %collective-permute-done.12 = bf16[256,1024]{1,0:T(8,128)(2,1)S(1)} collective-permute-done((bf16[256,1024]{1,0:T(8,128)(2,1)S(1)}, bf16[256,1024]{1,0:T(8,128)(2,1)S(1)}, u32[]{:S(2)}, u32[]{:S(2)}) %collective-permute-start.12) | collective-permute-done | bytes 524320 | tf_op jit(solution)/shard_map/ppermute | solution.py:876
  305.5 5.2 collective-permute-start.15
  313.1 2.2 all-to-all-done.5
  315.3 9.3 %combine.3 = bf16[1024,1024]{1,0:T(8,128)(2,1)} custom-call(s32[4]{0:T(128)S(1)} %copy-done.46, s32[1024,1]{1,0:T(8,128)S(1)} %copy-done.19, bf16[2048,1024]{1,0:T(8,128)(2,1)} %bitcast.20.refs_1_, f32[1024,1024]{1,0:T(8,128)} %get-tuple-element.197.refs_2_, f32[256,1024]{1,0:T(8,128)S(1)} %copy-done.7), custom_call_target="tpu_custom_call" | custom-call | flops 1048576 | bytes 1048576 | tf_op jit(solution)/shard_map/combine/pallas_call | solution.py:30
  324.7 3.2 collective-permute-done.14.refs_1_
  330.1 4.2 mid_back.1
  337.4 3.5 collective-permute-done.16.refs_1_
  340.9 6.9 %collective-permute-done.17.refs_2_ = bf16[256,256]{1,0:T(8,128)(2,1)S(1)} collective-permute-done((bf16[256,256]{1,0:T(8,128)(2,1)S(1)}, bf16[256,256]{1,0:T(8,128)(2,1)S(1)}, u32[]{:S(2)}, u32[]{:S(2)}) %collective-permute-start.17) | collective-permute-done | bytes 131104 | tf_op jit(solution)/shard_map/ppermute | solution.py:876
  350.3 3.5 add_convert_fusion.1
  360.8 32.1 %attend_back.1 = (bf16[192,1024]{1,0:T(8,128)(2,1)S(1)}, bf16[192,1024]{1,0:T(8,128)(2,1)S(1)}, bf16[192,1024]{1,0:T(8,128)(2,1)S(1)}, bf16[192,1024]{1,0:T(8,128)(2,1)S(1)}) custom-call(s32[4]{0:T(128)S(1)} %copy-done.46, bf16[192,1024]{1,0:T(8,128)(2,1)S(1)} %get-tuple-element.141.refs_0_, bf16[192,1024]{1,0:T(8,128)(2,1)S(1)} %copy-done.23, ...), custom_call_target="tpu_custom_call" | custom-call | flops 1048576 | bytes 1048576 | tf_op jit(solution)/shard_map/attend_back/pallas_call | solution.py:30
  394.9 10.2 %fusion.10 = f32[1024,1024]{1,0:T(8,128)} fusion(bf16[2048,1024]{1,0:T(8,128)(2,1)} %get-tuple-element.233, bf16[2048,1024]{1,0:T(8,128)(2,1)} %get-tuple-element.234), kind=kOutput, calls=%fused_computation.46 | convolution fusion | flops 4294967296 | bytes 12582912 | tf_op jit(solution)/shard_map/rf,rd->fd/dot_general | solution.py:26
  405.1 7.4 %collective-permute-done.26.refs_3_ = bf16[192,1024]{1,0:T(8,128)(2,1)S(1)} collective-permute-done((bf16[192,1024]{1,0:T(8,128)(2,1)S(1)}, bf16[192,1024]{1,0:T(8,128)(2,1)S(1)}, u32[]{:S(2)}, u32[]{:S(2)}) %collective-permute-start.26) | collective-permute-done | bytes 393248 | tf_op jit(solution)/shard_map/ppermute | solution.py:913
  412.5 6.3 %project_back.1 = (f32[256,1024]{1,0:T(8,128)S(1)}, bf16[256,1024]{1,0:T(8,128)(2,1)S(1)}, bf16[256,1024]{1,0:T(8,128)(2,1)}, bf16[256,1024]{1,0:T(8,128)(2,1)S(1)}, bf16[256,1024]{1,0:T(8,128)(2,1)}) custom-call(s32[4]{0:T(128)S(1)} %copy-done.46, bf16[192,1024]{1,0:T(8,128)(2,1)S(1)} %get-tuple-element.235.refs_0_, ...), custom_call_target="tpu_custom_call" | custom-call | flops 1048576 | bytes 1048576 | tf_op jit(solution)/shard_map/project_back/pallas_call | solution.py:30
  419.7 2.8 collective-permute-start.28
  423.3 5.6 %collective-permute-start.29 = (bf16[256,1024]{1,0:T(8,128)(2,1)}, bf16[256,1024]{1,0:T(8,128)(2,1)S(1)}, u32[]{:S(2)}, u32[]{:S(2)}) collective-permute-start(bf16[256,1024]{1,0:T(8,128)(2,1)} %get-tuple-element.250), channel_id=1, source_target_pairs={{0,3},{3,0},{4,7},{7,4},{8,11},{11,8},{12,15},{15,12},{16,19},{19,... | collective-permute-start | bytes 1572872 | tf_op jit(solution)/shard_map/ppermute | solution.py:876
  428.9 8.3 %fusion.11 = f32[1024,1024]{1,0:T(8,128)} fusion(bf16[2048,1024]{1,0:T(8,128)(2,1)S(1)} %copy-done.63, bf16[2048,1024]{1,0:T(8,128)(2,1)} %get-tuple-element.248), kind=kOutput, calls=%fused_computation.47 | convolution fusion | flops 4294967296 | bytes 12582912 | tf_op jit(solution)/shard_map/rd,rf->df/dot_general | solution.py:26
  437.3 8.5 %attention_grads.1 = bf16[1024,1920]{1,0:T(8,128)(2,1)} custom-call(s32[4]{0:T(128)S(1)} %copy-done.46, bf16[192,1024]{1,0:T(8,128)(2,1)S(1)} %get-tuple-element.235.refs_0_, bf16[192,1024]{1,0:T(8,128)(2,1)S(1)} %collective-permute-done.24.refs_1_, bf16[192,1024]{1,0:T(8,128)(2,1)S(1)} %collective-permute-done.25.refs_2_, ...), custom_call_target="tpu_custom_call" | custom-call | flops 1048576 | bytes 1048576 | tf_op jit(solution)/shard_map/attention_grads/pallas_call | solution.py:30
  445.9 13.4 %all-reduce.2.cloned.1.call-done = bf16[1024,1024]{1,0:T(8,128)(2,1)} async-done(((bf16[1024,1024]{1,0:T(8,128)(2,1)}), bf16[1024,1024]{1,0:T(8,128)(2,1)}) %all-reduce.2.cloned.1.call-update) | async-done | bytes 2097168 | tf_op jit(solution)/shard_map/psum | solution.py:1030
  459.9 7.3 %collective-permute-done.29.refs_3_ = bf16[256,1024]{1,0:T(8,128)(2,1)S(1)} collective-permute-done((bf16[256,1024]{1,0:T(8,128)(2,1)}, bf16[256,1024]{1,0:T(8,128)(2,1)S(1)}, u32[]{:S(2)}, u32[]{:S(2)}) %collective-permute-start.29) | collective-permute-done | bytes 524320 | tf_op jit(solution)/shard_map/ppermute | solution.py:876
  471.5 10.0 %collective-permute-done.31.refs_2_ = bf16[256,1024]{1,0:T(8,128)(2,1)S(1)} collective-permute-done((bf16[256,1024]{1,0:T(8,128)(2,1)S(1)}, bf16[256,1024]{1,0:T(8,128)(2,1)S(1)}, u32[]{:S(2)}, u32[]{:S(2)}) %collective-permute-start.31) | collective-permute-done | bytes 524320 | tf_op jit(solution)/shard_map/ppermute | solution.py:876
  481.5 4.4 collective-permute-done.30.refs_1_
  486.9 2.5 first_back.1.refs_0_
  490.7 4.6 collective-permute-start.32
  499.3 2.8 collective-permute-start.34
  502.1 2.9 collective-permute-done.33.refs_2_
  508.3 18.0 %reduce-scatter.2.cloned.1.call-done = bf16[128,1920]{1,0:T(8,128)(2,1)} async-done(((bf16[1024,1920]{1,0:T(8,128)(2,1)}), bf16[128,1920]{1,0:T(8,128)(2,1)}) %reduce-scatter.2.cloned.1.call-update) | async-done | bytes 491536 | tf_op jit(solution)/shard_map/reduce_scatter | solution.py:1066
  528.9 4.6 all-to-all-start.6
  535.9 2.0 copy.91
  537.9 2.9 join.1
  542.9 2.4 all-to-all-done.6
  (260 shorter events, 79.3 us)
Async XLA Ops:
  7.2 57.8 %all-gather.2.cloned.1.call-start = ((), (), s32[]{:S(2)}) async-start(), calls=%async_computation.8 | async-start | bytes 2621440 | tf_op jit(solution)/shard_map/all_gather | solution.py:961
  11.6 128.6 %copy-start.45 = (s32[4]{0:T(128)}, s32[4]{0:T(128)S(1)}, u32[]{:S(2)}) copy-start(s32[4]{0:T(128)S(1)} %pad_add_fusion.at_ref) | copy-start | bytes 52
  20.4 21.6 %collective-permute-start = (bf16[192,1024]{1,0:T(8,128)(2,1)}, bf16[192,1024]{1,0:T(8,128)(2,1)S(1)}, u32[]{:S(2)}, u32[]{:S(2)}) collective-permute-start(bf16[192,1024]{1,0:T(8,128)(2,1)} %get-tuple-element.138), channel_id=1, source_target_pairs={{0,4},{4,0},{8,12},{12,8},{16,20},{20,16},{24,28},{28,24},{1,5},{5... | collective-permute-start | bytes 1179656 | tf_op jit(solution)/shard_map/ppermute | solution.py:913
  20.9 21.2 %collective-permute-start.1 = (bf16[192,1024]{1,0:T(8,128)(2,1)}, bf16[192,1024]{1,0:T(8,128)(2,1)S(1)}, u32[]{:S(2)}, u32[]{:S(2)}) collective-permute-start(bf16[192,1024]{1,0:T(8,128)(2,1)} %get-tuple-element.139), channel_id=1, source_target_pairs={{0,8},{4,12},{8,0},{12,4},{16,24},{20,28},{24,16},{28,20},{1,9},{5... | collective-permute-start | bytes 1179656 | tf_op jit(solution)/shard_map/ppermute | solution.py:913
  23.4 18.7 %collective-permute-start.2 = (bf16[192,1024]{1,0:T(8,128)(2,1)}, bf16[192,1024]{1,0:T(8,128)(2,1)S(1)}, u32[]{:S(2)}, u32[]{:S(2)}) collective-permute-start(bf16[192,1024]{1,0:T(8,128)(2,1)} %get-tuple-element.140), channel_id=1, source_target_pairs={{0,12},{4,8},{8,4},{12,0},{16,28},{20,24},{24,20},{28,16},{1,13},{... | collective-permute-start | bytes 1179656 | tf_op jit(solution)/shard_map/ppermute | solution.py:913
  42.1 31.2 %copy-start.22 = (bf16[192,1024]{1,0:T(8,128)(2,1)}, bf16[192,1024]{1,0:T(8,128)(2,1)S(1)}, u32[]{:S(2)}) copy-start(bf16[192,1024]{1,0:T(8,128)(2,1)S(1)} %collective-permute-done.refs_1_) | copy-start | bytes 1179652
  42.1 31.2 %copy-start.24 = (bf16[192,1024]{1,0:T(8,128)(2,1)}, bf16[192,1024]{1,0:T(8,128)(2,1)S(1)}, u32[]{:S(2)}) copy-start(bf16[192,1024]{1,0:T(8,128)(2,1)S(1)} %collective-permute-done.1.refs_2_) | copy-start | bytes 1179652
  42.1 31.2 %copy-start.26 = (bf16[192,1024]{1,0:T(8,128)(2,1)}, bf16[192,1024]{1,0:T(8,128)(2,1)S(1)}, u32[]{:S(2)}) copy-start(bf16[192,1024]{1,0:T(8,128)(2,1)S(1)} %collective-permute-done.2.refs_3_) | copy-start | bytes 1179652
  64.9 2.9 collective-permute-start.3
  65.1 6.3 %collective-permute-start.4 = (bf16[64,1024]{1,0:T(8,128)(2,1)S(1)}, bf16[64,1024]{1,0:T(8,128)(2,1)S(1)}, u32[]{:S(2)}, u32[]{:S(2)}) collective-permute-start(bf16[64,1024]{1,0:T(8,128)(2,1)S(1)} %get-tuple-element.151.refs_10_), channel_id=1, source_target_pairs={{0,8},{4,12},{8,0},{12,4},{16,24},{20,28},{24,16},{28,20},{1,9},{5... | collective-permute-start | bytes 393224 | tf_op jit(solution)/shard_map/ppermute | solution.py:913
  67.0 6.3 %collective-permute-start.5 = (bf16[64,1024]{1,0:T(8,128)(2,1)S(1)}, bf16[64,1024]{1,0:T(8,128)(2,1)S(1)}, u32[]{:S(2)}, u32[]{:S(2)}) collective-permute-start(bf16[64,1024]{1,0:T(8,128)(2,1)S(1)} %get-tuple-element.152.refs_11_), channel_id=1, source_target_pairs={{0,12},{4,8},{8,4},{12,0},{16,28},{20,24},{24,20},{28,16},{1,13},{... | collective-permute-start | bytes 393224 | tf_op jit(solution)/shard_map/ppermute | solution.py:913
  73.3 45.8 %copy-start.58 = (f32[1,1024]{1,0:T(1,128)S(1)}, f32[1,1024]{1,0:T(1,128)}, u32[]{:S(2)}) copy-start(f32[1,1024]{1,0:T(1,128)} %get-tuple-element.327.refs_9_) | copy-start | bytes 12292
  73.3 62.4 %all-to-all-start = ((bf16[8,256,1024]{2,1,0:T(8,128)(2,1)}), bf16[8,256,1024]{2,1,0:T(8,128)(2,1)}, u32[]{:S(2)}, u32[]{:S(2)}) async-start(bf16[8,256,1024]{2,1,0:T(8,128)(2,1)} %bitcast.72), calls=%async_computation | async-start | bytes 8388608 | tf_op jit(solution)/shard_map/all_to_all | solution.py:918
  78.5 16.1 %collective-permute-start.7 = (bf16[256,1024]{1,0:T(8,128)(2,1)S(1)}, bf16[256,1024]{1,0:T(8,128)(2,1)S(1)}, u32[]{:S(2)}, u32[]{:S(2)}) collective-permute-start(bf16[256,1024]{1,0:T(8,128)(2,1)S(1)} %stack.26.refs_0_.refs_4_), channel_id=1, source_target_pairs={{1,0},{2,1},{3,2},{5,4},{6,5},{7,6},{9,8},{10,9},{11,10},{13,12},{... | collective-permute-start | bytes 1572872 | tf_op jit(solution)/shard_map/ppermute | solution.py:876
  79.8 16.8 %collective-permute-start.6 = (bf16[256,1024]{1,0:T(8,128)(2,1)S(1)}, bf16[256,1024]{1,0:T(8,128)(2,1)S(1)}, u32[]{:S(2)}, u32[]{:S(2)}) collective-permute-start(bf16[256,1024]{1,0:T(8,128)(2,1)S(1)} %stack.26.refs_0_.refs_4_), channel_id=1, source_target_pairs={{0,1},{1,2},{2,3},{4,5},{5,6},{6,7},{8,9},{9,10},{10,11},{12,13},{... | collective-permute-start | bytes 1572872 | tf_op jit(solution)/shard_map/ppermute | solution.py:876
  84.4 23.6 %collective-permute-start.8 = (bf16[256,1024]{1,0:T(8,128)(2,1)S(1)}, bf16[256,1024]{1,0:T(8,128)(2,1)S(1)}, u32[]{:S(2)}, u32[]{:S(2)}) collective-permute-start(bf16[256,1024]{1,0:T(8,128)(2,1)S(1)} %stack.26.refs_0_.refs_4_), channel_id=1, source_target_pairs={{0,3},{3,0},{4,7},{7,4},{8,11},{11,8},{12,15},{15,12},{16,19},{19,... | collective-permute-start | bytes 1572872 | tf_op jit(solution)/shard_map/ppermute | solution.py:876
  94.6 24.5 %collective-permute-start.10 = (bf16[256,1024]{1,0:T(8,128)(2,1)S(1)}, bf16[256,1024]{1,0:T(8,128)(2,1)S(1)}, u32[]{:S(2)}, u32[]{:S(2)}) collective-permute-start(bf16[256,1024]{1,0:T(8,128)(2,1)S(1)} %collective-permute-done.7.refs_2_.refs_6_), channel_id=1, source_target_pairs={{1,0},{2,1},{5,4},{6,5},{9,8},{10,9},{13,12},{14,13},{17,16},{18,1... | collective-permute-start | bytes 1572872 | tf_op jit(solution)/shard_map/ppermute | solution.py:876
  96.6 30.9 %copy-start.8 = (bf16[256,1024]{1,0:T(8,128)(2,1)}, bf16[256,1024]{1,0:T(8,128)(2,1)S(1)}, u32[]{:S(2)}) copy-start(bf16[256,1024]{1,0:T(8,128)(2,1)S(1)} %collective-permute-done.6.refs_1_.refs_5_) | copy-start | bytes 1572868
  96.7 22.4 %collective-permute-start.9 = (bf16[256,1024]{1,0:T(8,128)(2,1)S(1)}, bf16[256,1024]{1,0:T(8,128)(2,1)S(1)}, u32[]{:S(2)}, u32[]{:S(2)}) collective-permute-start(bf16[256,1024]{1,0:T(8,128)(2,1)S(1)} %collective-permute-done.6.refs_1_.refs_5_), channel_id=1, source_target_pairs={{1,2},{2,3},{5,6},{6,7},{9,10},{10,11},{13,14},{14,15},{17,18},{18... | collective-permute-start | bytes 1572872 | tf_op jit(solution)/shard_map/ppermute | solution.py:876
  108.0 19.6 %copy-start.10 = (bf16[256,1024]{1,0:T(8,128)(2,1)}, bf16[256,1024]{1,0:T(8,128)(2,1)S(1)}, u32[]{:S(2)}) copy-start(bf16[256,1024]{1,0:T(8,128)(2,1)S(1)} %collective-permute-done.8.refs_3_.refs_7_) | copy-start | bytes 1572868
  135.8 31.1 %all-to-all-start.1 = ((bf16[8,128,1024]{2,1,0:T(8,128)(2,1)}), bf16[8,128,1024]{2,1,0:T(8,128)(2,1)}, u32[]{:S(2)}, u32[]{:S(2)}) async-start(bf16[8,128,1024]{2,1,0:T(8,128)(2,1)} %bitcast.71), calls=%async_computation.1 | async-start | bytes 4194304 | tf_op jit(solution)/shard_map/all_to_all | solution.py:918
  166.9 30.6 %all-to-all-start.3 = ((bf16[8,128,1024]{2,1,0:T(8,128)(2,1)}), bf16[8,128,1024]{2,1,0:T(8,128)(2,1)S(1)}, u32[]{:S(2)}, u32[]{:S(2)}) async-start(bf16[8,128,1024]{2,1,0:T(8,128)(2,1)} %bitcast.70), calls=%async_computation.3 | async-start | bytes 4194304 | tf_op jit(solution)/shard_map/all_to_all | solution.py:918
  198.8 30.4 %all-to-all-start.2 = ((bf16[8,128,1024]{2,1,0:T(8,128)(2,1)}), bf16[8,128,1024]{2,1,0:T(8,128)(2,1)S(1)}, u32[]{:S(2)}, u32[]{:S(2)}) async-start(bf16[8,128,1024]{2,1,0:T(8,128)(2,1)} %bitcast.81), calls=%async_computation.2 | async-start | bytes 4194304 | tf_op jit(solution)/shard_map/all_to_all | solution.py:918
  230.5 31.0 %all-to-all-start.4 = ((bf16[8,128,1024]{2,1,0:T(8,128)(2,1)}), bf16[8,128,1024]{2,1,0:T(8,128)(2,1)}, u32[]{:S(2)}, u32[]{:S(2)}) async-start(bf16[8,128,1024]{2,1,0:T(8,128)(2,1)} %bitcast.80), calls=%async_computation.4 | async-start | bytes 4194304 | tf_op jit(solution)/shard_map/all_to_all | solution.py:918
  261.5 53.8 %all-to-all-start.5 = ((bf16[8,256,1024]{2,1,0:T(8,128)(2,1)}), bf16[8,256,1024]{2,1,0:T(8,128)(2,1)}, u32[]{:S(2)}, u32[]{:S(2)}) async-start(bf16[8,256,1024]{2,1,0:T(8,128)(2,1)} %get-tuple-element.196), calls=%async_computation.5 | async-start | bytes 8388608 | tf_op jit(solution)/shard_map/all_to_all | solution.py:918
  266.2 193.0 %all-reduce.2.cloned.1.call-start = ((), (), s32[]{:S(2)}) async-start(), calls=%async_computation.9 | async-start | bytes 4194304 | tf_op jit(solution)/shard_map/psum | solution.py:1030
  275.8 39.5 %copy-start.7 = (f32[256,1024]{1,0:T(8,128)S(1)}, f32[256,1024]{1,0:T(8,128)}, u32[]{:S(2)}) copy-start(f32[256,1024]{1,0:T(8,128)} %copy-done.6) | copy-start | bytes 3145732
  275.8 39.5 %copy-start.19 = (s32[1024,1]{1,0:T(8,128)S(1)}, s32[1024,1]{1,0:T(8,128)}, u32[]{:S(2)}) copy-start(s32[1024,1]{1,0:T(8,128)} %get-tuple-element.314.refs_0_) | copy-start | bytes 12292
  275.8 18.6 %collective-permute-start.13 = (bf16[256,1024]{1,0:T(8,128)(2,1)S(1)}, bf16[256,1024]{1,0:T(8,128)(2,1)S(1)}, u32[]{:S(2)}, u32[]{:S(2)}) collective-permute-start(bf16[256,1024]{1,0:T(8,128)(2,1)S(1)} %get-tuple-element.189), channel_id=1, source_target_pairs={{0,3},{3,0},{4,7},{7,4},{8,11},{11,8},{12,15},{15,12},{16,19},{19,... | collective-permute-start | bytes 1572872 | tf_op jit(solution)/shard_map/ppermute | solution.py:876
  281.5 22.9 %collective-permute-start.12 = (bf16[256,1024]{1,0:T(8,128)(2,1)S(1)}, bf16[256,1024]{1,0:T(8,128)(2,1)S(1)}, u32[]{:S(2)}, u32[]{:S(2)}) collective-permute-start(bf16[256,1024]{1,0:T(8,128)(2,1)S(1)} %get-tuple-element.188), channel_id=1, source_target_pairs={{0,1},{1,2},{4,5},{5,6},{8,9},{9,10},{12,13},{13,14},{16,17},{17,1... | collective-permute-start | bytes 1572872 | tf_op jit(solution)/shard_map/ppermute | solution.py:876
  282.8 21.6 %collective-permute-start.11 = (bf16[256,1024]{1,0:T(8,128)(2,1)S(1)}, bf16[256,1024]{1,0:T(8,128)(2,1)S(1)}, u32[]{:S(2)}, u32[]{:S(2)}) collective-permute-start(bf16[256,1024]{1,0:T(8,128)(2,1)S(1)} %get-tuple-element.188), channel_id=1, source_target_pairs={{2,1},{3,2},{6,5},{7,6},{10,9},{11,10},{14,13},{15,14},{18,17},{19... | collective-permute-start | bytes 1572872 | tf_op jit(solution)/shard_map/ppermute | solution.py:876
  294.4 30.3 %copy-start.37 = (bf16[256,1024]{1,0:T(8,128)(2,1)}, bf16[256,1024]{1,0:T(8,128)(2,1)S(1)}, u32[]{:S(2)}) copy-start(bf16[256,1024]{1,0:T(8,128)(2,1)S(1)} %collective-permute-done.13.refs_3_) | copy-start | bytes 1572868
  304.5 45.8 %collective-permute-start.22 = (bf16[4,128,2048]{2,1,0:T(8,128)(2,1)}, bf16[4,128,2048]{2,1,0:T(8,128)(2,1)}, u32[]{:S(2)}, u32[]{:S(2)}) collective-permute-start(bf16[4,128,2048]{2,1,0:T(8,128)(2,1)} %get-tuple-element.213), channel_id=1, source_target_pairs={{0,4},{4,0},{8,12},{12,8},{16,20},{20,16},{24,28},{28,24},{1,5},{5... | collective-permute-start | bytes 6291464 | tf_op jit(solution)/shard_map/ppermute | solution.py:913
  305.5 19.2 %collective-permute-start.15 = (bf16[256,1024]{1,0:T(8,128)(2,1)}, bf16[256,1024]{1,0:T(8,128)(2,1)}, u32[]{:S(2)}, u32[]{:S(2)}) collective-permute-start(bf16[256,1024]{1,0:T(8,128)(2,1)} %add_convert_fusion.6), channel_id=1, source_target_pairs={{0,1},{1,2},{2,3},{4,5},{5,6},{6,7},{8,9},{9,10},{10,11},{12,13},{... | collective-permute-start | bytes 1572872 | tf_op jit(solution)/shard_map/ppermute | solution.py:876
  311.6 16.3 %collective-permute-start.14 = (bf16[256,1024]{1,0:T(8,128)(2,1)}, bf16[256,1024]{1,0:T(8,128)(2,1)}, u32[]{:S(2)}, u32[]{:S(2)}) collective-permute-start(bf16[256,1024]{1,0:T(8,128)(2,1)} %add_convert_fusion.7), channel_id=1, source_target_pairs={{1,0},{2,1},{3,2},{5,4},{6,5},{7,6},{9,8},{10,9},{11,10},{13,12},{... | collective-permute-start | bytes 1572872 | tf_op jit(solution)/shard_map/ppermute | solution.py:876
  330.1 20.2 %copy-start.18 = (bf16[4,128,2048]{2,1,0:T(8,128)(2,1)S(1)}, bf16[4,128,2048]{2,1,0:T(8,128)(2,1)}, u32[]{:S(2)}) copy-start(bf16[4,128,2048]{2,1,0:T(8,128)(2,1)} %copy-done.17) | copy-start | bytes 6291460
  335.4 18.5 %copy-start.33 = (bf16[256,1024]{1,0:T(8,128)(2,1)}, bf16[256,1024]{1,0:T(8,128)(2,1)S(1)}, u32[]{:S(2)}) copy-start(bf16[256,1024]{1,0:T(8,128)(2,1)S(1)} %get-tuple-element.242.refs_11_) | copy-start | bytes 1572868
  335.4 18.5 %copy-start.59 = (f32[2,1024]{1,0:T(2,128)}, f32[2,1024]{1,0:T(2,128)S(1)}, u32[]{:S(2)}) copy-start(f32[2,1024]{1,0:T(2,128)S(1)} %get-tuple-element.243.refs_15_) | copy-start | bytes 24580
  335.4 5.5 collective-permute-start.16
  335.9 11.9 %collective-permute-start.17 = (bf16[256,256]{1,0:T(8,128)(2,1)S(1)}, bf16[256,256]{1,0:T(8,128)(2,1)S(1)}, u32[]{:S(2)}, u32[]{:S(2)}) collective-permute-start(bf16[256,256]{1,0:T(8,128)(2,1)S(1)} %get-tuple-element.206), channel_id=1, source_target_pairs={{0,2},{1,3},{2,0},{3,1},{4,6},{5,7},{6,4},{7,5},{8,10},{9,11},{10,... | collective-permute-start | bytes 393224 | tf_op jit(solution)/shard_map/ppermute | solution.py:876
  336.4 11.4 %collective-permute-start.18 = (bf16[256,256]{1,0:T(8,128)(2,1)S(1)}, bf16[256,256]{1,0:T(8,128)(2,1)S(1)}, u32[]{:S(2)}, u32[]{:S(2)}) collective-permute-start(bf16[256,256]{1,0:T(8,128)(2,1)S(1)} %get-tuple-element.207), channel_id=1, source_target_pairs={{0,1},{1,2},{2,3},{3,0},{4,5},{5,6},{6,7},{7,4},{8,9},{9,10},{10,1... | collective-permute-start | bytes 393224 | tf_op jit(solution)/shard_map/ppermute | solution.py:876
  348.4 5.5 collective-permute-start.19
  348.4 6.4 %collective-permute-start.20 = (bf16[64,1024]{1,0:T(8,128)(2,1)S(1)}, bf16[64,1024]{1,0:T(8,128)(2,1)S(1)}, u32[]{:S(2)}, u32[]{:S(2)}) collective-permute-start(bf16[64,1024]{1,0:T(8,128)(2,1)S(1)} %get-tuple-element.210), channel_id=1, source_target_pairs={{0,8},{4,12},{8,0},{12,4},{16,24},{20,28},{24,16},{28,20},{1,9},{5... | collective-permute-start | bytes 393224 | tf_op jit(solution)/shard_map/ppermute | solution.py:913
  350.2 6.5 %collective-permute-start.21 = (bf16[64,1024]{1,0:T(8,128)(2,1)S(1)}, bf16[64,1024]{1,0:T(8,128)(2,1)S(1)}, u32[]{:S(2)}, u32[]{:S(2)}) collective-permute-start(bf16[64,1024]{1,0:T(8,128)(2,1)S(1)} %get-tuple-element.211), channel_id=1, source_target_pairs={{0,12},{4,8},{8,4},{12,0},{16,28},{20,24},{24,20},{28,16},{1,13},{... | collective-permute-start | bytes 393224 | tf_op jit(solution)/shard_map/ppermute | solution.py:913
  357.4 35.6 %collective-permute-start.23 = (bf16[2,128,2048]{2,1,0:T(8,128)(2,1)}, bf16[2,128,2048]{2,1,0:T(8,128)(2,1)}, u32[]{:S(2)}, u32[]{:S(2)}) collective-permute-start(bf16[2,128,2048]{2,1,0:T(8,128)(2,1)} %get-tuple-element.223), channel_id=1, source_target_pairs={{0,8},{4,12},{8,0},{12,4},{16,24},{20,28},{24,16},{28,20},{1,9},{5... | collective-permute-start | bytes 3145736 | tf_op jit(solution)/shard_map/ppermute | solution.py:913
  359.1 167.2 %reduce-scatter.2.cloned.1.call-start = ((), (), s32[]{:S(2)}) async-start(), calls=%async_computation.10 | async-start | bytes 4423680 | tf_op jit(solution)/shard_map/reduce_scatter | solution.py:1066
  392.9 12.2 %collective-permute-start.24 = (bf16[192,1024]{1,0:T(8,128)(2,1)S(1)}, bf16[192,1024]{1,0:T(8,128)(2,1)S(1)}, u32[]{:S(2)}, u32[]{:S(2)}) collective-permute-start(bf16[192,1024]{1,0:T(8,128)(2,1)S(1)} %get-tuple-element.230), channel_id=1, source_target_pairs={{0,4},{4,0},{8,12},{12,8},{16,20},{20,16},{24,28},{28,24},{1,5},{5... | collective-permute-start | bytes 1179656 | tf_op jit(solution)/shard_map/ppermute | solution.py:913
  393.0 12.1 %collective-permute-start.25 = (bf16[192,1024]{1,0:T(8,128)(2,1)S(1)}, bf16[192,1024]{1,0:T(8,128)(2,1)S(1)}, u32[]{:S(2)}, u32[]{:S(2)}) collective-permute-start(bf16[192,1024]{1,0:T(8,128)(2,1)S(1)} %get-tuple-element.231), channel_id=1, source_target_pairs={{0,8},{4,12},{8,0},{12,4},{16,24},{20,28},{24,16},{28,20},{1,9},{5... | collective-permute-start | bytes 1179656 | tf_op jit(solution)/shard_map/ppermute | solution.py:913
  393.4 19.1 %collective-permute-start.26 = (bf16[192,1024]{1,0:T(8,128)(2,1)S(1)}, bf16[192,1024]{1,0:T(8,128)(2,1)S(1)}, u32[]{:S(2)}, u32[]{:S(2)}) collective-permute-start(bf16[192,1024]{1,0:T(8,128)(2,1)S(1)} %get-tuple-element.232), channel_id=1, source_target_pairs={{0,12},{4,8},{8,4},{12,0},{16,28},{20,24},{24,20},{28,16},{1,13},{... | collective-permute-start | bytes 1179656 | tf_op jit(solution)/shard_map/ppermute | solution.py:913
  394.9 34.0 %copy-start.63 = (bf16[2048,1024]{1,0:T(8,128)(2,1)S(1)}, bf16[2048,1024]{1,0:T(8,128)(2,1)}, u32[]{:S(2)}) copy-start(bf16[2048,1024]{1,0:T(8,128)(2,1)} %get-tuple-element.247) | copy-start | bytes 12582916
  419.7 47.6 %collective-permute-start.28 = (bf16[256,1024]{1,0:T(8,128)(2,1)}, bf16[256,1024]{1,0:T(8,128)(2,1)}, u32[]{:S(2)}, u32[]{:S(2)}) collective-permute-start(bf16[256,1024]{1,0:T(8,128)(2,1)} %get-tuple-element.249), channel_id=1, source_target_pairs={{0,1},{1,2},{4,5},{5,6},{8,9},{9,10},{12,13},{13,14},{16,17},{17,1... | collective-permute-start | bytes 1572872 | tf_op jit(solution)/shard_map/ppermute | solution.py:876
  422.5 44.7 %collective-permute-start.27 = (bf16[256,1024]{1,0:T(8,128)(2,1)}, bf16[256,1024]{1,0:T(8,128)(2,1)S(1)}, u32[]{:S(2)}, u32[]{:S(2)}) collective-permute-start(bf16[256,1024]{1,0:T(8,128)(2,1)} %get-tuple-element.249), channel_id=1, source_target_pairs={{2,1},{3,2},{6,5},{7,6},{10,9},{11,10},{14,13},{15,14},{18,17},{19... | collective-permute-start | bytes 1572872 | tf_op jit(solution)/shard_map/ppermute | solution.py:876
  423.3 44.0 %collective-permute-start.29 = (bf16[256,1024]{1,0:T(8,128)(2,1)}, bf16[256,1024]{1,0:T(8,128)(2,1)S(1)}, u32[]{:S(2)}, u32[]{:S(2)}) collective-permute-start(bf16[256,1024]{1,0:T(8,128)(2,1)} %get-tuple-element.250), channel_id=1, source_target_pairs={{0,3},{3,0},{4,7},{7,4},{8,11},{11,8},{12,15},{15,12},{16,19},{19,... | collective-permute-start | bytes 1572872 | tf_op jit(solution)/shard_map/ppermute | solution.py:876
  445.9 21.4 %copy-start.42 = (bf16[256,1024]{1,0:T(8,128)(2,1)S(1)}, bf16[256,1024]{1,0:T(8,128)(2,1)}, u32[]{:S(2)}) copy-start(bf16[256,1024]{1,0:T(8,128)(2,1)} %copy-done.41) | copy-start | bytes 1572868
  467.3 18.6 %copy-start.29 = (f32[256,1024]{1,0:T(8,128)S(1)}, f32[256,1024]{1,0:T(8,128)}, u32[]{:S(2)}) copy-start(f32[256,1024]{1,0:T(8,128)} %copy-done.28) | copy-start | bytes 3145732
  468.7 12.8 %collective-permute-start.31 = (bf16[256,1024]{1,0:T(8,128)(2,1)S(1)}, bf16[256,1024]{1,0:T(8,128)(2,1)S(1)}, u32[]{:S(2)}, u32[]{:S(2)}) collective-permute-start(bf16[256,1024]{1,0:T(8,128)(2,1)S(1)} %add_convert_fusion.4), channel_id=1, source_target_pairs={{0,1},{1,2},{2,3},{4,5},{5,6},{6,7},{8,9},{9,10},{10,11},{12,13},{... | collective-permute-start | bytes 1572872 | tf_op jit(solution)/shard_map/ppermute | solution.py:876
  470.2 15.7 %collective-permute-start.30 = (bf16[256,1024]{1,0:T(8,128)(2,1)S(1)}, bf16[256,1024]{1,0:T(8,128)(2,1)S(1)}, u32[]{:S(2)}, u32[]{:S(2)}) collective-permute-start(bf16[256,1024]{1,0:T(8,128)(2,1)S(1)} %add_convert_fusion.5), channel_id=1, source_target_pairs={{1,0},{2,1},{3,2},{5,4},{6,5},{7,6},{9,8},{10,9},{11,10},{13,12},{... | collective-permute-start | bytes 1572872 | tf_op jit(solution)/shard_map/ppermute | solution.py:876
  489.4 15.6 %collective-permute-start.33 = (bf16[256,1024]{1,0:T(8,128)(2,1)S(1)}, bf16[256,1024]{1,0:T(8,128)(2,1)S(1)}, u32[]{:S(2)}, u32[]{:S(2)}) collective-permute-start(bf16[256,1024]{1,0:T(8,128)(2,1)S(1)} %first_back.1.refs_0_), channel_id=1, source_target_pairs={{1,0},{2,1},{3,2},{5,4},{6,5},{7,6},{9,8},{10,9},{11,10},{13,12},{... | collective-permute-start | bytes 1572872 | tf_op jit(solution)/shard_map/ppermute | solution.py:876
  490.7 16.9 %collective-permute-start.32 = (bf16[256,1024]{1,0:T(8,128)(2,1)S(1)}, bf16[256,1024]{1,0:T(8,128)(2,1)S(1)}, u32[]{:S(2)}, u32[]{:S(2)}) collective-permute-start(bf16[256,1024]{1,0:T(8,128)(2,1)S(1)} %first_back.1.refs_0_), channel_id=1, source_target_pairs={{0,1},{1,2},{2,3},{4,5},{5,6},{6,7},{8,9},{9,10},{10,11},{12,13},{... | collective-permute-start | bytes 1572872 | tf_op jit(solution)/shard_map/ppermute | solution.py:876
  497.8 35.6 %collective-permute-start.37 = (bf16[1,128,2048]{2,1,0:T(8,128)(2,1)}, bf16[1,128,2048]{2,1,0:T(8,128)(2,1)}, u32[]{:S(2)}, u32[]{:S(2)}) collective-permute-start(bf16[1,128,2048]{2,1,0:T(8,128)(2,1)} %slice.123), channel_id=1, source_target_pairs={{0,16},{4,20},{8,24},{12,28},{16,0},{20,4},{24,8},{28,12},{1,17},{... | collective-permute-start | bytes 1572872 | tf_op jit(solution)/shard_map/ppermute | solution.py:913
  499.3 38.7 %collective-permute-start.34 = (bf16[256,1024]{1,0:T(8,128)(2,1)S(1)}, bf16[256,1024]{1,0:T(8,128)(2,1)S(1)}, u32[]{:S(2)}, u32[]{:S(2)}) collective-permute-start(bf16[256,1024]{1,0:T(8,128)(2,1)S(1)} %first_back.1.refs_0_), channel_id=1, source_target_pairs={{0,3},{3,0},{4,7},{7,4},{8,11},{11,8},{12,15},{15,12},{16,19},{19,... | collective-permute-start | bytes 1572872 | tf_op jit(solution)/shard_map/ppermute | solution.py:876
  505.1 32.9 %collective-permute-start.36 = (bf16[256,1024]{1,0:T(8,128)(2,1)S(1)}, bf16[256,1024]{1,0:T(8,128)(2,1)S(1)}, u32[]{:S(2)}, u32[]{:S(2)}) collective-permute-start(bf16[256,1024]{1,0:T(8,128)(2,1)S(1)} %collective-permute-done.33.refs_2_), channel_id=1, source_target_pairs={{1,0},{2,1},{5,4},{6,5},{9,8},{10,9},{13,12},{14,13},{17,16},{18,1... | collective-permute-start | bytes 1572872 | tf_op jit(solution)/shard_map/ppermute | solution.py:876
  507.6 30.3 %collective-permute-start.35 = (bf16[256,1024]{1,0:T(8,128)(2,1)S(1)}, bf16[256,1024]{1,0:T(8,128)(2,1)S(1)}, u32[]{:S(2)}, u32[]{:S(2)}) collective-permute-start(bf16[256,1024]{1,0:T(8,128)(2,1)S(1)} %collective-permute-done.32.refs_1_), channel_id=1, source_target_pairs={{1,2},{2,3},{5,6},{6,7},{9,10},{10,11},{13,14},{14,15},{17,18},{18... | collective-permute-start | bytes 1572872 | tf_op jit(solution)/shard_map/ppermute | solution.py:876
  528.9 16.4 %all-to-all-start.6 = ((bf16[4,384,128]{1,2,0:T(8,128)(2,1)}), bf16[4,384,128]{1,2,0:T(8,128)(2,1)}, u32[]{:S(2)}, u32[]{:S(2)}) async-start(bf16[4,384,128]{1,2,0:T(8,128)(2,1)} %pad_maximum_fusion), calls=%async_computation.7 | async-start | bytes 786432 | tf_op jit(solution)/shard_map/all_to_all | solution.py:1078
  (57 other events, 344.1 us)
Sparse Core Ops, SparseCore 0:
  9.6 48.6 all-gather.1
  359.2 100.0 all-reduce.1
  467.4 58.8 reduce-scatter.1
